TPU v7x, 256 devices: a whole 4x4x8 slice. The times are simulated.
256 devices in a mesh: gx: 32 (over z, y_hi, core), gy: 8 (over x, y_lo).
Axes of the slice: x: 4, y: 4 (y_hi: 2, y_lo: 2; y = y_hi * 2 + y_lo), z: 8, core: 2. Of those that a mesh axis runs over, the one named last changes fastest.
Arguments:
- cotangent: float32 [256, 64, 1024], P('gx', 'gy'), may hold values from -6 to 6
- diagonal: float32 [256, 64, 1024], P('gx', 'gy'), may hold values from 0.01 to 0.1
Outputs:
- grad_guess: float32 [256, 64, 1024], P('gx', 'gy')
- grad_source: float32 [256, 64, 1024], P('gx', 'gy')
All inputs are finite; a program needn't handle non-finite values.
Results may differ from a plain program's by a relative error of at most 0.0003.
Values sent between devices are 32-bit elements; how exact they have to be, the bound alone decides.
No kernel may reach another device: no remote copies, remote signals or barrier semaphores. Data moves between devices by JAX's collectives and lax.ppermute only.
A program may use at most 128 MiB of HBM per device.

v0:
```python
import jax
import jax.numpy as jnp
from jax import lax
from jax.experimental import pallas as pl
from jax.experimental.pallas import tpu as pltpu
from jax.sharding import PartitionSpec as P

GX = 32
GY = 8
OMEGA = 2.0 / 3.0
THIRD = 1.0 / 3.0
F32 = jnp.float32
VMEM_LIMIT = 48 * 1024 * 1024


def params():
    return pltpu.CompilerParams(vmem_limit_bytes=VMEM_LIMIT)


def shape(*dims):
    return jax.ShapeDtypeStruct(dims, F32)


def smem():
    return pl.BlockSpec(memory_space=pltpu.SMEM)


def vmem():
    return pl.BlockSpec(memory_space=pltpu.VMEM)


def z_sum_fine(v):
    last = v.ndim - 1
    place = lax.broadcasted_iota(jnp.int32, v.shape, last - 1)
    after = pltpu.roll(v, 7, last - 1)
    after = jnp.where(place == 7, pltpu.roll(after, 127, last), after)
    before = pltpu.roll(v, 1, last - 1)
    before = jnp.where(place == 0, pltpu.roll(before, 1, last), before)
    return after + before


def yz_sum(v):
    count, rows = v.shape[0], v.shape[1]
    total = pltpu.roll(v, 1, 1) + pltpu.roll(v, rows - 1, 1)
    parts = []
    for c in range(count):
        after = v[c + 1] if c < count - 1 else pltpu.roll(v[0], 127, 1)
        before = v[c - 1] if c > 0 else pltpu.roll(v[count - 1], 1, 1)
        parts.append(after + before)
    return total + jnp.stack(parts, 0)


def coarse_neighbours(ref, x):
    return ref[x + 1] + ref[x - 1] + yz_sum(ref[x])


def restrict_fine(pairs_ref, out_ref, scale):
    for x in range(4):
        for c in range(4):
            out_ref[x, c] = scale * (
                pairs_ref[x, pl.ds(2 * c, 4, stride=8), :] + pairs_ref[x, pl.ds(2 * c + 1, 4, stride=8), :]
            )


def block_pairs(field, pairs_ref):
    for x in range(4):
        row = field[2 * x] + field[2 * x + 1]
        for y in range(4):
            pairs_ref[x, pl.ds(8 * y, 8), :] = row[2 * y] + row[2 * y + 1]


def prepare_kernel(cot_ref, diag_ref, f_ref, sg_ref, ylo_ref, yhi_ref, c1_ref, turned, placed, pairs):
    stacked = jnp.concatenate([cot_ref[...].reshape(64, 1024), diag_ref[...].reshape(64, 1024)], axis=0)
    turned[...] = stacked.T
    for c in range(8):
        placed[pl.ds(c, 128, stride=8), :] = turned[pl.ds(c, 128, stride=8), :].T
    f = placed[0:512, :].reshape(8, 8, 8, 128)
    diag = placed[512:1024, :].reshape(8, 8, 8, 128)
    g = OMEGA / (6.0 + diag)
    s = g * f
    f_ref[...] = f
    sg_ref[0] = s
    sg_ref[1] = g
    ylo_ref[0] = s[:, 0:2]
    ylo_ref[1] = g[:, 0:2]
    yhi_ref[0] = s[:, 6:8]
    yhi_ref[1] = g[:, 6:8]
    block_pairs(diag, pairs)
    restrict_fine(pairs, c1_ref, 0.125)


def prepare(cot, diag):
    return pl.pallas_call(
        prepare_kernel,
        out_shape=(
            shape(8, 8, 8, 128),
            shape(2, 8, 8, 8, 128),
            shape(2, 8, 2, 8, 128),
            shape(2, 8, 2, 8, 128),
            shape(4, 4, 4, 128),
        ),
        scratch_shapes=[
            pltpu.VMEM((1024, 128), F32),
            pltpu.VMEM((1024, 128), F32),
            pltpu.VMEM((4, 32, 128), F32),
        ],
        compiler_params=params(),
    )(cot, diag)


def fine_neighbours(ref, x, lo, hi):
    row = ref[x]
    mid = row[lo:hi]
    return (
        ref[x + 1, lo:hi] + ref[x - 1, lo:hi] + row[lo - 1 : hi - 1] + row[lo + 1 : hi + 1] + z_sum_fine(mid)
    )


def fine_down_kernel(
    f_ref, sg_ref, ylo_ref, yhi_ref, xlo_ref, xhi_ref, f2_ref, src_ref, gext_ref, fylo_ref, fyhi_ref, rhs_ref, s0, s1, pairs
):
    s0[2:10, 2:10] = sg_ref[0]
    s0[2:10, 0:2] = ylo_ref[0]
    s0[2:10, 10:12] = yhi_ref[0]
    s0[0:2] = xlo_ref[0]
    s0[10:12] = xhi_ref[0]
    gext_ref[2:10, 2:10] = sg_ref[1]
    gext_ref[2:10, 0:2] = ylo_ref[1]
    gext_ref[2:10, 10:12] = yhi_ref[1]
    gext_ref[0:2] = xlo_ref[1]
    gext_ref[10:12] = xhi_ref[1]

    def first(x, carry):
        total = fine_neighbours(s0, x, 1, 11)
        s1[x, 1:11] = THIRD * s0[x, 1:11] + gext_ref[x, 1:11] * total
        return carry

    lax.fori_loop(1, 11, first, 0)

    def second(x, carry):
        f1 = THIRD * f_ref[x - 2] + fine_neighbours(s0, x, 2, 10)
        f2_ref[x - 2] = THIRD * f1 + fine_neighbours(s1, x, 2, 10)
        src_ref[x - 2] = s0[x, 2:10] + s1[x, 2:10]
        return carry

    lax.fori_loop(2, 10, second, 0)
    fylo_ref[...] = f2_ref[:, 0:2]
    fyhi_ref[...] = f2_ref[:, 6:8]
    block_pairs(f2_ref, pairs)
    restrict_fine(pairs, rhs_ref, 1.0)


def fine_down(f, sg, ylo, yhi, xlo, xhi):
    return pl.pallas_call(
        fine_down_kernel,
        out_shape=(
            shape(8, 8, 8, 128),
            shape(8, 8, 8, 128),
            shape(12, 12, 8, 128),
            shape(8, 2, 8, 128),
            shape(8, 2, 8, 128),
            shape(4, 4, 4, 128),
        ),
        scratch_shapes=[
            pltpu.VMEM((12, 12, 8, 128), F32),
            pltpu.VMEM((12, 12, 8, 128), F32),
            pltpu.VMEM((4, 32, 128), F32),
        ],
        compiler_params=params(),
    )(f, sg, ylo, yhi, xlo, xhi)


def assemble_y(index_ref, blocks_ref, out_ref):
    me = index_ref[1]
    for k in range(8):
        source = lax.rem(me + (k + 4), 8)
        out_ref[:, :, 4 * k : 4 * k + 4, :] = blocks_ref[source]


def coefficients_kernel(index_ref, blocks_ref, g1_ref, c2_ref, field, pairs):
    assemble_y(index_ref, blocks_ref, field)
    g1_ref[...] = OMEGA / (6.0 + 4.0 * field[...])
    for x in range(2):
        row = field[4 + 2 * x] + field[5 + 2 * x]
        for c in range(2):
            pairs[x, c] = row[2 * c] + row[2 * c + 1]
            c2_ref[x, c] = 0.125 * (
                pairs[x, c, pl.ds(0, 16, stride=2), :] + pairs[x, c, pl.ds(1, 16, stride=2), :]
            )


def coefficients(index, blocks):
    return pl.pallas_call(
        coefficients_kernel,
        out_shape=(shape(12, 4, 32, 128), shape(2, 2, 16, 128)),
        in_specs=[smem(), vmem()],
        scratch_shapes=[pltpu.VMEM((12, 4, 32, 128), F32), pltpu.VMEM((2, 2, 32, 128), F32)],
        compiler_params=params(),
    )(index, blocks)


def middle_down_kernel(index_ref, blocks_ref, g_ref, f2_ref, src_ref, flo_ref, fhi_ref, rhs2_ref, rhs, s0, s1, pairs):
    assemble_y(index_ref, blocks_ref, rhs)
    s0[...] = g_ref[...] * rhs[...]

    def first(x, carry):
        total = coarse_neighbours(s0, x)
        s1[x] = THIRD * s0[x] + g_ref[x] * total
        rhs[x] = THIRD * rhs[x] + total
        return carry

    lax.fori_loop(1, 11, first, 0)

    def second(x, carry):
        f2_ref[x - 2] = THIRD * rhs[x] + coarse_neighbours(s1, x)
        src_ref[x - 2] = s0[x] + s1[x]
        return carry

    lax.fori_loop(2, 10, second, 0)
    flo_ref[...] = f2_ref[3]
    fhi_ref[...] = f2_ref[4]
    for x in range(2):
        row = f2_ref[2 + 2 * x] + f2_ref[3 + 2 * x]
        for c in range(2):
            pairs[x, c] = row[2 * c] + row[2 * c + 1]
            rhs2_ref[x, c] = pairs[x, c, pl.ds(0, 16, stride=2), :] + pairs[x, c, pl.ds(1, 16, stride=2), :]


def middle_down(index, blocks, g1):
    return pl.pallas_call(
        middle_down_kernel,
        out_shape=(
            shape(8, 4, 32, 128),
            shape(8, 4, 32, 128),
            shape(4, 32, 128),
            shape(4, 32, 128),
            shape(2, 2, 16, 128),
        ),
        in_specs=[smem(), vmem(), vmem()],
        scratch_shapes=[
            pltpu.VMEM((12, 4, 32, 128), F32),
            pltpu.VMEM((12, 4, 32, 128), F32),
            pltpu.VMEM((12, 4, 32, 128), F32),
            pltpu.VMEM((2, 2, 32, 128), F32),
        ],
        compiler_params=params(),
    )(index, blocks, g1)


def place_x(index_ref, pieces, out_ref):
    me = index_ref[0]
    z_me = lax.div(me, 4)
    step_y = 4 - 8 * lax.rem(lax.div(me, 2), 2)
    step_core = 2 - 4 * lax.rem(me, 2)
    offsets = (0, step_y, step_core, step_y + step_core)
    for piece, offset in zip(pieces, offsets):
        for k in range(8):
            source = lax.rem(z_me + (k + 4), 8)
            target = lax.rem(8 * k + offset + 64, 64)
            out_ref[pl.ds(target, 2)] = piece[source]


def up_kernel(
    index_ref, ra, rb, rc, rd, ca, cb, cc, cd, g1_ref, f1_ref, src1_ref, f1lo_ref, f1hi_ref,
    g0_ref, f0_ref, src0_ref, fylo_ref, fyhi_ref, fxlo_ref, fxhi_ref,
    guess_ref, source_ref,
    rhs2, g2, p2, q2, out3, e3, pairs3, win2, r2, sa2, out2, r1, sa1, out1, pairs1,
    rep, r0, f0, s3, s4, turned, placed,
):
    place_x(index_ref, (ra, rb, rc, rd), rhs2)
    place_x(index_ref, (ca, cb, cc, cd), g2)

    def restrict2(x, ref):
        row = ref[2 * x] + ref[2 * x + 1]
        pairs3[x] = row[0] + row[1]
        return pairs3[x, pl.ds(0, 8, stride=2), :] + pairs3[x, pl.ds(1, 8, stride=2), :]

    def scale2(x, carry):
        g3 = OMEGA / (6.0 + 64.0 * 0.125 * restrict2(x, g2))
        e3[1, x] = g3
        for r in range(2):
            row = 2 * x + r
            g = OMEGA / (6.0 + 16.0 * g2[row])
            g2[row] = g
            p2[row + 1] = g * rhs2[row]
        return carry

    lax.fori_loop(0, 32, scale2, 0)
    p2[0] = p2[64]
    p2[65] = p2[1]

    def first2(x, carry):
        total = coarse_neighbours(p2, x)
        q2[x] = THIRD * p2[x] + g2[x - 1] * total
        rhs2[x - 1] = THIRD * rhs2[x - 1] + total
        return carry

    lax.fori_loop(1, 65, first2, 0)
    q2[0] = q2[64]
    q2[65] = q2[1]

    def second2(x, carry):
        for r in range(2):
            row = 2 * x + r
            rhs2[row] = THIRD * rhs2[row] + coarse_neighbours(q2, row + 1)
        e3[0, x] = restrict2(x, rhs2)
        return carry

    lax.fori_loop(0, 32, second2, 0)

    g3 = e3[1]
    s = g3 * e3[0]
    acc = s
    for sweep in range(7):
        total = jnp.concatenate([s[1:], s[:1]], 0) + jnp.concatenate([s[31:], s[:31]], 0)
        total = total + pltpu.roll(s, 1, 1) + pltpu.roll(s, 7, 1)
        total = total + pltpu.roll(s, 1, 2) + pltpu.roll(s, 127, 2)
        s = THIRD * s + g3 * total
        acc = acc + s
    out3[...] = 0.5 * acc

    for x in range(10):
        half = out3[14 + x // 2]
        for c in range(2):
            r2[x, c, pl.ds(0, 8, stride=2), :] = half
            r2[x, c, pl.ds(1, 8, stride=2), :] = half
    for x in range(1, 9):
        g = g2[28 + x]
        f = rhs2[28 + x] - (OMEGA / g) * r2[x] + coarse_neighbours(r2, x)
        sa2[x] = g * f
    for x in range(2, 8):
        sb = THIRD * sa2[x] + g2[28 + x] * coarse_neighbours(sa2, x)
        out2[x - 2] = 0.5 * (p2[29 + x] + q2[29 + x] + r2[x] + sa2[x] + sb)

    for x in range(12):
        for c in range(4):
            half = out2[x // 2, c // 2]
            r1[x, c, pl.ds(0, 16, stride=2), :] = half
            r1[x, c, pl.ds(1, 16, stride=2), :] = half

    def residual1(x, f):
        g = g1_ref[x]
        sa1[x] = g * (f - (OMEGA / g) * r1[x] + coarse_neighbours(r1, x))

    residual1(1, f1lo_ref[...])
    residual1(10, f1hi_ref[...])

    def middle1(x, carry):
        residual1(x, f1_ref[x - 2])
        return carry

    lax.fori_loop(2, 10, middle1, 0)

    def last1(x, carry):
        sb = THIRD * sa1[x] + g1_ref[x] * coarse_neighbours(sa1, x)
        row = 0.5 * (src1_ref[x - 2] + r1[x] + sa1[x] + sb)
        for c in range(4):
            out1[x - 2, pl.ds(32 * c, 32), :] = row[c]
        return carry

    lax.fori_loop(2, 10, last1, 0)

    def spread0(x, carry):
        for y in range(8):
            row = out1[x, pl.ds(14 + y, 4, stride=32), :]
            rep[pl.ds(0, 4, stride=2), :] = row
            rep[pl.ds(1, 4, stride=2), :] = row
            both = rep[...]
            for p in range(2):
                for q in range(2):
                    r0[2 * x + p, 2 * y + q] = both
        return carry

    lax.fori_loop(0, 8, spread0, 0)
    f0[2:10, 2:10] = f0_ref[...]
    f0[2:10, 0:2] = fylo_ref[...]
    f0[2:10, 10:12] = fyhi_ref[...]
    f0[0:2] = fxlo_ref[...]
    f0[10:12] = fxhi_ref[...]

    def residual0(x, carry):
        g = g0_ref[x]
        f = f0[x] - (OMEGA / g) * r0[x + 2, 2:14] + fine_neighbours(r0, x + 2, 2, 14)
        f0[x] = f
        s3[x] = g * f
        return carry

    lax.fori_loop(0, 12, residual0, 0)

    def first0(x, carry):
        s4[x, 1:11] = THIRD * s3[x, 1:11] + g0_ref[x, 1:11] * fine_neighbours(s3, x, 1, 11)
        return carry

    lax.fori_loop(1, 11, first0, 0)

    def second0(x, carry):
        f4 = THIRD * f0[x, 2:10] + fine_neighbours(s3, x, 2, 10)
        f5 = THIRD * f4 + fine_neighbours(s4, x, 2, 10)
        source = src0_ref[x - 2] + r0[x + 2, 4:12] + s3[x, 2:10] + s4[x, 2:10]
        placed[pl.ds(64 * (x - 2), 64), :] = f5.reshape(64, 128)
        placed[pl.ds(64 * (x - 2) + 512, 64), :] = source.reshape(64, 128)
        return carry

    lax.fori_loop(2, 10, second0, 0)
    for c in range(8):
        turned[pl.ds(c, 128, stride=8), :] = placed[pl.ds(c, 128, stride=8), :].T
    result = turned[...].T
    guess_ref[...] = result[0:64].reshape(8, 8, 1024)
    source_ref[...] = result[64:128].reshape(8, 8, 1024)


def up(index, *arrays):
    scratch = [
        (64, 2, 16, 128), (64, 2, 16, 128), (66, 2, 16, 128), (66, 2, 16, 128),
        (32, 8, 128), (2, 32, 8, 128), (32, 16, 128), (8, 128),
        (10, 2, 16, 128), (10, 2, 16, 128), (6, 2, 16, 128),
        (12, 4, 32, 128), (12, 4, 32, 128), (8, 128, 128), (8, 128),
        (8, 128), (16, 16, 8, 128), (12, 12, 8, 128), (12, 12, 8, 128), (12, 12, 8, 128),
        (1024, 128), (1024, 128),
    ]
    return pl.pallas_call(
        up_kernel,
        out_shape=(shape(8, 8, 1024), shape(8, 8, 1024)),
        in_specs=[smem()] + [vmem()] * len(arrays),
        scratch_shapes=[pltpu.VMEM(dims, F32) for dims in scratch],
        compiler_params=params(),
    )(index, *arrays)


def shifted(v, axis, count, step):
    return lax.ppermute(v, axis, [(i, (i + step) % count) for i in range(count)])


def swapped(v, bit):
    return lax.ppermute(v, "gx", [(i, i ^ bit) for i in range(GX)])


def gather_y(v):
    return lax.all_to_all(jnp.broadcast_to(v[None], (GY,) + v.shape), "gy", 0, 0)


def with_x_blocks(v):
    before = shifted(v, "gx", GX, 1)
    after = shifted(v, "gx", GX, -1)
    return jnp.concatenate([before, v, after], axis=0)


def gather_x(v):
    groups = [[q + 4 * z for z in range(8)] for q in range(4)]
    along = lax.all_to_all(jnp.broadcast_to(v[None], (8,) + v.shape), "gx", 0, 0, axis_index_groups=groups)
    across = swapped(along, 2)
    return along, across, swapped(along, 1), swapped(across, 1)


def per_device(cotangent, diagonal):
    index = jnp.stack([lax.axis_index("gx"), lax.axis_index("gy")]).astype(jnp.int32)
    f, sg, ylo, yhi, c1 = prepare(cotangent, diagonal)

    ylo, yhi = shifted(yhi, "gy", GY, 1), shifted(ylo, "gy", GY, -1)
    xlo = jnp.concatenate([ylo[:, 0:2], sg[:, 0:2], yhi[:, 0:2]], axis=2)
    xhi = jnp.concatenate([ylo[:, 6:8], sg[:, 6:8], yhi[:, 6:8]], axis=2)
    xlo, xhi = shifted(xhi, "gx", GX, 1), shifted(xlo, "gx", GX, -1)

    g1, c2 = coefficients(index, gather_y(with_x_blocks(c1)))
    c2_pieces = gather_x(c2)

    f2, src0, g0, fylo, fyhi, rhs1 = fine_down(f, sg, ylo, yhi, xlo, xhi)
    fylo, fyhi = shifted(fyhi, "gy", GY, 1), shifted(fylo, "gy", GY, -1)
    fxlo = jnp.concatenate([fylo[0:2], f2[0:2], fyhi[0:2]], axis=1)
    fxhi = jnp.concatenate([fylo[6:8], f2[6:8], fyhi[6:8]], axis=1)
    fxlo, fxhi = shifted(fxhi, "gx", GX, 1), shifted(fxlo, "gx", GX, -1)

    f1, src1, f1lo, f1hi, rhs2 = middle_down(index, gather_y(with_x_blocks(rhs1)), g1)
    f1lo, f1hi = shifted(f1lo, "gx", GX, 1), shifted(f1hi, "gx", GX, -1)
    rhs2_pieces = gather_x(rhs2)

    return up(
        index, *rhs2_pieces, *c2_pieces, g1, f1, src1, f1lo, f1hi, g0, f2, src0, fylo, fyhi, fxlo, fxhi
    )


def solution(mesh):
    spec = P("gx", "gy", None)
    return jax.shard_map(per_device, mesh=mesh, in_specs=(spec, spec), out_specs=(spec, spec), check_vma=False)
```

profile of v0, /device:TPU:1, one launch (start us, length us, event | category | flops | bytes accessed | tf_op | source)
XLA Modules:
  0.0 137.6 jit_solution(4933676837059342683)
XLA Ops:
  0.6 0.9 copy-done.4
  1.6 0.9 copy-done.5
  2.5 0.5 shard_map.41
  3.0 3.3 %collective-permute-start.7 = (f32[4,4,4,128]{3,2,1,0:T(4,128)S(1)}, f32[4,4,4,128]{3,2,1,0:T(4,128)S(1)}, u32[]{:S(2)}, u32[]{:S(2)}) collective-permute-start(f32[4,4,4,128]{3,2,1,0:T(4,128)S(1)} %get-tuple-element.25), channel_id=1, source_target_pairs={{0,248},{8,0},{16,8},{24,16},{32,24},{40,32},{48,40},{56,48},{64,5... | collective-permute-start | bytes 98312 | tf_op jit(solution)/shard_map/ppermute | solution.py:431
  6.3 1.2 collective-permute-start.6
  7.5 1.0 collective-permute-start
  8.5 2.6 %collective-permute-start.1 = (f32[2,8,2,8,128]{4,3,2,1,0:T(8,128)S(1)}, f32[2,8,2,8,128]{4,3,2,1,0:T(8,128)S(1)}, u32[]{:S(2)}, u32[]{:S(2)}) collective-permute-start(f32[2,8,2,8,128]{4,3,2,1,0:T(8,128)S(1)} %get-tuple-element.23), channel_id=1, source_target_pairs={{0,7},{1,0},{2,1},{3,2},{4,3},{5,4},{6,5},{7,6},{8,15},{9,8},{10,9... | collective-permute-start | bytes 393224 | tf_op jit(solution)/shard_map/ppermute | solution.py:431
  11.1 0.0 collective-permute-done.7
  11.1 2.1 %collective-permute-done.6 = f32[4,4,4,128]{3,2,1,0:T(4,128)S(1)} collective-permute-done((f32[4,4,4,128]{3,2,1,0:T(4,128)S(1)}, f32[4,4,4,128]{3,2,1,0:T(4,128)S(1)}, u32[]{:S(2)}, u32[]{:S(2)}) %collective-permute-start.6) | collective-permute-done | bytes 32800 | tf_op jit(solution)/shard_map/ppermute | solution.py:431
  13.3 1.0 broadcast_in_dim.9
  14.3 4.1 %all-to-all-start.1 = ((f32[8,12,4,4,128]{4,3,2,1,0:T(4,128)}), f32[8,12,4,4,128]{4,3,2,1,0:T(4,128)S(1)}, u32[]{:S(2)}, u32[]{:S(2)}) async-start(f32[8,12,4,4,128]{4,3,2,1,0:T(4,128)} %broadcast_in_dim.9), calls=%async_computation.1 | async-start | bytes 1572864 | tf_op jit(solution)/shard_map/all_to_all | solution.py:439
  18.4 0.0 collective-permute-done.ylo_ref
  18.4 0.0 collective-permute-done.1.yhi_ref
  18.5 1.0 collective-permute-start.2
  19.5 5.7 %collective-permute-start.3 = (f32[2,2,12,8,128]{4,3,2,1,0:T(8,128)S(1)}, f32[2,2,12,8,128]{4,3,2,1,0:T(8,128)S(1)}, u32[]{:S(2)}, u32[]{:S(2)}) collective-permute-start(f32[2,2,12,8,128]{4,3,2,1,0:T(8,128)S(1)} %pad_maximum_fusion.1), channel_id=1, source_target_pairs={{0,248},{8,0},{16,8},{24,16},{32,24},{40,32},{48,40},{56,48},{64,5... | collective-permute-start | bytes 589832 | tf_op jit(solution)/shard_map/ppermute | solution.py:431
  25.2 3.5 %collective-permute-done.2.xlo_ref = f32[2,2,12,8,128]{4,3,2,1,0:T(8,128)S(1)} collective-permute-done((f32[2,2,12,8,128]{4,3,2,1,0:T(8,128)S(1)}, f32[2,2,12,8,128]{4,3,2,1,0:T(8,128)S(1)}, u32[]{:S(2)}, u32[]{:S(2)}) %collective-permute-start.2) | collective-permute-done | bytes 196640 | tf_op jit(solution)/shard_map/ppermute | solution.py:431
  28.7 2.5 %collective-permute-done.3.xhi_ref = f32[2,2,12,8,128]{4,3,2,1,0:T(8,128)S(1)} collective-permute-done((f32[2,2,12,8,128]{4,3,2,1,0:T(8,128)S(1)}, f32[2,2,12,8,128]{4,3,2,1,0:T(8,128)S(1)}, u32[]{:S(2)}, u32[]{:S(2)}) %collective-permute-start.3) | collective-permute-done | bytes 196640 | tf_op jit(solution)/shard_map/ppermute | solution.py:431
  31.2 1.9 %shard_map.42 = (f32[8,8,8,128]{3,2,1,0:T(8,128)S(1)}, f32[8,8,8,128]{3,2,1,0:T(8,128)S(1)}, f32[12,12,8,128]{3,2,1,0:T(8,128)S(1)}, f32[8,2,8,128]{3,2,1,0:T(8,...) custom-call(f32[8,8,8,128]{3,2,1,0:T(8,128)S(1)} %get-tuple-element.20.f_ref, ...), custom_call_target="tpu_custom_call" | custom-call | tf_op jit(solution)/shard_map/pallas_call | solution.py:154
  33.1 0.6 copy-done.6
  33.7 0.6 copy-done.11
  34.3 2.6 %collective-permute-start.5 = (f32[4,4,4,128]{3,2,1,0:T(4,128)S(1)}, f32[4,4,4,128]{3,2,1,0:T(4,128)S(1)}, u32[]{:S(2)}, u32[]{:S(2)}) collective-permute-start(f32[4,4,4,128]{3,2,1,0:T(4,128)S(1)} %get-tuple-element.24), channel_id=1, source_target_pairs={{0,248},{8,0},{16,8},{24,16},{32,24},{40,32},{48,40},{56,48},{64,5... | collective-permute-start | bytes 98312 | tf_op jit(solution)/shard_map/ppermute | solution.py:431
  36.9 0.6 collective-permute-start.4
  37.6 1.6 %collective-permute-done.5 = f32[4,4,4,128]{3,2,1,0:T(4,128)S(1)} collective-permute-done((f32[4,4,4,128]{3,2,1,0:T(4,128)S(1)}, f32[4,4,4,128]{3,2,1,0:T(4,128)S(1)}, u32[]{:S(2)}, u32[]{:S(2)}) %collective-permute-start.5) | collective-permute-done | bytes 32800 | tf_op jit(solution)/shard_map/ppermute | solution.py:431
  39.2 3.9 %collective-permute-done.4 = f32[4,4,4,128]{3,2,1,0:T(4,128)S(1)} collective-permute-done((f32[4,4,4,128]{3,2,1,0:T(4,128)S(1)}, f32[4,4,4,128]{3,2,1,0:T(4,128)S(1)}, u32[]{:S(2)}, u32[]{:S(2)}) %collective-permute-start.4) | collective-permute-done | bytes 32800 | tf_op jit(solution)/shard_map/ppermute | solution.py:431
  43.1 1.0 broadcast_in_dim.8
  44.1 5.4 %all-to-all-start = ((f32[8,12,4,4,128]{4,3,2,1,0:T(4,128)}), f32[8,12,4,4,128]{4,3,2,1,0:T(4,128)S(1)}, u32[]{:S(2)}, u32[]{:S(2)}) async-start(f32[8,12,4,4,128]{4,3,2,1,0:T(4,128)} %broadcast_in_dim.8), calls=%async_computation | async-start | bytes 1572864 | tf_op jit(solution)/shard_map/all_to_all | solution.py:439
  49.6 0.1 pad_add_fusion.index_ref
  49.6 0.9 shard_map.43
  50.5 7.4 %all-to-all-done.blocks_ref = f32[8,12,4,4,128]{4,3,2,1,0:T(4,128)S(1)} async-done(((f32[8,12,4,4,128]{4,3,2,1,0:T(4,128)}), f32[8,12,4,4,128]{4,3,2,1,0:T(4,128)S(1)}, u32[]{:S(2)}, u32[]{:S(2)}) %all-to-all-start) | async-done | bytes 786464 | tf_op jit(solution)/shard_map/all_to_all | solution.py:439
  58.0 0.7 broadcast_in_dim.11
  58.7 9.7 %all-to-all-start.3 = ((f32[8,2,2,16,128]{4,3,2,1,0:T(8,128)}), f32[8,2,2,16,128]{4,3,2,1,0:T(8,128)S(1)}, u32[]{:S(2)}, u32[]{:S(2)}) async-start(f32[8,2,2,16,128]{4,3,2,1,0:T(8,128)} %broadcast_in_dim.11), calls=%async_computation.3 | async-start | bytes 524288 | tf_op jit(solution)/shard_map/all_to_all | solution.py:450
  68.4 2.3 %shard_map.44 = (f32[8,4,32,128]{3,2,1,0:T(8,128)S(1)}, f32[8,4,32,128]{3,2,1,0:T(8,128)S(1)}, f32[4,32,128]{2,1,0:T(8,128)S(1)}, f32[4,32,128]{2,1,0:T(8,128)S(1)}, f32[2,2,16,128]{3,2,1,0:T(8,128)S(1)}) custom-call(s32[2]{0:T(128)S(1)} %pad_add_fusion.index_ref, f32[8,12,4,4,128]{4,3,2,1,0:T(4,128)S(1)} %all-to-all-done.blocks_ref, ...), custom_call_target="tpu_custom_call" | custom-call | tf_op jit(solution)/shard_map/pallas_call | solution.py:230
  70.7 0.8 copy-done
  71.5 0.8 copy-done.2
  72.3 0.6 copy-done.7
  72.9 0.6 copy-done.9
  73.6 4.3 %all-to-all-done.3.ca = f32[8,2,2,16,128]{4,3,2,1,0:T(8,128)S(1)} async-done(((f32[8,2,2,16,128]{4,3,2,1,0:T(8,128)}), f32[8,2,2,16,128]{4,3,2,1,0:T(8,128)S(1)}, u32[]{:S(2)}, u32[]{:S(2)}) %all-to-all-start.3) | async-done | bytes 262176 | tf_op jit(solution)/shard_map/all_to_all | solution.py:450
  77.9 0.7 broadcast_in_dim.10
  78.6 3.5 %all-to-all-start.2 = ((f32[8,2,2,16,128]{4,3,2,1,0:T(8,128)}), f32[8,2,2,16,128]{4,3,2,1,0:T(8,128)S(1)}, u32[]{:S(2)}, u32[]{:S(2)}) async-start(f32[8,2,2,16,128]{4,3,2,1,0:T(8,128)} %broadcast_in_dim.10), calls=%async_computation.2 | async-start | bytes 524288 | tf_op jit(solution)/shard_map/all_to_all | solution.py:450
  82.2 0.8 collective-permute-start.16
  83.0 2.8 %collective-permute-start.17 = (f32[8,2,8,128]{3,2,1,0:T(8,128)}, f32[8,2,8,128]{3,2,1,0:T(8,128)}, u32[]{:S(2)}, u32[]{:S(2)}) collective-permute-start(f32[8,2,8,128]{3,2,1,0:T(8,128)} %copy-done.6), channel_id=1, source_target_pairs={{0,7},{1,0},{2,1},{3,2},{4,3},{5,4},{6,5},{7,6},{8,15},{9,8},{10,9... | collective-permute-start | bytes 196616 | tf_op jit(solution)/shard_map/ppermute | solution.py:431
  85.9 0.6 fusion.1
  86.5 1.2 collective-permute-done.16.fylo_ref
  87.7 0.6 fusion.4
  88.3 2.5 %collective-permute-start.11 = (f32[8,2,2,16,128]{4,3,2,1,0:T(8,128)S(1)}, f32[8,2,2,16,128]{4,3,2,1,0:T(8,128)}, u32[]{:S(2)}, u32[]{:S(2)}) collective-permute-start(f32[8,2,2,16,128]{4,3,2,1,0:T(8,128)S(1)} %all-to-all-done.3.ca), channel_id=1, source_target_pairs={{0,16},{8,24},{16,0},{24,8},{32,48},{40,56},{48,32},{56,40},{64,80... | collective-permute-start | bytes 786440 | tf_op jit(solution)/shard_map/ppermute | solution.py:435
  90.8 0.7 all-to-all-done.2.ra
  91.5 2.5 %collective-permute-start.8 = (f32[8,2,2,16,128]{4,3,2,1,0:T(8,128)S(1)}, f32[8,2,2,16,128]{4,3,2,1,0:T(8,128)S(1)}, u32[]{:S(2)}, u32[]{:S(2)}) collective-permute-start(f32[8,2,2,16,128]{4,3,2,1,0:T(8,128)S(1)} %all-to-all-done.2.ra), channel_id=1, source_target_pairs={{0,16},{8,24},{16,0},{24,8},{32,48},{40,56},{48,32},{56,40},{64,80... | collective-permute-start | bytes 786440 | tf_op jit(solution)/shard_map/ppermute | solution.py:435
  94.0 0.0 collective-permute-done.17.fyhi_ref
  94.0 0.7 fusion.5
  94.8 0.9 pad_maximum_fusion.4
  95.6 5.1 %collective-permute-start.18 = (f32[2,12,8,128]{3,2,1,0:T(8,128)S(1)}, f32[2,12,8,128]{3,2,1,0:T(8,128)S(1)}, u32[]{:S(2)}, u32[]{:S(2)}) collective-permute-start(f32[2,12,8,128]{3,2,1,0:T(8,128)S(1)} %pad_maximum_fusion.4), channel_id=1, source_target_pairs={{0,8},{8,16},{16,24},{24,32},{32,40},{40,48},{48,56},{56,64},{64,7... | collective-permute-start | bytes 294920 | tf_op jit(solution)/shard_map/ppermute | solution.py:431
  100.7 0.0 collective-permute-start.12
  100.7 0.0 collective-permute-done.11.cb
  100.7 1.2 collective-permute-start.13
  102.0 0.0 collective-permute-start.9
  102.0 2.7 %collective-permute-start.10 = (f32[8,2,2,16,128]{4,3,2,1,0:T(8,128)S(1)}, f32[8,2,2,16,128]{4,3,2,1,0:T(8,128)S(1)}, u32[]{:S(2)}, u32[]{:S(2)}) collective-permute-start(f32[8,2,2,16,128]{4,3,2,1,0:T(8,128)S(1)} %collective-permute-done.8.rb), channel_id=1, source_target_pairs={{0,8},{8,0},{16,24},{24,16},{32,40},{40,32},{48,56},{56,48},{64,72... | collective-permute-start | bytes 786440 | tf_op jit(solution)/shard_map/ppermute | solution.py:435
  104.7 3.0 %collective-permute-start.19 = (f32[2,12,8,128]{3,2,1,0:T(8,128)S(1)}, f32[2,12,8,128]{3,2,1,0:T(8,128)S(1)}, u32[]{:S(2)}, u32[]{:S(2)}) collective-permute-start(f32[2,12,8,128]{3,2,1,0:T(8,128)S(1)} %pad_maximum_fusion.5), channel_id=1, source_target_pairs={{0,248},{8,0},{16,8},{24,16},{32,24},{40,32},{48,40},{56,48},{64,5... | collective-permute-start | bytes 294920 | tf_op jit(solution)/shard_map/ppermute | solution.py:431
  107.7 2.7 %collective-permute-done.19.fxhi_ref = f32[2,12,8,128]{3,2,1,0:T(8,128)S(1)} collective-permute-done((f32[2,12,8,128]{3,2,1,0:T(8,128)S(1)}, f32[2,12,8,128]{3,2,1,0:T(8,128)S(1)}, u32[]{:S(2)}, u32[]{:S(2)}) %collective-permute-start.19) | collective-permute-done | bytes 98336 | tf_op jit(solution)/shard_map/ppermute | solution.py:431
  110.4 3.0 %collective-permute-done.14.f1lo_ref = f32[4,32,128]{2,1,0:T(8,128)S(1)} collective-permute-done((f32[4,32,128]{2,1,0:T(8,128)S(1)}, f32[4,32,128]{2,1,0:T(8,128)S(1)}, u32[]{:S(2)}, u32[]{:S(2)}) %collective-permute-start.14) | collective-permute-done | bytes 65568 | tf_op jit(solution)/shard_map/ppermute | solution.py:431
  113.4 6.6 %collective-permute-start.15 = (f32[4,32,128]{2,1,0:T(8,128)S(1)}, f32[4,32,128]{2,1,0:T(8,128)S(1)}, u32[]{:S(2)}, u32[]{:S(2)}) collective-permute-start(f32[4,32,128]{2,1,0:T(8,128)S(1)} %copy-done.8), channel_id=1, source_target_pairs={{0,248},{8,0},{16,8},{24,16},{32,24},{40,32},{48,40},{56,48},{64,5... | collective-permute-start | bytes 196616 | tf_op jit(solution)/shard_map/ppermute | solution.py:431
  120.1 0.9 collective-permute-done.15.f1hi_ref
  121.0 0.0 collective-permute-done.12.cc
  121.0 0.0 collective-permute-done.10.rd
  121.0 16.6 %shard_map.45 = (f32[8,8,1024]{2,1,0:T(8,128)}, f32[8,8,1024]{2,1,0:T(8,128)}) custom-call(s32[2]{0:T(128)S(1)} %pad_add_fusion.index_ref, f32[8,2,2,16,128]{4,3,2,1,0:T(8,128)S(1)} %all-to-all-done.2.ra, f32[8,2,2,16,128]{4,3,2,1,0:T(8,128)S(1)} %collective-permute-done.8.rb, f32[8,2,2,16,128]{4,3,2,1,0:T(8,128)S(1)} %collective-permute-done.9.rc, ...), custom_call_target="tpu_custom_call" | custom-call | tf_op jit(solution)/shard_map/pallas_call | solution.py:421
  (34 shorter events, 0.2 us)
Async XLA Ops:
  0.6 1.0 copy-start.4
  1.6 0.9 copy-start.5
  3.0 8.1 %collective-permute-start.7 = (f32[4,4,4,128]{3,2,1,0:T(4,128)S(1)}, f32[4,4,4,128]{3,2,1,0:T(4,128)S(1)}, u32[]{:S(2)}, u32[]{:S(2)}) collective-permute-start(f32[4,4,4,128]{3,2,1,0:T(4,128)S(1)} %get-tuple-element.25), channel_id=1, source_target_pairs={{0,248},{8,0},{16,8},{24,16},{32,24},{40,32},{48,40},{56,48},{64,5... | collective-permute-start | bytes 98312 | tf_op jit(solution)/shard_map/ppermute | solution.py:431
  6.3 6.9 %collective-permute-start.6 = (f32[4,4,4,128]{3,2,1,0:T(4,128)S(1)}, f32[4,4,4,128]{3,2,1,0:T(4,128)S(1)}, u32[]{:S(2)}, u32[]{:S(2)}) collective-permute-start(f32[4,4,4,128]{3,2,1,0:T(4,128)S(1)} %get-tuple-element.25), channel_id=1, source_target_pairs={{0,8},{8,16},{16,24},{24,32},{32,40},{40,48},{48,56},{56,64},{64,7... | collective-permute-start | bytes 98312 | tf_op jit(solution)/shard_map/ppermute | solution.py:431
  7.5 10.9 %collective-permute-start = (f32[2,8,2,8,128]{4,3,2,1,0:T(8,128)S(1)}, f32[2,8,2,8,128]{4,3,2,1,0:T(8,128)S(1)}, u32[]{:S(2)}, u32[]{:S(2)}) collective-permute-start(f32[2,8,2,8,128]{4,3,2,1,0:T(8,128)S(1)} %get-tuple-element.22), channel_id=1, source_target_pairs={{0,1},{1,2},{2,3},{3,4},{4,5},{5,6},{6,7},{7,0},{8,9},{9,10},{10,1... | collective-permute-start | bytes 393224 | tf_op jit(solution)/shard_map/ppermute | solution.py:431
  8.5 10.0 %collective-permute-start.1 = (f32[2,8,2,8,128]{4,3,2,1,0:T(8,128)S(1)}, f32[2,8,2,8,128]{4,3,2,1,0:T(8,128)S(1)}, u32[]{:S(2)}, u32[]{:S(2)}) collective-permute-start(f32[2,8,2,8,128]{4,3,2,1,0:T(8,128)S(1)} %get-tuple-element.23), channel_id=1, source_target_pairs={{0,7},{1,0},{2,1},{3,2},{4,3},{5,4},{6,5},{7,6},{8,15},{9,8},{10,9... | collective-permute-start | bytes 393224 | tf_op jit(solution)/shard_map/ppermute | solution.py:431
  14.3 28.8 %all-to-all-start.1 = ((f32[8,12,4,4,128]{4,3,2,1,0:T(4,128)}), f32[8,12,4,4,128]{4,3,2,1,0:T(4,128)S(1)}, u32[]{:S(2)}, u32[]{:S(2)}) async-start(f32[8,12,4,4,128]{4,3,2,1,0:T(4,128)} %broadcast_in_dim.9), calls=%async_computation.1 | async-start | bytes 1572864 | tf_op jit(solution)/shard_map/all_to_all | solution.py:439
  18.5 10.2 %collective-permute-start.2 = (f32[2,2,12,8,128]{4,3,2,1,0:T(8,128)S(1)}, f32[2,2,12,8,128]{4,3,2,1,0:T(8,128)S(1)}, u32[]{:S(2)}, u32[]{:S(2)}) collective-permute-start(f32[2,2,12,8,128]{4,3,2,1,0:T(8,128)S(1)} %pad_maximum_fusion), channel_id=1, source_target_pairs={{0,8},{8,16},{16,24},{24,32},{32,40},{40,48},{48,56},{56,64},{64,7... | collective-permute-start | bytes 589832 | tf_op jit(solution)/shard_map/ppermute | solution.py:431
  19.5 11.7 %collective-permute-start.3 = (f32[2,2,12,8,128]{4,3,2,1,0:T(8,128)S(1)}, f32[2,2,12,8,128]{4,3,2,1,0:T(8,128)S(1)}, u32[]{:S(2)}, u32[]{:S(2)}) collective-permute-start(f32[2,2,12,8,128]{4,3,2,1,0:T(8,128)S(1)} %pad_maximum_fusion.1), channel_id=1, source_target_pairs={{0,248},{8,0},{16,8},{24,16},{32,24},{40,32},{48,40},{56,48},{64,5... | collective-permute-start | bytes 589832 | tf_op jit(solution)/shard_map/ppermute | solution.py:431
  33.1 0.6 copy-start.6
  33.7 0.6 copy-start.11
  34.3 4.8 %collective-permute-start.5 = (f32[4,4,4,128]{3,2,1,0:T(4,128)S(1)}, f32[4,4,4,128]{3,2,1,0:T(4,128)S(1)}, u32[]{:S(2)}, u32[]{:S(2)}) collective-permute-start(f32[4,4,4,128]{3,2,1,0:T(4,128)S(1)} %get-tuple-element.24), channel_id=1, source_target_pairs={{0,248},{8,0},{16,8},{24,16},{32,24},{40,32},{48,40},{56,48},{64,5... | collective-permute-start | bytes 98312 | tf_op jit(solution)/shard_map/ppermute | solution.py:431
  36.9 6.1 %collective-permute-start.4 = (f32[4,4,4,128]{3,2,1,0:T(4,128)S(1)}, f32[4,4,4,128]{3,2,1,0:T(4,128)S(1)}, u32[]{:S(2)}, u32[]{:S(2)}) collective-permute-start(f32[4,4,4,128]{3,2,1,0:T(4,128)S(1)} %get-tuple-element.24), channel_id=1, source_target_pairs={{0,8},{8,16},{16,24},{24,32},{32,40},{40,48},{48,56},{56,64},{64,7... | collective-permute-start | bytes 98312 | tf_op jit(solution)/shard_map/ppermute | solution.py:431
  44.1 13.8 %all-to-all-start = ((f32[8,12,4,4,128]{4,3,2,1,0:T(4,128)}), f32[8,12,4,4,128]{4,3,2,1,0:T(4,128)S(1)}, u32[]{:S(2)}, u32[]{:S(2)}) async-start(f32[8,12,4,4,128]{4,3,2,1,0:T(4,128)} %broadcast_in_dim.8), calls=%async_computation | async-start | bytes 1572864 | tf_op jit(solution)/shard_map/all_to_all | solution.py:439
  58.7 19.2 %all-to-all-start.3 = ((f32[8,2,2,16,128]{4,3,2,1,0:T(8,128)}), f32[8,2,2,16,128]{4,3,2,1,0:T(8,128)S(1)}, u32[]{:S(2)}, u32[]{:S(2)}) async-start(f32[8,2,2,16,128]{4,3,2,1,0:T(8,128)} %broadcast_in_dim.11), calls=%async_computation.3 | async-start | bytes 524288 | tf_op jit(solution)/shard_map/all_to_all | solution.py:450
  70.7 0.8 copy-start
  71.5 0.8 copy-start.2
  72.3 0.6 copy-start.7
  72.9 0.6 copy-start.9
  78.6 42.4 %copy-start.3 = (f32[8,4,32,128]{3,2,1,0:T(8,128)S(1)}, f32[8,4,32,128]{3,2,1,0:T(8,128)}, u32[]{:S(2)}) copy-start(f32[8,4,32,128]{3,2,1,0:T(8,128)} %copy-done.2) | copy-start | bytes 1572868
  78.6 12.9 %all-to-all-start.2 = ((f32[8,2,2,16,128]{4,3,2,1,0:T(8,128)}), f32[8,2,2,16,128]{4,3,2,1,0:T(8,128)S(1)}, u32[]{:S(2)}, u32[]{:S(2)}) async-start(f32[8,2,2,16,128]{4,3,2,1,0:T(8,128)} %broadcast_in_dim.10), calls=%async_computation.2 | async-start | bytes 524288 | tf_op jit(solution)/shard_map/all_to_all | solution.py:450
  82.2 38.8 %copy-start.1 = (f32[8,4,32,128]{3,2,1,0:T(8,128)S(1)}, f32[8,4,32,128]{3,2,1,0:T(8,128)}, u32[]{:S(2)}) copy-start(f32[8,4,32,128]{3,2,1,0:T(8,128)} %copy-done) | copy-start | bytes 1572868
  82.2 5.5 %collective-permute-start.16 = (f32[8,2,8,128]{3,2,1,0:T(8,128)}, f32[8,2,8,128]{3,2,1,0:T(8,128)S(1)}, u32[]{:S(2)}, u32[]{:S(2)}) collective-permute-start(f32[8,2,8,128]{3,2,1,0:T(8,128)} %copy-done.11), channel_id=1, source_target_pairs={{0,1},{1,2},{2,3},{3,4},{4,5},{5,6},{6,7},{7,0},{8,9},{9,10},{10,1... | collective-permute-start | bytes 196616 | tf_op jit(solution)/shard_map/ppermute | solution.py:431
  83.0 11.0 %collective-permute-start.17 = (f32[8,2,8,128]{3,2,1,0:T(8,128)}, f32[8,2,8,128]{3,2,1,0:T(8,128)}, u32[]{:S(2)}, u32[]{:S(2)}) collective-permute-start(f32[8,2,8,128]{3,2,1,0:T(8,128)} %copy-done.6), channel_id=1, source_target_pairs={{0,7},{1,0},{2,1},{3,2},{4,3},{5,4},{6,5},{7,6},{8,15},{9,8},{10,9... | collective-permute-start | bytes 196616 | tf_op jit(solution)/shard_map/ppermute | solution.py:431
  88.3 12.4 %collective-permute-start.11 = (f32[8,2,2,16,128]{4,3,2,1,0:T(8,128)S(1)}, f32[8,2,2,16,128]{4,3,2,1,0:T(8,128)}, u32[]{:S(2)}, u32[]{:S(2)}) collective-permute-start(f32[8,2,2,16,128]{4,3,2,1,0:T(8,128)S(1)} %all-to-all-done.3.ca), channel_id=1, source_target_pairs={{0,16},{8,24},{16,0},{24,8},{32,48},{40,56},{48,32},{56,40},{64,80... | collective-permute-start | bytes 786440 | tf_op jit(solution)/shard_map/ppermute | solution.py:435
  91.5 10.4 %collective-permute-start.8 = (f32[8,2,2,16,128]{4,3,2,1,0:T(8,128)S(1)}, f32[8,2,2,16,128]{4,3,2,1,0:T(8,128)S(1)}, u32[]{:S(2)}, u32[]{:S(2)}) collective-permute-start(f32[8,2,2,16,128]{4,3,2,1,0:T(8,128)S(1)} %all-to-all-done.2.ra), channel_id=1, source_target_pairs={{0,16},{8,24},{16,0},{24,8},{32,48},{40,56},{48,32},{56,40},{64,80... | collective-permute-start | bytes 786440 | tf_op jit(solution)/shard_map/ppermute | solution.py:435
  94.8 9.9 %copy-start.12 = (f32[2,8,8,128]{3,2,1,0:T(8,128)S(1)}, f32[2,8,8,128]{3,2,1,0:T(8,128)}, u32[]{:S(2)}) copy-start(f32[2,8,8,128]{3,2,1,0:T(8,128)} %get-tuple-element.40) | copy-start | bytes 196612
  94.8 9.9 %copy-start.13 = (f32[2,2,8,128]{3,2,1,0:T(8,128)S(1)}, f32[2,2,8,128]{3,2,1,0:T(8,128)}, u32[]{:S(2)}) copy-start(f32[2,2,8,128]{3,2,1,0:T(8,128)} %get-tuple-element.46) | copy-start | bytes 49156
  95.6 9.1 %collective-permute-start.18 = (f32[2,12,8,128]{3,2,1,0:T(8,128)S(1)}, f32[2,12,8,128]{3,2,1,0:T(8,128)S(1)}, u32[]{:S(2)}, u32[]{:S(2)}) collective-permute-start(f32[2,12,8,128]{3,2,1,0:T(8,128)S(1)} %pad_maximum_fusion.4), channel_id=1, source_target_pairs={{0,8},{8,16},{16,24},{24,32},{32,40},{40,48},{48,56},{56,64},{64,7... | collective-permute-start | bytes 294920 | tf_op jit(solution)/shard_map/ppermute | solution.py:431
  100.7 20.3 %collective-permute-start.12 = (f32[8,2,2,16,128]{4,3,2,1,0:T(8,128)S(1)}, f32[8,2,2,16,128]{4,3,2,1,0:T(8,128)S(1)}, u32[]{:S(2)}, u32[]{:S(2)}) collective-permute-start(f32[8,2,2,16,128]{4,3,2,1,0:T(8,128)S(1)} %all-to-all-done.3.ca), channel_id=1, source_target_pairs={{0,8},{8,0},{16,24},{24,16},{32,40},{40,32},{48,56},{56,48},{64,72... | collective-permute-start | bytes 786440 | tf_op jit(solution)/shard_map/ppermute | solution.py:435
  100.7 20.3 %collective-permute-start.13 = (f32[8,2,2,16,128]{4,3,2,1,0:T(8,128)}, f32[8,2,2,16,128]{4,3,2,1,0:T(8,128)S(1)}, u32[]{:S(2)}, u32[]{:S(2)}) collective-permute-start(f32[8,2,2,16,128]{4,3,2,1,0:T(8,128)} %collective-permute-done.11.cb), channel_id=1, source_target_pairs={{0,8},{8,0},{16,24},{24,16},{32,40},{40,32},{48,56},{56,48},{64,72... | collective-permute-start | bytes 786440 | tf_op jit(solution)/shard_map/ppermute | solution.py:435
  102.0 19.0 %collective-permute-start.9 = (f32[8,2,2,16,128]{4,3,2,1,0:T(8,128)S(1)}, f32[8,2,2,16,128]{4,3,2,1,0:T(8,128)S(1)}, u32[]{:S(2)}, u32[]{:S(2)}) collective-permute-start(f32[8,2,2,16,128]{4,3,2,1,0:T(8,128)S(1)} %all-to-all-done.2.ra), channel_id=1, source_target_pairs={{0,8},{8,0},{16,24},{24,16},{32,40},{40,32},{48,56},{56,48},{64,72... | collective-permute-start | bytes 786440 | tf_op jit(solution)/shard_map/ppermute | solution.py:435
  102.0 19.0 %collective-permute-start.10 = (f32[8,2,2,16,128]{4,3,2,1,0:T(8,128)S(1)}, f32[8,2,2,16,128]{4,3,2,1,0:T(8,128)S(1)}, u32[]{:S(2)}, u32[]{:S(2)}) collective-permute-start(f32[8,2,2,16,128]{4,3,2,1,0:T(8,128)S(1)} %collective-permute-done.8.rb), channel_id=1, source_target_pairs={{0,8},{8,0},{16,24},{24,16},{32,40},{40,32},{48,56},{56,48},{64,72... | collective-permute-start | bytes 786440 | tf_op jit(solution)/shard_map/ppermute | solution.py:435
  104.7 5.8 %copy-start.10 = (f32[4,32,128]{2,1,0:T(8,128)S(1)}, f32[4,32,128]{2,1,0:T(8,128)}, u32[]{:S(2)}) copy-start(f32[4,32,128]{2,1,0:T(8,128)} %copy-done.9) | copy-start | bytes 196612
  104.7 8.8 %copy-start.8 = (f32[4,32,128]{2,1,0:T(8,128)S(1)}, f32[4,32,128]{2,1,0:T(8,128)}, u32[]{:S(2)}) copy-start(f32[4,32,128]{2,1,0:T(8,128)} %copy-done.7) | copy-start | bytes 196612
  104.7 5.7 %collective-permute-start.19 = (f32[2,12,8,128]{3,2,1,0:T(8,128)S(1)}, f32[2,12,8,128]{3,2,1,0:T(8,128)S(1)}, u32[]{:S(2)}, u32[]{:S(2)}) collective-permute-start(f32[2,12,8,128]{3,2,1,0:T(8,128)S(1)} %pad_maximum_fusion.5), channel_id=1, source_target_pairs={{0,248},{8,0},{16,8},{24,16},{32,24},{40,32},{48,40},{56,48},{64,5... | collective-permute-start | bytes 294920 | tf_op jit(solution)/shard_map/ppermute | solution.py:431
  110.4 3.0 %collective-permute-start.14 = (f32[4,32,128]{2,1,0:T(8,128)S(1)}, f32[4,32,128]{2,1,0:T(8,128)S(1)}, u32[]{:S(2)}, u32[]{:S(2)}) collective-permute-start(f32[4,32,128]{2,1,0:T(8,128)S(1)} %copy-done.10), channel_id=1, source_target_pairs={{0,8},{8,16},{16,24},{24,32},{32,40},{40,48},{48,56},{56,64},{64,7... | collective-permute-start | bytes 196616 | tf_op jit(solution)/shard_map/ppermute | solution.py:431
  113.4 7.5 %collective-permute-start.15 = (f32[4,32,128]{2,1,0:T(8,128)S(1)}, f32[4,32,128]{2,1,0:T(8,128)S(1)}, u32[]{:S(2)}, u32[]{:S(2)}) collective-permute-start(f32[4,32,128]{2,1,0:T(8,128)S(1)} %copy-done.8), channel_id=1, source_target_pairs={{0,248},{8,0},{16,8},{24,16},{32,24},{40,32},{48,40},{56,48},{64,5... | collective-permute-start | bytes 196616 | tf_op jit(solution)/shard_map/ppermute | solution.py:431
where the time goes:
time: 138 us
  starting transfers between devices  68.1 us (49%)
  waiting for transfers between devices  34 us (25%)
  Pallas kernels  22.2 us (16%)
  local copies, waits for them, and re-layouts  11.5 us (8%)
    ppermute x14, starting transfers between devices, shifted(): lax.ppermute(v, axis, [(i, (i + step) % count) for i in range(count)])  36.4 us
    ppermute x14, waiting for transfers between devices, shifted(): lax.ppermute(v, axis, [(i, (i + step) % count) for i in range(count)])  21.4 us
    pallas_call x1, Pallas kernels, up(): pl.pallas_call(up_kernel, out_shape=(shape(8, 8, 1024), shape(8, 8, 1024)...  16.6 us
    all_to_all x2, starting transfers between devices, gather_x(): lax.all_to_all(jnp.broadcast_to(v[None], (8,) + v.shape), 'gx', 0, 0, axi...  13.2 us
    all_to_all x2, starting transfers between devices, gather_y(): lax.all_to_all(jnp.broadcast_to(v[None], (GY,) + v.shape), 'gy', 0, 0)  9.55 us
    ppermute x6, starting transfers between devices, swapped(): return lax.ppermute(v, 'gx', [(i, i ^ bit) for i in range(GX)])  8.9 us
    all_to_all x2, waiting for transfers between devices, gather_y(): lax.all_to_all(jnp.broadcast_to(v[None], (GY,) + v.shape), 'gy', 0, 0)  7.44 us
    unnamed x28, local copies, waits for them, and re-layouts  5.99 us
  transfers between devices with their start and end apart: 24, of which 12 were waited for; matrix products, arithmetic and copies ran while one was open for 3% of the time, Pallas kernels for 4%

commit v1 on v0

--- a/solution.py
+++ b/solution.py
@@ -170,146 +170,139 @@
     )(f, sg, ylo, yhi, xlo, xhi)
 
 
-def assemble_y(index_ref, blocks_ref, out_ref):
-    me = index_ref[1]
-    for k in range(8):
-        source = lax.rem(me + (k + 4), 8)
-        out_ref[:, :, 4 * k : 4 * k + 4, :] = blocks_ref[source]
-
-
-def coefficients_kernel(index_ref, blocks_ref, g1_ref, c2_ref, field, pairs):
-    assemble_y(index_ref, blocks_ref, field)
-    g1_ref[...] = OMEGA / (6.0 + 4.0 * field[...])
-    for x in range(2):
-        row = field[4 + 2 * x] + field[5 + 2 * x]
-        for c in range(2):
-            pairs[x, c] = row[2 * c] + row[2 * c + 1]
-            c2_ref[x, c] = 0.125 * (
-                pairs[x, c, pl.ds(0, 16, stride=2), :] + pairs[x, c, pl.ds(1, 16, stride=2), :]
-            )
-
-
-def coefficients(index, blocks):
+def core_of(index_ref):
+    return lax.rem(index_ref[0], 2)
+
+
+def assemble(index_ref, pieces, out_ref):
+    core = core_of(index_ref)
+    own, pair, outer, skip, far = pieces
+    places = ((own, 6, 4), (pair, 10 - 8 * core, 4), (outer, 2 + 8 * core, 4), (skip, 14 * core, 2), (far, 14 - 14 * core, 2))
+    for piece, base, count in places:
+        for k in range(8):
+            source = lax.rem(index_ref[1] + (k + 4), 8)
+            out_ref[pl.ds(base, count), :, 4 * k : 4 * k + 4, :] = piece[source]
+
+
+def restrict_middle(ref, x, pairs, scale):
+    row = ref[x] + ref[x + 1]
+    parts = []
+    for c in range(2):
+        pairs[c] = row[2 * c] + row[2 * c + 1]
+        parts.append(scale * (pairs[c, pl.ds(0, 16, stride=2), :] + pairs[c, pl.ds(1, 16, stride=2), :]))
+    return jnp.stack(parts, 0)
+
+
+def restrict_coarse(upper, lower, pairs, scale):
+    row = upper + lower
+    pairs[0, 0:16] = row[0] + row[1]
+    return scale * (pairs[0, pl.ds(0, 8, stride=2), :] + pairs[0, pl.ds(1, 8, stride=2), :])
+
+
+def coefficients_kernel(index_ref, own, pair, outer, skip, far, g1_ref, g2_ref, c3_ref, field, c2, pairs):
+    assemble(index_ref, (own, pair, outer, skip, far), field)
+
+    def scale1(x, carry):
+        g1_ref[x] = OMEGA / (6.0 + 4.0 * field[x])
+        return carry
+
+    lax.fori_loop(0, 16, scale1, 0)
+    for x in range(8):
+        c2[x] = restrict_middle(field, 2 * x, pairs, 0.125)
+        g2_ref[x] = OMEGA / (6.0 + 16.0 * c2[x])
+    c3_ref[...] = restrict_coarse(c2[3], c2[4], pairs, 0.125)
+
+
+def coefficients(index, *pieces):
     return pl.pallas_call(
         coefficients_kernel,
-        out_shape=(shape(12, 4, 32, 128), shape(2, 2, 16, 128)),
-        in_specs=[smem(), vmem()],
-        scratch_shapes=[pltpu.VMEM((12, 4, 32, 128), F32), pltpu.VMEM((2, 2, 32, 128), F32)],
+        out_shape=(shape(16, 4, 32, 128), shape(8, 2, 16, 128), shape(8, 128)),
+        in_specs=[smem()] + [vmem()] * 5,
+        scratch_shapes=[pltpu.VMEM((16, 4, 32, 128), F32), pltpu.VMEM((8, 2, 16, 128), F32), pltpu.VMEM((2, 32, 128), F32)],
         compiler_params=params(),
-    )(index, blocks)
-
-
-def middle_down_kernel(index_ref, blocks_ref, g_ref, f2_ref, src_ref, flo_ref, fhi_ref, rhs2_ref, rhs, s0, s1, pairs):
-    assemble_y(index_ref, blocks_ref, rhs)
-    s0[...] = g_ref[...] * rhs[...]
+    )(index, *pieces)
+
+
+def middle_down_kernel(
+    index_ref, own, pair, outer, skip, far, g1_ref, g2_ref, c3_ref,
+    f1_ref, src1_ref, fs2_ref, part2_ref, both3_ref,
+    rhs, s0, s1, f2, rhs2, t0, t1, pairs,
+):
+    assemble(index_ref, (own, pair, outer, skip, far), rhs)
+
+    def start(x, carry):
+        s0[x] = g1_ref[x] * rhs[x]
+        return carry
+
+    lax.fori_loop(0, 16, start, 0)
 
     def first(x, carry):
         total = coarse_neighbours(s0, x)
-        s1[x] = THIRD * s0[x] + g_ref[x] * total
+        s1[x] = THIRD * s0[x] + g1_ref[x] * total
         rhs[x] = THIRD * rhs[x] + total
         return carry
 
-    lax.fori_loop(1, 11, first, 0)
+    lax.fori_loop(1, 15, first, 0)
 
     def second(x, carry):
-        f2_ref[x - 2] = THIRD * rhs[x] + coarse_neighbours(s1, x)
-        src_ref[x - 2] = s0[x] + s1[x]
-        return carry
-
-    lax.fori_loop(2, 10, second, 0)
-    flo_ref[...] = f2_ref[3]
-    fhi_ref[...] = f2_ref[4]
-    for x in range(2):
-        row = f2_ref[2 + 2 * x] + f2_ref[3 + 2 * x]
-        for c in range(2):
-            pairs[x, c] = row[2 * c] + row[2 * c + 1]
-            rhs2_ref[x, c] = pairs[x, c, pl.ds(0, 16, stride=2), :] + pairs[x, c, pl.ds(1, 16, stride=2), :]
-
-
-def middle_down(index, blocks, g1):
+        f2[x - 2] = THIRD * rhs[x] + coarse_neighbours(s1, x)
+        return carry
+
+    lax.fori_loop(2, 14, second, 0)
+    f1_ref[...] = f2[1:11]
+    src1_ref[...] = s0[4:12] + s1[4:12]
+
+    for x in range(6):
+        row = restrict_middle(f2, 2 * x, pairs, 1.0)
+        rhs2[x] = row
+        t0[x] = g2_ref[x + 1] * row
+    for x in range(1, 5):
+        total = coarse_neighbours(t0, x)
+        t1[x] = THIRD * t0[x] + g2_ref[x + 1] * total
+        rhs2[x] = THIRD * rhs2[x] + total
+    for x in range(2, 4):
+        fs2_ref[0, x - 2] = THIRD * rhs2[x] + coarse_neighbours(t1, x)
+        fs2_ref[1, x - 2] = t0[x] + t1[x]
+    part2_ref[...] = fs2_ref[0, 1 - core_of(index_ref)]
+    both3_ref[0] = restrict_coarse(fs2_ref[0, 0], fs2_ref[0, 1], pairs, 1.0)
+    both3_ref[1] = c3_ref[...]
+
+
+def middle_down(index, pieces, g1, g2, c3):
     return pl.pallas_call(
         middle_down_kernel,
         out_shape=(
+            shape(10, 4, 32, 128),
             shape(8, 4, 32, 128),
-            shape(8, 4, 32, 128),
-            shape(4, 32, 128),
-            shape(4, 32, 128),
-            shape(2, 2, 16, 128),
+            shape(2, 2, 2, 16, 128),
+            shape(2, 16, 128),
+            shape(2, 8, 128),
         ),
-        in_specs=[smem(), vmem(), vmem()],
-        scratch_shapes=[
-            pltpu.VMEM((12, 4, 32, 128), F32),
-            pltpu.VMEM((12, 4, 32, 128), F32),
-            pltpu.VMEM((12, 4, 32, 128), F32),
-            pltpu.VMEM((2, 2, 32, 128), F32),
-        ],
+        in_specs=[smem()] + [vmem()] * 8,
+        scratch_shapes=[pltpu.VMEM((16, 4, 32, 128), F32)] * 3
+        + [pltpu.VMEM((12, 4, 32, 128), F32)]
+        + [pltpu.VMEM((6, 2, 16, 128), F32)] * 3
+        + [pltpu.VMEM((2, 32, 128), F32)],
         compiler_params=params(),
-    )(index, blocks, g1)
-
-
-def place_x(index_ref, pieces, out_ref):
-    me = index_ref[0]
-    z_me = lax.div(me, 4)
-    step_y = 4 - 8 * lax.rem(lax.div(me, 2), 2)
-    step_core = 2 - 4 * lax.rem(me, 2)
-    offsets = (0, step_y, step_core, step_y + step_core)
-    for piece, offset in zip(pieces, offsets):
-        for k in range(8):
-            source = lax.rem(z_me + (k + 4), 8)
-            target = lax.rem(8 * k + offset + 64, 64)
-            out_ref[pl.ds(target, 2)] = piece[source]
+    )(index, *pieces, g1, g2, c3)
 
 
 def up_kernel(
-    index_ref, ra, rb, rc, rd, ca, cb, cc, cd, g1_ref, f1_ref, src1_ref, f1lo_ref, f1hi_ref,
+    index_ref, mine3, other3, fs2, pair2, outer2, skip2, far2, g2_ref, g1_ref, f1_ref, src1_ref,
     g0_ref, f0_ref, src0_ref, fylo_ref, fyhi_ref, fxlo_ref, fxhi_ref,
     guess_ref, source_ref,
-    rhs2, g2, p2, q2, out3, e3, pairs3, win2, r2, sa2, out2, r1, sa1, out1, pairs1,
+    e3, out3, f2, src2, r2, sa2, out2, r1, sa1, out1,
     rep, r0, f0, s3, s4, turned, placed,
 ):
-    place_x(index_ref, (ra, rb, rc, rd), rhs2)
-    place_x(index_ref, (ca, cb, cc, cd), g2)
-
-    def restrict2(x, ref):
-        row = ref[2 * x] + ref[2 * x + 1]
-        pairs3[x] = row[0] + row[1]
-        return pairs3[x, pl.ds(0, 8, stride=2), :] + pairs3[x, pl.ds(1, 8, stride=2), :]
-
-    def scale2(x, carry):
-        g3 = OMEGA / (6.0 + 64.0 * 0.125 * restrict2(x, g2))
-        e3[1, x] = g3
-        for r in range(2):
-            row = 2 * x + r
-            g = OMEGA / (6.0 + 16.0 * g2[row])
-            g2[row] = g
-            p2[row + 1] = g * rhs2[row]
-        return carry
-
-    lax.fori_loop(0, 32, scale2, 0)
-    p2[0] = p2[64]
-    p2[65] = p2[1]
-
-    def first2(x, carry):
-        total = coarse_neighbours(p2, x)
-        q2[x] = THIRD * p2[x] + g2[x - 1] * total
-        rhs2[x - 1] = THIRD * rhs2[x - 1] + total
-        return carry
-
-    lax.fori_loop(1, 65, first2, 0)
-    q2[0] = q2[64]
-    q2[65] = q2[1]
-
-    def second2(x, carry):
-        for r in range(2):
-            row = 2 * x + r
-            rhs2[row] = THIRD * rhs2[row] + coarse_neighbours(q2, row + 1)
-        e3[0, x] = restrict2(x, rhs2)
-        return carry
-
-    lax.fori_loop(0, 32, second2, 0)
-
-    g3 = e3[1]
-    s = g3 * e3[0]
+    core = core_of(index_ref)
+    chip = lax.div(index_ref[0], 2)
+
+    for k in range(16):
+        source = lax.rem(chip + (k + 8), 16)
+        e3[2 * k + core] = mine3[source]
+        e3[2 * k + 1 - core] = other3[source]
+    g3 = OMEGA / (6.0 + 64.0 * e3[:, 1])
+    s = g3 * e3[:, 0]
     acc = s
     for sweep in range(7):
         total = jnp.concatenate([s[1:], s[:1]], 0) + jnp.concatenate([s[31:], s[:31]], 0)
@@ -319,18 +312,31 @@
         acc = acc + s
     out3[...] = 0.5 * acc
 
+    f2[2:4] = fs2[0]
+    src2[2:4] = fs2[1]
+    f2[pl.ds(4 - 4 * core, 2)] = pair2[0]
+    src2[pl.ds(4 - 4 * core, 2)] = pair2[1]
+    f2[pl.ds(4 * core, 2)] = outer2[0]
+    src2[pl.ds(4 * core, 2)] = outer2[1]
+
+    def row2(x):
+        if x == 1:
+            return jnp.where(core == 0, skip2[...], far2[...])
+        if x == 8:
+            return jnp.where(core == 0, far2[...], skip2[...])
+        return f2[x - 2]
+
     for x in range(10):
-        half = out3[14 + x // 2]
+        half = out3[14 + core + x // 2]
         for c in range(2):
             r2[x, c, pl.ds(0, 8, stride=2), :] = half
             r2[x, c, pl.ds(1, 8, stride=2), :] = half
     for x in range(1, 9):
-        g = g2[28 + x]
-        f = rhs2[28 + x] - (OMEGA / g) * r2[x] + coarse_neighbours(r2, x)
-        sa2[x] = g * f
+        g = g2_ref[x - 1]
+        sa2[x] = g * (row2(x) - (OMEGA / g) * r2[x] + coarse_neighbours(r2, x))
     for x in range(2, 8):
-        sb = THIRD * sa2[x] + g2[28 + x] * coarse_neighbours(sa2, x)
-        out2[x - 2] = 0.5 * (p2[29 + x] + q2[29 + x] + r2[x] + sa2[x] + sb)
+        sb = THIRD * sa2[x] + g2_ref[x - 1] * coarse_neighbours(sa2, x)
+        out2[x - 2] = 0.5 * (src2[x - 2] + r2[x] + sa2[x] + sb)
 
     for x in range(12):
         for c in range(4):
@@ -338,21 +344,15 @@
             r1[x, c, pl.ds(0, 16, stride=2), :] = half
             r1[x, c, pl.ds(1, 16, stride=2), :] = half
 
-    def residual1(x, f):
-        g = g1_ref[x]
-        sa1[x] = g * (f - (OMEGA / g) * r1[x] + coarse_neighbours(r1, x))
-
-    residual1(1, f1lo_ref[...])
-    residual1(10, f1hi_ref[...])
-
     def middle1(x, carry):
-        residual1(x, f1_ref[x - 2])
-        return carry
-
-    lax.fori_loop(2, 10, middle1, 0)
+        g = g1_ref[x + 2]
+        sa1[x] = g * (f1_ref[x - 1] - (OMEGA / g) * r1[x] + coarse_neighbours(r1, x))
+        return carry
+
+    lax.fori_loop(1, 11, middle1, 0)
 
     def last1(x, carry):
-        sb = THIRD * sa1[x] + g1_ref[x] * coarse_neighbours(sa1, x)
+        sb = THIRD * sa1[x] + g1_ref[x + 2] * coarse_neighbours(sa1, x)
         row = 0.5 * (src1_ref[x - 2] + r1[x] + sa1[x] + sb)
         for c in range(4):
             out1[x - 2, pl.ds(32 * c, 32), :] = row[c]
@@ -411,10 +411,9 @@
 
 def up(index, *arrays):
     scratch = [
-        (64, 2, 16, 128), (64, 2, 16, 128), (66, 2, 16, 128), (66, 2, 16, 128),
-        (32, 8, 128), (2, 32, 8, 128), (32, 16, 128), (8, 128),
+        (32, 2, 8, 128), (32, 8, 128), (6, 2, 16, 128), (6, 2, 16, 128),
         (10, 2, 16, 128), (10, 2, 16, 128), (6, 2, 16, 128),
-        (12, 4, 32, 128), (12, 4, 32, 128), (8, 128, 128), (8, 128),
+        (12, 4, 32, 128), (12, 4, 32, 128), (8, 128, 128),
         (8, 128), (16, 16, 8, 128), (12, 12, 8, 128), (12, 12, 8, 128), (12, 12, 8, 128),
         (1024, 128), (1024, 128),
     ]
@@ -431,28 +430,32 @@
     return lax.ppermute(v, axis, [(i, (i + step) % count) for i in range(count)])
 
 
-def swapped(v, bit):
-    return lax.ppermute(v, "gx", [(i, i ^ bit) for i in range(GX)])
+def swap_core(v):
+    return lax.ppermute(v, "gx", [(i, i ^ 1) for i in range(GX)])
+
+
+def swap_outer(v):
+    return lax.ppermute(v, "gx", [(i, (i + 1 if i % 2 else i - 1) % GX) for i in range(GX)])
+
+
+def skip_chip(v):
+    return lax.ppermute(v, "gx", [(i, (i - 2 if i % 2 else i + 2) % GX) for i in range(GX)])
 
 
 def gather_y(v):
     return lax.all_to_all(jnp.broadcast_to(v[None], (GY,) + v.shape), "gy", 0, 0)
 
 
-def with_x_blocks(v):
-    before = shifted(v, "gx", GX, 1)
-    after = shifted(v, "gx", GX, -1)
-    return jnp.concatenate([before, v, after], axis=0)
-
-
-def gather_x(v):
-    groups = [[q + 4 * z for z in range(8)] for q in range(4)]
-    along = lax.all_to_all(jnp.broadcast_to(v[None], (8,) + v.shape), "gx", 0, 0, axis_index_groups=groups)
-    across = swapped(along, 2)
-    return along, across, swapped(along, 1), swapped(across, 1)
+def level1_rows(core, v):
+    pair = swap_core(v)
+    outer = swap_outer(v)
+    skip = skip_chip(jnp.where(core == 0, v[:, 2:4], v[:, 0:2]))
+    far = swap_core(jnp.where(core == 0, outer[:, 2:4], outer[:, 0:2]))
+    return v, pair, outer, skip, far
 
 
 def per_device(cotangent, diagonal):
+    core = lax.axis_index("gx") % 2
     index = jnp.stack([lax.axis_index("gx"), lax.axis_index("gy")]).astype(jnp.int32)
     f, sg, ylo, yhi, c1 = prepare(cotangent, diagonal)
 
@@ -461,8 +464,7 @@
     xhi = jnp.concatenate([ylo[:, 6:8], sg[:, 6:8], yhi[:, 6:8]], axis=2)
     xlo, xhi = shifted(xhi, "gx", GX, 1), shifted(xlo, "gx", GX, -1)
 
-    g1, c2 = coefficients(index, gather_y(with_x_blocks(c1)))
-    c2_pieces = gather_x(c2)
+    g1, g2, c3 = coefficients(index, *level1_rows(core, gather_y(c1)))
 
     f2, src0, g0, fylo, fyhi, rhs1 = fine_down(f, sg, ylo, yhi, xlo, xhi)
     fylo, fyhi = shifted(fyhi, "gy", GY, 1), shifted(fylo, "gy", GY, -1)
@@ -470,12 +472,16 @@
     fxhi = jnp.concatenate([fylo[6:8], f2[6:8], fyhi[6:8]], axis=1)
     fxlo, fxhi = shifted(fxhi, "gx", GX, 1), shifted(fxlo, "gx", GX, -1)
 
-    f1, src1, f1lo, f1hi, rhs2 = middle_down(index, gather_y(with_x_blocks(rhs1)), g1)
-    f1lo, f1hi = shifted(f1lo, "gx", GX, 1), shifted(f1hi, "gx", GX, -1)
-    rhs2_pieces = gather_x(rhs2)
+    f1, src1, fs2, part2, both3 = middle_down(index, level1_rows(core, gather_y(rhs1)), g1, g2, c3)
+    pair2, outer2, skip2 = swap_core(fs2), swap_outer(fs2), skip_chip(part2)
+    far2 = swap_core(jnp.where(core == 0, outer2[0, 1], outer2[0, 0]))
+
+    groups = [[c + 2 * k for k in range(16)] for c in range(2)]
+    mine3 = lax.all_to_all(jnp.broadcast_to(both3[None], (16,) + both3.shape), "gx", 0, 0, axis_index_groups=groups)
+    other3 = swap_core(mine3)
 
     return up(
-        index, *rhs2_pieces, *c2_pieces, g1, f1, src1, f1lo, f1hi, g0, f2, src0, fylo, fyhi, fxlo, fxhi
+        index, mine3, other3, fs2, pair2, outer2, skip2, far2, g2, g1, f1, src1, g0, f2, src0, fylo, fyhi, fxlo, fxhi
     )
 
 

time: 138 us -> 97.1 us (0.70)
  waiting for transfers between devices: 34 us -> 15 us
  starting transfers between devices: 68.1 us -> 54.3 us
  Pallas kernels: 22.2 us -> 16.1 us
  local copies, waits for them, and re-layouts: 11.5 us -> 7.75 us
    ppermute x14 -> x8, waiting for transfers between devices: 21.4 us -> 0.75 us  [shifted(): lax.ppermute(v, axis, [(i, (i + step) % count) for i in range(count)])]
    ppermute x14 -> x8, starting transfers between devices: 36.4 us -> 19.3 us  [shifted(): lax.ppermute(v, axis, [(i, (i + step) % count) for i in range(count)])]
    ppermute x6 -> x13, starting transfers between devices: 8.9 us -> 20.1 us  [the longest x3 13.6 us: skip_chip(): lax.ppermute(v, 'gx', [(i, (i - 2 if i % 2 else i + 2) % GX) for i in ran...]
    ppermute x6 -> x13, waiting for transfers between devices: 0.02 us -> 10.5 us  [the longest x3 10.3 us: swap_outer(): lax.ppermute(v, 'gx', [(i, (i + 1 if i % 2 else i - 1) % GX) for i in ran...]
    pallas_call x1, Pallas kernels: 16.6 us -> 8.01 us  [up(): pl.pallas_call(up_kernel, out_shape=(shape(8, 8, 1024), shape(8, 8, 1024)...]
    all_to_all x2 -> x1, starting transfers between devices: 13.2 us -> 7.1 us  [per_device(): lax.all_to_all(jnp.broadcast_to(both3[None], (16,) + both3.shape), 'gx',...]
    all_to_all x2 -> x1, waiting for transfers between devices: 5.06 us -> 0.01 us  [per_device(): lax.all_to_all(jnp.broadcast_to(both3[None], (16,) + both3.shape), 'gx',...]
    all_to_all x2, waiting for transfers between devices: 7.44 us -> 3.74 us  [gather_y(): lax.all_to_all(jnp.broadcast_to(v[None], (GY,) + v.shape), 'gy', 0, 0)]
  transfers between devices with their start and end apart: 24 -> 24, of which waited for: 12 -> 7; matrix products, arithmetic and copies ran while one was open for 3% -> 6% of each run, Pallas kernels for 4% -> 8%
where the time goes in v1:
time: 97.1 us; the launch traced here: 96.2 us
  starting transfers between devices  54.3 us (56%)
  Pallas kernels  16.1 us (17%)
  waiting for transfers between devices  15 us (15%)
  local copies, waits for them, and re-layouts  7.75 us (8%)
  other arithmetic  2.21 us (2%)
    ppermute x8, starting transfers between devices, shifted(): lax.ppermute(v, axis, [(i, (i + step) % count) for i in range(count)])  19.3 us
    ppermute x3, starting transfers between devices, skip_chip(): lax.ppermute(v, 'gx', [(i, (i - 2 if i % 2 else i + 2) % GX) for i in ran...  13.6 us
    ppermute x3, waiting for transfers between devices, swap_outer(): lax.ppermute(v, 'gx', [(i, (i + 1 if i % 2 else i - 1) % GX) for i in ran...  10.3 us
    pallas_call x1, Pallas kernels, up(): pl.pallas_call(up_kernel, out_shape=(shape(8, 8, 1024), shape(8, 8, 1024)...  8.01 us
    all_to_all x2, starting transfers between devices, gather_y(): lax.all_to_all(jnp.broadcast_to(v[None], (GY,) + v.shape), 'gy', 0, 0)  7.82 us
    all_to_all x1, starting transfers between devices, per_device(): lax.all_to_all(jnp.broadcast_to(both3[None], (16,) + both3.shape), 'gx',...  7.1 us
    ppermute x3, starting transfers between devices, swap_outer(): lax.ppermute(v, 'gx', [(i, (i + 1 if i % 2 else i - 1) % GX) for i in ran...  5.21 us
    unnamed x24, local copies, waits for them, and re-layouts  4.24 us
  transfers between devices with their start and end apart: 24, of which 7 were waited for; matrix products, arithmetic and copies ran while one was open for 6% of the time, Pallas kernels for 8%

profile of v1, /device:TPU:1, one launch (start us, length us, event | category | flops | bytes accessed | tf_op | source)
XLA Modules:
  0.0 96.2 jit_solution(16147769013023854662)
XLA Ops:
  0.6 0.9 copy-done.2
  1.6 0.9 copy-done.3
  2.5 0.5 shard_map.41
  3.0 2.2 %collective-permute-start = (f32[2,8,2,8,128]{4,3,2,1,0:T(8,128)S(1)}, f32[2,8,2,8,128]{4,3,2,1,0:T(8,128)S(1)}, u32[]{:S(2)}, u32[]{:S(2)}) collective-permute-start(f32[2,8,2,8,128]{4,3,2,1,0:T(8,128)S(1)} %get-tuple-element.23), channel_id=1, source_target_pairs={{0,1},{1,2},{2,3},{3,4},{4,5},{5,6},{6,7},{7,0},{8,9},{9,10},{10,1... | collective-permute-start | bytes 393224 | tf_op jit(solution)/shard_map/ppermute | solution.py:430
  5.2 2.3 %collective-permute-start.1 = (f32[2,8,2,8,128]{4,3,2,1,0:T(8,128)S(1)}, f32[2,8,2,8,128]{4,3,2,1,0:T(8,128)S(1)}, u32[]{:S(2)}, u32[]{:S(2)}) collective-permute-start(f32[2,8,2,8,128]{4,3,2,1,0:T(8,128)S(1)} %get-tuple-element.24), channel_id=1, source_target_pairs={{0,7},{1,0},{2,1},{3,2},{4,3},{5,4},{6,5},{7,6},{8,15},{9,8},{10,9... | collective-permute-start | bytes 393224 | tf_op jit(solution)/shard_map/ppermute | solution.py:430
  7.5 0.7 broadcast_in_dim.7
  8.3 3.4 %all-to-all-start.1 = ((f32[8,4,4,4,128]{4,3,2,1,0:T(4,128)}), f32[8,4,4,4,128]{4,3,2,1,0:T(4,128)S(1)}, u32[]{:S(2)}, u32[]{:S(2)}) async-start(f32[8,4,4,4,128]{4,3,2,1,0:T(4,128)} %broadcast_in_dim.7), calls=%async_computation.1 | async-start | bytes 524288 | tf_op jit(solution)/shard_map/all_to_all | solution.py:446
  11.7 0.1 pad_add_fusion.index_ref
  11.8 0.0 collective-permute-done.1.yhi_ref
  11.8 0.0 collective-permute-done.ylo_ref
  11.9 4.7 %collective-permute-start.2 = (f32[2,2,12,8,128]{4,3,2,1,0:T(8,128)S(1)}, f32[2,2,12,8,128]{4,3,2,1,0:T(8,128)S(1)}, u32[]{:S(2)}, u32[]{:S(2)}) collective-permute-start(f32[2,2,12,8,128]{4,3,2,1,0:T(8,128)S(1)} %pad_maximum_fusion), channel_id=1, source_target_pairs={{0,8},{8,16},{16,24},{24,32},{32,40},{40,48},{48,56},{56,64},{64,7... | collective-permute-start | bytes 589832 | tf_op jit(solution)/shard_map/ppermute | solution.py:430
  16.6 0.1 collective-permute-start.3
  16.7 0.7 all-to-all-done.1.own
  17.4 5.2 %collective-permute-start.9 = (f32[8,4,4,4,128]{4,3,2,1,0:T(4,128)S(1)}, f32[8,4,4,4,128]{4,3,2,1,0:T(4,128)S(1)}, u32[]{:S(2)}, u32[]{:S(2)}) collective-permute-start(f32[8,4,4,4,128]{4,3,2,1,0:T(4,128)S(1)} %all-to-all-done.1.own), channel_id=1, source_target_pairs={{0,248},{8,16},{16,8},{24,32},{32,24},{40,48},{48,40},{56,64},{64,... | collective-permute-start | bytes 786440 | tf_op jit(solution)/shard_map/ppermute | solution.py:438
  22.6 0.7 slice_select_fusion.1
  23.3 3.9 %collective-permute-start.10 = (f32[8,2,4,4,128]{4,3,2,1,0:T(4,128)}, f32[8,2,4,4,128]{4,3,2,1,0:T(4,128)S(1)}, u32[]{:S(2)}, u32[]{:S(2)}) collective-permute-start(f32[8,2,4,4,128]{4,3,2,1,0:T(4,128)} %slice_select_fusion.1), channel_id=1, source_target_pairs={{0,16},{8,248},{16,32},{24,8},{32,48},{40,24},{48,64},{56,40},{64,... | collective-permute-start | bytes 393224 | tf_op jit(solution)/shard_map/ppermute | solution.py:442
  27.2 0.0 collective-permute-done.2.xlo_ref
  27.2 0.0 collective-permute-done.3.xhi_ref
  27.2 2.5 %shard_map.42 = (f32[8,8,8,128]{3,2,1,0:T(8,128)S(1)}, f32[8,8,8,128]{3,2,1,0:T(8,128)S(1)}, f32[12,12,8,128]{3,2,1,0:T(8,128)S(1)}, f32[8,2,8,128]{3,2,1,0:T(8,...) custom-call(f32[8,8,8,128]{3,2,1,0:T(8,128)S(1)} %get-tuple-element.21.f_ref, ...), custom_call_target="tpu_custom_call" | custom-call | tf_op jit(solution)/shard_map/pallas_call | solution.py:154
  29.7 0.8 broadcast_in_dim.6
  30.5 4.4 %all-to-all-start = ((f32[8,4,4,4,128]{4,3,2,1,0:T(4,128)}), f32[8,4,4,4,128]{4,3,2,1,0:T(4,128)S(1)}, u32[]{:S(2)}, u32[]{:S(2)}) async-start(f32[8,4,4,4,128]{4,3,2,1,0:T(4,128)} %broadcast_in_dim.6), calls=%async_computation | async-start | bytes 524288 | tf_op jit(solution)/shard_map/all_to_all | solution.py:446
  34.9 0.0 collective-permute-start.8
  34.9 1.5 %collective-permute-start.17 = (f32[8,2,8,128]{3,2,1,0:T(8,128)}, f32[8,2,8,128]{3,2,1,0:T(8,128)S(1)}, u32[]{:S(2)}, u32[]{:S(2)}) collective-permute-start(f32[8,2,8,128]{3,2,1,0:T(8,128)} %get-tuple-element.38), channel_id=1, source_target_pairs={{0,1},{1,2},{2,3},{3,4},{4,5},{5,6},{6,7},{7,0},{8,9},{9,10},{10,1... | collective-permute-start | bytes 196616 | tf_op jit(solution)/shard_map/ppermute | solution.py:430
  36.4 2.2 %collective-permute-start.18 = (f32[8,2,8,128]{3,2,1,0:T(8,128)S(1)}, f32[8,2,8,128]{3,2,1,0:T(8,128)S(1)}, u32[]{:S(2)}, u32[]{:S(2)}) collective-permute-start(f32[8,2,8,128]{3,2,1,0:T(8,128)S(1)} %get-tuple-element.39), channel_id=1, source_target_pairs={{0,7},{1,0},{2,1},{3,2},{4,3},{5,4},{6,5},{7,6},{8,15},{9,8},{10,9... | collective-permute-start | bytes 196616 | tf_op jit(solution)/shard_map/ppermute | solution.py:430
  38.6 0.7 fusion.2
  39.2 0.0 collective-permute-done.9.outer
  39.2 3.0 %all-to-all-done.own = f32[8,4,4,4,128]{4,3,2,1,0:T(4,128)S(1)} async-done(((f32[8,4,4,4,128]{4,3,2,1,0:T(4,128)}), f32[8,4,4,4,128]{4,3,2,1,0:T(4,128)S(1)}, u32[]{:S(2)}, u32[]{:S(2)}) %all-to-all-start) | async-done | bytes 262176 | tf_op jit(solution)/shard_map/all_to_all | solution.py:446
  42.3 0.0 collective-permute-start.5
  42.3 10.0 %collective-permute-done.5.outer = f32[8,4,4,4,128]{4,3,2,1,0:T(4,128)S(1)} collective-permute-done((f32[8,4,4,4,128]{4,3,2,1,0:T(4,128)S(1)}, f32[8,4,4,4,128]{4,3,2,1,0:T(4,128)S(1)}, u32[]{:S(2)}, u32[]{:S(2)}) %collective-permute-start.5) | collective-permute-done | bytes 262176 | tf_op jit(solution)/shard_map/ppermute | solution.py:438
  52.4 0.0 collective-permute-start.4
  52.4 0.0 collective-permute-done.10.skip
  52.4 0.6 collective-permute-start.11
  53.0 0.0 collective-permute-done.18.fyhi_ref
  53.0 6.6 %collective-permute-start.6 = (f32[8,2,4,4,128]{4,3,2,1,0:T(4,128)S(1)}, f32[8,2,4,4,128]{4,3,2,1,0:T(4,128)S(1)}, u32[]{:S(2)}, u32[]{:S(2)}) collective-permute-start(f32[8,2,4,4,128]{4,3,2,1,0:T(4,128)S(1)} %slice_select_fusion.3), channel_id=1, source_target_pairs={{0,16},{8,248},{16,32},{24,8},{32,48},{40,24},{48,64},{56,40},{64,... | collective-permute-start | bytes 393224 | tf_op jit(solution)/shard_map/ppermute | solution.py:442
  59.6 0.0 collective-permute-done.8.pair
  59.6 0.0 collective-permute-start.7
  59.6 0.6 fusion.6
  60.2 0.0 collective-permute-done.11.far
  60.2 1.2 %shard_map.43 = (f32[16,4,32,128]{3,2,1,0:T(8,128)S(1)}, f32[8,2,16,128]{3,2,1,0:T(8,128)S(1)}, f32[8,128]{1,0:T(8,128)S(1)}) custom-call(s32[2]{0:T(128)S(1)} %pad_add_fusion.index_ref, f32[8,4,4,4,128]{4,3,2,1,0:T(4,128)S(1)} %all-to-all-done.1.own, f32[8,4,4,4,128]{4,3,2,1,0:T(4,128)S(1)} %collective-permute-done.8.pair, ...), custom_call_target="tpu_custom_call" | custom-call | tf_op jit(solution)/shard_map/pallas_call | solution.py:217
  61.4 0.1 collective-permute-done.6.skip
  61.5 3.9 %shard_map.44 = (f32[10,4,32,128]{3,2,1,0:T(8,128)S(1)}, f32[8,4,32,128]{3,2,1,0:T(8,128)S(1)}, f32[2,2,2,16,128]{4,3,2,1,0:T(8,128)}, f32[2,16,128]{2,1,0:T(8,128)}, f32[2,8,128]{2,1,0:T(8,128)S(1)}) custom-call(s32[2]{0:T(128)S(1)} %pad_add_fusion.index_ref, f32[8,4,4,4,128]{4,3,2,1,0:T(4,128)S(1)} %all-to-all-done.own, ...), custom_call_target="tpu_custom_call" | custom-call | tf_op jit(solution)/shard_map/pallas_call | solution.py:272
  65.4 0.7 broadcast_in_dim.8
  66.1 7.1 %all-to-all-start.2 = ((f32[16,2,8,128]{3,2,1,0:T(8,128)}), f32[16,2,8,128]{3,2,1,0:T(8,128)S(1)}, u32[]{:S(2)}, u32[]{:S(2)}) async-start(f32[16,2,8,128]{3,2,1,0:T(8,128)} %broadcast_in_dim.8), calls=%async_computation.2 | async-start | bytes 262144 | tf_op jit(solution)/shard_map/all_to_all | solution.py:480
  73.2 0.0 collective-permute-done.17.fylo_ref
  73.2 0.8 copy-done.9
  74.0 0.6 pad_maximum_fusion.2
  74.7 4.1 %collective-permute-start.19 = (f32[2,12,8,128]{3,2,1,0:T(8,128)}, f32[2,12,8,128]{3,2,1,0:T(8,128)}, u32[]{:S(2)}, u32[]{:S(2)}) collective-permute-start(f32[2,12,8,128]{3,2,1,0:T(8,128)} %pad_maximum_fusion.2), channel_id=1, source_target_pairs={{0,8},{8,16},{16,24},{24,32},{32,40},{40,48},{48,56},{56,64},{64,7... | collective-permute-start | bytes 294920 | tf_op jit(solution)/shard_map/ppermute | solution.py:430
  78.7 0.0 collective-permute-start.14
  78.8 0.6 pad_maximum_fusion.3
  79.4 2.3 %collective-permute-start.20 = (f32[2,12,8,128]{3,2,1,0:T(8,128)}, f32[2,12,8,128]{3,2,1,0:T(8,128)}, u32[]{:S(2)}, u32[]{:S(2)}) collective-permute-start(f32[2,12,8,128]{3,2,1,0:T(8,128)} %pad_maximum_fusion.3), channel_id=1, source_target_pairs={{0,248},{8,0},{16,8},{24,16},{32,24},{40,32},{48,40},{56,48},{64,5... | collective-permute-start | bytes 294920 | tf_op jit(solution)/shard_map/ppermute | solution.py:430
  81.7 0.0 collective-permute-start.13
  81.8 3.2 %collective-permute-start.15 = (f32[2,16,128]{2,1,0:T(8,128)}, f32[2,16,128]{2,1,0:T(8,128)S(1)}, u32[]{:S(2)}, u32[]{:S(2)}) collective-permute-start(f32[2,16,128]{2,1,0:T(8,128)} %get-tuple-element.32), channel_id=1, source_target_pairs={{0,16},{8,248},{16,32},{24,8},{32,48},{40,24},{48,64},{56,40},{64,... | collective-permute-start | bytes 49160 | tf_op jit(solution)/shard_map/ppermute | solution.py:442
  84.9 0.2 collective-permute-done.14.outer2
  85.1 0.2 collective-permute-start.12
  85.4 0.0 collective-permute-done.19.fxlo_ref
  85.4 0.4 collective-permute-start.16
  85.8 0.7 collective-permute-done.20.fxhi_ref
  86.5 0.0 collective-permute-done.15.skip2
  86.5 0.0 collective-permute-done.13.pair2
  86.5 0.1 collective-permute-done.16.far2
  86.6 0.0 collective-permute-done.12.other3
  86.6 0.6 copy-done.7
  87.2 0.9 copy-done.1
  88.2 8.0 %shard_map.45 = (f32[8,8,1024]{2,1,0:T(8,128)}, f32[8,8,1024]{2,1,0:T(8,128)}) custom-call(s32[2]{0:T(128)S(1)} %copy-done.7, f32[16,2,8,128]{3,2,1,0:T(8,128)S(1)} %all-to-all-done.2.mine3, f32[16,2,8,128]{3,2,1,0:T(8,128)S(1)} %collective-permute-done.12.other3, f32[2,2,2,16,128]{4,3,2,1,0:T(8,128)} %get-tuple-element.31.fs2, ...), custom_call_target="tpu_custom_call" | custom-call | tf_op jit(solution)/shard_map/pallas_call | solution.py:420
  (32 shorter events, 0.2 us)
Async XLA Ops:
  0.6 1.0 copy-start.2
  1.6 0.9 copy-start.3
  3.0 8.8 %collective-permute-start = (f32[2,8,2,8,128]{4,3,2,1,0:T(8,128)S(1)}, f32[2,8,2,8,128]{4,3,2,1,0:T(8,128)S(1)}, u32[]{:S(2)}, u32[]{:S(2)}) collective-permute-start(f32[2,8,2,8,128]{4,3,2,1,0:T(8,128)S(1)} %get-tuple-element.23), channel_id=1, source_target_pairs={{0,1},{1,2},{2,3},{3,4},{4,5},{5,6},{6,7},{7,0},{8,9},{9,10},{10,1... | collective-permute-start | bytes 393224 | tf_op jit(solution)/shard_map/ppermute | solution.py:430
  5.2 6.6 %collective-permute-start.1 = (f32[2,8,2,8,128]{4,3,2,1,0:T(8,128)S(1)}, f32[2,8,2,8,128]{4,3,2,1,0:T(8,128)S(1)}, u32[]{:S(2)}, u32[]{:S(2)}) collective-permute-start(f32[2,8,2,8,128]{4,3,2,1,0:T(8,128)S(1)} %get-tuple-element.24), channel_id=1, source_target_pairs={{0,7},{1,0},{2,1},{3,2},{4,3},{5,4},{6,5},{7,6},{8,15},{9,8},{10,9... | collective-permute-start | bytes 393224 | tf_op jit(solution)/shard_map/ppermute | solution.py:430
  8.3 9.1 %all-to-all-start.1 = ((f32[8,4,4,4,128]{4,3,2,1,0:T(4,128)}), f32[8,4,4,4,128]{4,3,2,1,0:T(4,128)S(1)}, u32[]{:S(2)}, u32[]{:S(2)}) async-start(f32[8,4,4,4,128]{4,3,2,1,0:T(4,128)} %broadcast_in_dim.7), calls=%async_computation.1 | async-start | bytes 524288 | tf_op jit(solution)/shard_map/all_to_all | solution.py:446
  11.8 49.7 %copy-start.6 = (s32[2]{0:T(128)}, s32[2]{0:T(128)S(1)}, u32[]{:S(2)}) copy-start(s32[2]{0:T(128)S(1)} %pad_add_fusion.index_ref) | copy-start | bytes 28
  11.9 15.3 %collective-permute-start.2 = (f32[2,2,12,8,128]{4,3,2,1,0:T(8,128)S(1)}, f32[2,2,12,8,128]{4,3,2,1,0:T(8,128)S(1)}, u32[]{:S(2)}, u32[]{:S(2)}) collective-permute-start(f32[2,2,12,8,128]{4,3,2,1,0:T(8,128)S(1)} %pad_maximum_fusion), channel_id=1, source_target_pairs={{0,8},{8,16},{16,24},{24,32},{32,40},{40,48},{48,56},{56,64},{64,7... | collective-permute-start | bytes 589832 | tf_op jit(solution)/shard_map/ppermute | solution.py:430
  16.6 10.6 %collective-permute-start.3 = (f32[2,2,12,8,128]{4,3,2,1,0:T(8,128)S(1)}, f32[2,2,12,8,128]{4,3,2,1,0:T(8,128)S(1)}, u32[]{:S(2)}, u32[]{:S(2)}) collective-permute-start(f32[2,2,12,8,128]{4,3,2,1,0:T(8,128)S(1)} %pad_maximum_fusion.1), channel_id=1, source_target_pairs={{0,248},{8,0},{16,8},{24,16},{32,24},{40,32},{48,40},{56,48},{64,5... | collective-permute-start | bytes 589832 | tf_op jit(solution)/shard_map/ppermute | solution.py:430
  17.4 21.8 %collective-permute-start.9 = (f32[8,4,4,4,128]{4,3,2,1,0:T(4,128)S(1)}, f32[8,4,4,4,128]{4,3,2,1,0:T(4,128)S(1)}, u32[]{:S(2)}, u32[]{:S(2)}) collective-permute-start(f32[8,4,4,4,128]{4,3,2,1,0:T(4,128)S(1)} %all-to-all-done.1.own), channel_id=1, source_target_pairs={{0,248},{8,16},{16,8},{24,32},{32,24},{40,48},{48,40},{56,64},{64,... | collective-permute-start | bytes 786440 | tf_op jit(solution)/shard_map/ppermute | solution.py:438
  23.3 29.1 %collective-permute-start.10 = (f32[8,2,4,4,128]{4,3,2,1,0:T(4,128)}, f32[8,2,4,4,128]{4,3,2,1,0:T(4,128)S(1)}, u32[]{:S(2)}, u32[]{:S(2)}) collective-permute-start(f32[8,2,4,4,128]{4,3,2,1,0:T(4,128)} %slice_select_fusion.1), channel_id=1, source_target_pairs={{0,16},{8,248},{16,32},{24,8},{32,48},{40,24},{48,64},{56,40},{64,... | collective-permute-start | bytes 393224 | tf_op jit(solution)/shard_map/ppermute | solution.py:442
  29.7 0.8 copy-start
  30.5 11.8 %all-to-all-start = ((f32[8,4,4,4,128]{4,3,2,1,0:T(4,128)}), f32[8,4,4,4,128]{4,3,2,1,0:T(4,128)S(1)}, u32[]{:S(2)}, u32[]{:S(2)}) async-start(f32[8,4,4,4,128]{4,3,2,1,0:T(4,128)} %broadcast_in_dim.6), calls=%async_computation | async-start | bytes 524288 | tf_op jit(solution)/shard_map/all_to_all | solution.py:446
  34.9 24.7 %collective-permute-start.8 = (f32[8,4,4,4,128]{4,3,2,1,0:T(4,128)S(1)}, f32[8,4,4,4,128]{4,3,2,1,0:T(4,128)S(1)}, u32[]{:S(2)}, u32[]{:S(2)}) collective-permute-start(f32[8,4,4,4,128]{4,3,2,1,0:T(4,128)S(1)} %all-to-all-done.1.own), channel_id=1, source_target_pairs={{0,8},{8,0},{16,24},{24,16},{32,40},{40,32},{48,56},{56,48},{64,72... | collective-permute-start | bytes 786440 | tf_op jit(solution)/shard_map/ppermute | solution.py:434
  34.9 38.3 %collective-permute-start.17 = (f32[8,2,8,128]{3,2,1,0:T(8,128)}, f32[8,2,8,128]{3,2,1,0:T(8,128)S(1)}, u32[]{:S(2)}, u32[]{:S(2)}) collective-permute-start(f32[8,2,8,128]{3,2,1,0:T(8,128)} %get-tuple-element.38), channel_id=1, source_target_pairs={{0,1},{1,2},{2,3},{3,4},{4,5},{5,6},{6,7},{7,0},{8,9},{9,10},{10,1... | collective-permute-start | bytes 196616 | tf_op jit(solution)/shard_map/ppermute | solution.py:430
  36.4 16.7 %collective-permute-start.18 = (f32[8,2,8,128]{3,2,1,0:T(8,128)S(1)}, f32[8,2,8,128]{3,2,1,0:T(8,128)S(1)}, u32[]{:S(2)}, u32[]{:S(2)}) collective-permute-start(f32[8,2,8,128]{3,2,1,0:T(8,128)S(1)} %get-tuple-element.39), channel_id=1, source_target_pairs={{0,7},{1,0},{2,1},{3,2},{4,3},{5,4},{6,5},{7,6},{8,15},{9,8},{10,9... | collective-permute-start | bytes 196616 | tf_op jit(solution)/shard_map/ppermute | solution.py:430
  42.3 10.1 %collective-permute-start.5 = (f32[8,4,4,4,128]{4,3,2,1,0:T(4,128)S(1)}, f32[8,4,4,4,128]{4,3,2,1,0:T(4,128)S(1)}, u32[]{:S(2)}, u32[]{:S(2)}) collective-permute-start(f32[8,4,4,4,128]{4,3,2,1,0:T(4,128)S(1)} %all-to-all-done.own), channel_id=1, source_target_pairs={{0,248},{8,16},{16,8},{24,32},{32,24},{40,48},{48,40},{56,64},{64,... | collective-permute-start | bytes 786440 | tf_op jit(solution)/shard_map/ppermute | solution.py:438
  52.4 9.2 %collective-permute-start.4 = (f32[8,4,4,4,128]{4,3,2,1,0:T(4,128)S(1)}, f32[8,4,4,4,128]{4,3,2,1,0:T(4,128)S(1)}, u32[]{:S(2)}, u32[]{:S(2)}) collective-permute-start(f32[8,4,4,4,128]{4,3,2,1,0:T(4,128)S(1)} %all-to-all-done.own), channel_id=1, source_target_pairs={{0,8},{8,0},{16,24},{24,16},{32,40},{40,32},{48,56},{56,48},{64,72... | collective-permute-start | bytes 786440 | tf_op jit(solution)/shard_map/ppermute | solution.py:434
  52.4 7.8 %collective-permute-start.11 = (f32[8,2,4,4,128]{4,3,2,1,0:T(4,128)S(1)}, f32[8,2,4,4,128]{4,3,2,1,0:T(4,128)S(1)}, u32[]{:S(2)}, u32[]{:S(2)}) collective-permute-start(f32[8,2,4,4,128]{4,3,2,1,0:T(4,128)S(1)} %slice_select_fusion), channel_id=1, source_target_pairs={{0,8},{8,0},{16,24},{24,16},{32,40},{40,32},{48,56},{56,48},{64,72... | collective-permute-start | bytes 393224 | tf_op jit(solution)/shard_map/ppermute | solution.py:434
  53.0 8.4 %copy-start.4 = (f32[8,2,8,128]{3,2,1,0:T(8,128)}, f32[8,2,8,128]{3,2,1,0:T(8,128)S(1)}, u32[]{:S(2)}) copy-start(f32[8,2,8,128]{3,2,1,0:T(8,128)S(1)} %collective-permute-done.18.fyhi_ref) | copy-start | bytes 196612
  53.0 8.5 %collective-permute-start.6 = (f32[8,2,4,4,128]{4,3,2,1,0:T(4,128)S(1)}, f32[8,2,4,4,128]{4,3,2,1,0:T(4,128)S(1)}, u32[]{:S(2)}, u32[]{:S(2)}) collective-permute-start(f32[8,2,4,4,128]{4,3,2,1,0:T(4,128)S(1)} %slice_select_fusion.3), channel_id=1, source_target_pairs={{0,16},{8,248},{16,32},{24,8},{32,48},{40,24},{48,64},{56,40},{64,... | collective-permute-start | bytes 393224 | tf_op jit(solution)/shard_map/ppermute | solution.py:442
  59.6 2.0 %collective-permute-start.7 = (f32[8,2,4,4,128]{4,3,2,1,0:T(4,128)S(1)}, f32[8,2,4,4,128]{4,3,2,1,0:T(4,128)S(1)}, u32[]{:S(2)}, u32[]{:S(2)}) collective-permute-start(f32[8,2,4,4,128]{4,3,2,1,0:T(4,128)S(1)} %slice_select_fusion.2), channel_id=1, source_target_pairs={{0,8},{8,0},{16,24},{24,16},{32,40},{40,32},{48,56},{56,48},{64,72... | collective-permute-start | bytes 393224 | tf_op jit(solution)/shard_map/ppermute | solution.py:434
  66.1 7.1 %copy-start.11 = (f32[2,2,8,128]{3,2,1,0:T(8,128)S(1)}, f32[2,2,8,128]{3,2,1,0:T(8,128)}, u32[]{:S(2)}) copy-start(f32[2,2,8,128]{3,2,1,0:T(8,128)} %get-tuple-element.51) | copy-start | bytes 49156
  66.1 19.1 %all-to-all-start.2 = ((f32[16,2,8,128]{3,2,1,0:T(8,128)}), f32[16,2,8,128]{3,2,1,0:T(8,128)S(1)}, u32[]{:S(2)}, u32[]{:S(2)}) async-start(f32[16,2,8,128]{3,2,1,0:T(8,128)} %broadcast_in_dim.8), calls=%async_computation.2 | async-start | bytes 262144 | tf_op jit(solution)/shard_map/all_to_all | solution.py:480
  73.2 0.8 copy-start.9
  74.0 4.7 %copy-start.8 = (f32[2,8,8,128]{3,2,1,0:T(8,128)S(1)}, f32[2,8,8,128]{3,2,1,0:T(8,128)}, u32[]{:S(2)}) copy-start(f32[2,8,8,128]{3,2,1,0:T(8,128)} %get-tuple-element.42) | copy-start | bytes 196612
  74.0 4.7 %copy-start.10 = (f32[2,2,8,128]{3,2,1,0:T(8,128)S(1)}, f32[2,2,8,128]{3,2,1,0:T(8,128)}, u32[]{:S(2)}) copy-start(f32[2,2,8,128]{3,2,1,0:T(8,128)} %get-tuple-element.50) | copy-start | bytes 49156
  74.7 10.7 %collective-permute-start.19 = (f32[2,12,8,128]{3,2,1,0:T(8,128)}, f32[2,12,8,128]{3,2,1,0:T(8,128)}, u32[]{:S(2)}, u32[]{:S(2)}) collective-permute-start(f32[2,12,8,128]{3,2,1,0:T(8,128)} %pad_maximum_fusion.2), channel_id=1, source_target_pairs={{0,8},{8,16},{16,24},{24,32},{32,40},{40,48},{48,56},{56,64},{64,7... | collective-permute-start | bytes 294920 | tf_op jit(solution)/shard_map/ppermute | solution.py:430
  78.7 6.4 %collective-permute-start.14 = (f32[2,2,2,16,128]{4,3,2,1,0:T(8,128)}, f32[2,2,2,16,128]{4,3,2,1,0:T(8,128)S(1)}, u32[]{:S(2)}, u32[]{:S(2)}) collective-permute-start(f32[2,2,2,16,128]{4,3,2,1,0:T(8,128)} %get-tuple-element.31.fs2), channel_id=1, source_target_pairs={{0,248},{8,16},{16,8},{24,32},{32,24},{40,48},{48,40},{56,64},{64,... | collective-permute-start | bytes 196616 | tf_op jit(solution)/shard_map/ppermute | solution.py:438
  78.8 7.9 %copy-start.5 = (f32[8,2,8,128]{3,2,1,0:T(8,128)S(1)}, f32[8,2,8,128]{3,2,1,0:T(8,128)}, u32[]{:S(2)}) copy-start(f32[8,2,8,128]{3,2,1,0:T(8,128)} %copy-done.4) | copy-start | bytes 196612
  79.4 7.0 %collective-permute-start.20 = (f32[2,12,8,128]{3,2,1,0:T(8,128)}, f32[2,12,8,128]{3,2,1,0:T(8,128)}, u32[]{:S(2)}, u32[]{:S(2)}) collective-permute-start(f32[2,12,8,128]{3,2,1,0:T(8,128)} %pad_maximum_fusion.3), channel_id=1, source_target_pairs={{0,248},{8,0},{16,8},{24,16},{32,24},{40,32},{48,40},{56,48},{64,5... | collective-permute-start | bytes 294920 | tf_op jit(solution)/shard_map/ppermute | solution.py:430
  81.7 4.8 %collective-permute-start.13 = (f32[2,2,2,16,128]{4,3,2,1,0:T(8,128)}, f32[2,2,2,16,128]{4,3,2,1,0:T(8,128)}, u32[]{:S(2)}, u32[]{:S(2)}) collective-permute-start(f32[2,2,2,16,128]{4,3,2,1,0:T(8,128)} %get-tuple-element.31.fs2), channel_id=1, source_target_pairs={{0,8},{8,0},{16,24},{24,16},{32,40},{40,32},{48,56},{56,48},{64,72... | collective-permute-start | bytes 196616 | tf_op jit(solution)/shard_map/ppermute | solution.py:434
  81.8 4.7 %collective-permute-start.15 = (f32[2,16,128]{2,1,0:T(8,128)}, f32[2,16,128]{2,1,0:T(8,128)S(1)}, u32[]{:S(2)}, u32[]{:S(2)}) collective-permute-start(f32[2,16,128]{2,1,0:T(8,128)} %get-tuple-element.32), channel_id=1, source_target_pairs={{0,16},{8,248},{16,32},{24,8},{32,48},{40,24},{48,64},{56,40},{64,... | collective-permute-start | bytes 49160 | tf_op jit(solution)/shard_map/ppermute | solution.py:442
  85.1 1.5 %collective-permute-start.12 = (f32[16,2,8,128]{3,2,1,0:T(8,128)S(1)}, f32[16,2,8,128]{3,2,1,0:T(8,128)S(1)}, u32[]{:S(2)}, u32[]{:S(2)}) collective-permute-start(f32[16,2,8,128]{3,2,1,0:T(8,128)S(1)} %all-to-all-done.2.mine3), channel_id=1, source_target_pairs={{0,8},{8,0},{16,24},{24,16},{32,40},{40,32},{48,56},{56,48},{64,72... | collective-permute-start | bytes 393224 | tf_op jit(solution)/shard_map/ppermute | solution.py:434
  85.4 1.3 %collective-permute-start.16 = (f32[2,16,128]{2,1,0:T(8,128)S(1)}, f32[2,16,128]{2,1,0:T(8,128)S(1)}, u32[]{:S(2)}, u32[]{:S(2)}) collective-permute-start(f32[2,16,128]{2,1,0:T(8,128)S(1)} %fusion), channel_id=1, source_target_pairs={{0,8},{8,0},{16,24},{24,16},{32,40},{40,32},{48,56},{56,48},{64,72... | collective-permute-start | bytes 49160 | tf_op jit(solution)/shard_map/ppermute | solution.py:434
  86.6 0.6 copy-start.7
  87.2 0.9 copy-start.1

commit v2 on v1

--- a/solution.py
+++ b/solution.py
@@ -69,9 +69,17 @@
             pairs_ref[x, pl.ds(8 * y, 8), :] = row[2 * y] + row[2 * y + 1]
 
 
-def prepare_kernel(cot_ref, diag_ref, f_ref, sg_ref, ylo_ref, yhi_ref, c1_ref, turned, placed, pairs):
-    stacked = jnp.concatenate([cot_ref[...].reshape(64, 1024), diag_ref[...].reshape(64, 1024)], axis=0)
-    turned[...] = stacked.T
+def prepare_kernel(cot_ref, diag_ref, f_ref, sg_ref, ylo_ref, yhi_ref, c1_ref, stacked, turned, placed, pairs, sems):
+    fetches = [
+        pltpu.make_async_copy(ref.at[pl.ds(4 * h, 4)], stacked.at[k, pl.ds(4 * h, 4)], sems.at[k, h])
+        for k, ref in enumerate((cot_ref, diag_ref))
+        for h in range(2)
+    ]
+    for fetch in fetches:
+        fetch.start()
+    for fetch in fetches:
+        fetch.wait()
+    turned[...] = stacked[...].reshape(128, 1024).T
     for c in range(8):
         placed[pl.ds(c, 128, stride=8), :] = turned[pl.ds(c, 128, stride=8), :].T
     f = placed[0:512, :].reshape(8, 8, 8, 128)
@@ -99,12 +107,15 @@
             shape(2, 8, 2, 8, 128),
             shape(4, 4, 4, 128),
         ),
+        in_specs=[pl.BlockSpec(memory_space=pl.ANY)] * 2,
         scratch_shapes=[
+            pltpu.VMEM((2, 8, 8, 1024), F32),
             pltpu.VMEM((1024, 128), F32),
             pltpu.VMEM((1024, 128), F32),
             pltpu.VMEM((4, 32, 128), F32),
+            pltpu.SemaphoreType.DMA((2, 2)),
         ],
-        compiler_params=params(),
+        compiler_params=pltpu.CompilerParams(vmem_limit_bytes=62 * 1024 * 1024),
     )(cot, diag)
 
 
@@ -135,7 +146,7 @@
         s1[x, 1:11] = THIRD * s0[x, 1:11] + gext_ref[x, 1:11] * total
         return carry
 
-    lax.fori_loop(1, 11, first, 0)
+    lax.fori_loop(1, 11, first, 0, unroll=2)
 
     def second(x, carry):
         f1 = THIRD * f_ref[x - 2] + fine_neighbours(s0, x, 2, 10)
@@ -143,7 +154,7 @@
         src_ref[x - 2] = s0[x, 2:10] + s1[x, 2:10]
         return carry
 
-    lax.fori_loop(2, 10, second, 0)
+    lax.fori_loop(2, 10, second, 0, unroll=2)
     fylo_ref[...] = f2_ref[:, 0:2]
     fyhi_ref[...] = f2_ref[:, 6:8]
     block_pairs(f2_ref, pairs)
@@ -206,7 +217,7 @@
         g1_ref[x] = OMEGA / (6.0 + 4.0 * field[x])
         return carry
 
-    lax.fori_loop(0, 16, scale1, 0)
+    lax.fori_loop(0, 16, scale1, 0, unroll=2)
     for x in range(8):
         c2[x] = restrict_middle(field, 2 * x, pairs, 0.125)
         g2_ref[x] = OMEGA / (6.0 + 16.0 * c2[x])
@@ -234,7 +245,7 @@
         s0[x] = g1_ref[x] * rhs[x]
         return carry
 
-    lax.fori_loop(0, 16, start, 0)
+    lax.fori_loop(0, 16, start, 0, unroll=2)
 
     def first(x, carry):
         total = coarse_neighbours(s0, x)
@@ -242,13 +253,13 @@
         rhs[x] = THIRD * rhs[x] + total
         return carry
 
-    lax.fori_loop(1, 15, first, 0)
+    lax.fori_loop(1, 15, first, 0, unroll=2)
 
     def second(x, carry):
         f2[x - 2] = THIRD * rhs[x] + coarse_neighbours(s1, x)
         return carry
 
-    lax.fori_loop(2, 14, second, 0)
+    lax.fori_loop(2, 14, second, 0, unroll=2)
     f1_ref[...] = f2[1:11]
     src1_ref[...] = s0[4:12] + s1[4:12]
 
@@ -292,7 +303,7 @@
     g0_ref, f0_ref, src0_ref, fylo_ref, fyhi_ref, fxlo_ref, fxhi_ref,
     guess_ref, source_ref,
     e3, out3, f2, src2, r2, sa2, out2, r1, sa1, out1,
-    rep, r0, f0, s3, s4, turned, placed,
+    r0, f0, s3, s4, turned, placed,
 ):
     core = core_of(index_ref)
     chip = lax.div(index_ref[0], 2)
@@ -349,7 +360,7 @@
         sa1[x] = g * (f1_ref[x - 1] - (OMEGA / g) * r1[x] + coarse_neighbours(r1, x))
         return carry
 
-    lax.fori_loop(1, 11, middle1, 0)
+    lax.fori_loop(1, 11, middle1, 0, unroll=2)
 
     def last1(x, carry):
         sb = THIRD * sa1[x] + g1_ref[x + 2] * coarse_neighbours(sa1, x)
@@ -358,20 +369,18 @@
             out1[x - 2, pl.ds(32 * c, 32), :] = row[c]
         return carry
 
-    lax.fori_loop(2, 10, last1, 0)
+    lax.fori_loop(2, 10, last1, 0, unroll=2)
 
     def spread0(x, carry):
         for y in range(8):
             row = out1[x, pl.ds(14 + y, 4, stride=32), :]
-            rep[pl.ds(0, 4, stride=2), :] = row
-            rep[pl.ds(1, 4, stride=2), :] = row
-            both = rep[...]
             for p in range(2):
                 for q in range(2):
-                    r0[2 * x + p, 2 * y + q] = both
-        return carry
-
-    lax.fori_loop(0, 8, spread0, 0)
+                    for c in range(2):
+                        r0[2 * x + p, 2 * y + q, pl.ds(c, 4, stride=2), :] = row
+        return carry
+
+    lax.fori_loop(0, 8, spread0, 0, unroll=2)
     f0[2:10, 2:10] = f0_ref[...]
     f0[2:10, 0:2] = fylo_ref[...]
     f0[2:10, 10:12] = fyhi_ref[...]
@@ -385,13 +394,13 @@
         s3[x] = g * f
         return carry
 
-    lax.fori_loop(0, 12, residual0, 0)
+    lax.fori_loop(0, 12, residual0, 0, unroll=2)
 
     def first0(x, carry):
         s4[x, 1:11] = THIRD * s3[x, 1:11] + g0_ref[x, 1:11] * fine_neighbours(s3, x, 1, 11)
         return carry
 
-    lax.fori_loop(1, 11, first0, 0)
+    lax.fori_loop(1, 11, first0, 0, unroll=2)
 
     def second0(x, carry):
         f4 = THIRD * f0[x, 2:10] + fine_neighbours(s3, x, 2, 10)
@@ -401,7 +410,7 @@
         placed[pl.ds(64 * (x - 2) + 512, 64), :] = source.reshape(64, 128)
         return carry
 
-    lax.fori_loop(2, 10, second0, 0)
+    lax.fori_loop(2, 10, second0, 0, unroll=2)
     for c in range(8):
         turned[pl.ds(c, 128, stride=8), :] = placed[pl.ds(c, 128, stride=8), :].T
     result = turned[...].T
@@ -414,7 +423,7 @@
         (32, 2, 8, 128), (32, 8, 128), (6, 2, 16, 128), (6, 2, 16, 128),
         (10, 2, 16, 128), (10, 2, 16, 128), (6, 2, 16, 128),
         (12, 4, 32, 128), (12, 4, 32, 128), (8, 128, 128),
-        (8, 128), (16, 16, 8, 128), (12, 12, 8, 128), (12, 12, 8, 128), (12, 12, 8, 128),
+        (16, 16, 8, 128), (12, 12, 8, 128), (12, 12, 8, 128), (12, 12, 8, 128),
         (1024, 128), (1024, 128),
     ]
     return pl.pallas_call(
@@ -446,10 +455,15 @@
     return lax.all_to_all(jnp.broadcast_to(v[None], (GY,) + v.shape), "gy", 0, 0)
 
 
+def together(*arrays):
+    return lax.optimization_barrier(arrays)
+
+
 def level1_rows(core, v):
     pair = swap_core(v)
     outer = swap_outer(v)
     skip = skip_chip(jnp.where(core == 0, v[:, 2:4], v[:, 0:2]))
+    pair, outer, skip = together(pair, outer, skip)
     far = swap_core(jnp.where(core == 0, outer[:, 2:4], outer[:, 0:2]))
     return v, pair, outer, skip, far
 

time: 97.1 us -> 92.6 us (0.954)
  waiting for transfers between devices: 15 us -> 9.44 us
  starting transfers between devices: 54.3 us -> 57.1 us
  Pallas kernels: 16.1 us -> 14.2 us
    ppermute x7, starting transfers between devices: 1.23 us -> 11.4 us  [swap_core(): return lax.ppermute(v, 'gx', [(i, i ^ 1) for i in range(GX)])]
    ppermute x3, waiting for transfers between devices: 10.3 us -> 0.72 us  [swap_outer(): lax.ppermute(v, 'gx', [(i, (i + 1 if i % 2 else i - 1) % GX) for i in ran...]
    ppermute x3, starting transfers between devices: 5.21 us -> 1.1 us  [swap_outer(): lax.ppermute(v, 'gx', [(i, (i + 1 if i % 2 else i - 1) % GX) for i in ran...]
    ppermute x3, waiting for transfers between devices: 0.11 us -> 4.16 us  [skip_chip(): lax.ppermute(v, 'gx', [(i, (i - 2 if i % 2 else i + 2) % GX) for i in ran...]
    pallas_call x1, Pallas kernels: 0.48 us -> 2.51 us  [prepare(): pl.pallas_call(prepare_kernel, out_shape=(shape(8, 8, 8, 128), shape(2, 8...]
    pallas_call x1, Pallas kernels: 8.01 us -> 6.03 us  [up(): pl.pallas_call(up_kernel, out_shape=(shape(8, 8, 1024), shape(8, 8, 1024)...]
    all_to_all x1, starting transfers between devices: 7.1 us -> 5.13 us  [per_device(): lax.all_to_all(jnp.broadcast_to(both3[None], (16,) + both3.shape), 'gx',...]
    unnamed x24 -> x30, local copies, waits for them, and re-layouts: 4.24 us -> 2.97 us
  transfers between devices with their start and end apart: 24 -> 24, of which waited for: 7 -> 7; matrix products, arithmetic and copies ran while one was open for 6% -> 7% of each run, Pallas kernels for 8% -> 6%
where the time goes in v2:
time: 92.6 us; the launch traced here: 91.1 us
  starting transfers between devices  57.1 us (62%)
  Pallas kernels  14.2 us (15%)
  waiting for transfers between devices  9.44 us (10%)
  local copies, waits for them, and re-layouts  7.26 us (8%)
  other arithmetic  2.21 us (2%)
    ppermute x8, starting transfers between devices, shifted(): lax.ppermute(v, axis, [(i, (i + step) % count) for i in range(count)])  18.1 us
    ppermute x3, starting transfers between devices, skip_chip(): lax.ppermute(v, 'gx', [(i, (i - 2 if i % 2 else i + 2) % GX) for i in ran...  14.4 us
    ppermute x7, starting transfers between devices, swap_core(): return lax.ppermute(v, 'gx', [(i, i ^ 1) for i in range(GX)])  11.4 us
    all_to_all x2, starting transfers between devices, gather_y(): lax.all_to_all(jnp.broadcast_to(v[None], (GY,) + v.shape), 'gy', 0, 0)  6.96 us
    pallas_call x1, Pallas kernels, up(): pl.pallas_call(up_kernel, out_shape=(shape(8, 8, 1024), shape(8, 8, 1024)...  6.03 us
    all_to_all x1, starting transfers between devices, per_device(): lax.all_to_all(jnp.broadcast_to(both3[None], (16,) + both3.shape), 'gx',...  5.13 us
    ppermute x3, waiting for transfers between devices, skip_chip(): lax.ppermute(v, 'gx', [(i, (i - 2 if i % 2 else i + 2) % GX) for i in ran...  4.16 us
    all_to_all x2, waiting for transfers between devices, gather_y(): lax.all_to_all(jnp.broadcast_to(v[None], (GY,) + v.shape), 'gy', 0, 0)  3.27 us
  transfers between devices with their start and end apart: 24, of which 7 were waited for; matrix products, arithmetic and copies ran while one was open for 7% of the time, Pallas kernels for 6%

profile of v2, /device:TPU:1, one launch (start us, length us, event | category | flops | bytes accessed | tf_op | source)
XLA Modules:
  0.0 91.1 jit_solution(12127926002510780610)
XLA Ops:
  0.6 2.5 %shard_map.41 = (f32[8,8,8,128]{3,2,1,0:T(8,128)}, f32[2,8,8,8,128]{4,3,2,1,0:T(8,128)}, f32[2,8,2,8,128]{4,3,2,1,0:T(8,128)}, f32[2,8,2,8,128]{4,3,2,1,0:T(8,128)}, f32[4,4,4,128]{3,2,1,0:T(4,128)}) custom-call(f32[8,8,1024]{2,1,0:T(8,128)} %cot_ref.1, f32[8,8,1024]{2,1,0:T(8,128)} %diag_ref.1), custom_call_target="tpu_custom_call" | custom-call | tf_op jit(solution)/shard_map/pallas_call | solution.py:101
  3.2 2.2 %collective-permute-start = (f32[2,8,2,8,128]{4,3,2,1,0:T(8,128)}, f32[2,8,2,8,128]{4,3,2,1,0:T(8,128)S(1)}, u32[]{:S(2)}, u32[]{:S(2)}) collective-permute-start(f32[2,8,2,8,128]{4,3,2,1,0:T(8,128)} %get-tuple-element.29), channel_id=1, source_target_pairs={{0,1},{1,2},{2,3},{3,4},{4,5},{5,6},{6,7},{7,0},{8,9},{9,10},{10,1... | collective-permute-start | bytes 393224 | tf_op jit(solution)/shard_map/ppermute | solution.py:439
  5.4 2.3 %collective-permute-start.1 = (f32[2,8,2,8,128]{4,3,2,1,0:T(8,128)}, f32[2,8,2,8,128]{4,3,2,1,0:T(8,128)S(1)}, u32[]{:S(2)}, u32[]{:S(2)}) collective-permute-start(f32[2,8,2,8,128]{4,3,2,1,0:T(8,128)} %get-tuple-element.30), channel_id=1, source_target_pairs={{0,7},{1,0},{2,1},{3,2},{4,3},{5,4},{6,5},{7,6},{8,15},{9,8},{10,9... | collective-permute-start | bytes 393224 | tf_op jit(solution)/shard_map/ppermute | solution.py:439
  7.6 1.5 %broadcast_in_dim.7 = f32[8,4,4,4,128]{4,3,2,1,0:T(4,128)} broadcast(f32[4,4,4,128]{3,2,1,0:T(4,128)} %get-tuple-element.35), dimensions={1,2,3,4} | broadcast | bytes 294912 | tf_op jit(solution)/shard_map/broadcast_in_dim | solution.py:455
  9.1 3.4 %all-to-all-start.1 = ((f32[8,4,4,4,128]{4,3,2,1,0:T(4,128)}), f32[8,4,4,4,128]{4,3,2,1,0:T(4,128)S(1)}, u32[]{:S(2)}, u32[]{:S(2)}) async-start(f32[8,4,4,4,128]{4,3,2,1,0:T(4,128)} %broadcast_in_dim.7), calls=%async_computation.1 | async-start | bytes 524288 | tf_op jit(solution)/shard_map/all_to_all | solution.py:455
  12.6 0.1 pad_add_fusion.index_ref
  12.7 0.0 collective-permute-done.1.yhi_ref
  12.7 0.0 collective-permute-done.ylo_ref
  12.8 4.2 %collective-permute-start.2 = (f32[2,2,12,8,128]{4,3,2,1,0:T(8,128)S(1)}, f32[2,2,12,8,128]{4,3,2,1,0:T(8,128)S(1)}, u32[]{:S(2)}, u32[]{:S(2)}) collective-permute-start(f32[2,2,12,8,128]{4,3,2,1,0:T(8,128)S(1)} %pad_maximum_fusion), channel_id=1, source_target_pairs={{0,8},{8,16},{16,24},{24,32},{32,40},{40,48},{48,56},{56,64},{64,7... | collective-permute-start | bytes 589832 | tf_op jit(solution)/shard_map/ppermute | solution.py:439
  16.9 0.0 copy-start.3
  17.0 0.1 collective-permute-start.3
  17.0 1.2 %all-to-all-done.1.own = f32[8,4,4,4,128]{4,3,2,1,0:T(4,128)S(1)} async-done(((f32[8,4,4,4,128]{4,3,2,1,0:T(4,128)}), f32[8,4,4,4,128]{4,3,2,1,0:T(4,128)S(1)}, u32[]{:S(2)}, u32[]{:S(2)}) %all-to-all-start.1) | async-done | bytes 262176 | tf_op jit(solution)/shard_map/all_to_all | solution.py:455
  18.3 4.1 %collective-permute-start.8 = (f32[8,4,4,4,128]{4,3,2,1,0:T(4,128)S(1)}, f32[8,4,4,4,128]{4,3,2,1,0:T(4,128)S(1)}, u32[]{:S(2)}, u32[]{:S(2)}) collective-permute-start(f32[8,4,4,4,128]{4,3,2,1,0:T(4,128)S(1)} %all-to-all-done.1.own), channel_id=1, source_target_pairs={{0,8},{8,0},{16,24},{24,16},{32,40},{40,32},{48,56},{56,48},{64,72... | collective-permute-start | bytes 786440 | tf_op jit(solution)/shard_map/ppermute | solution.py:443
  22.4 1.1 %collective-permute-start.9 = (f32[8,4,4,4,128]{4,3,2,1,0:T(4,128)S(1)}, f32[8,4,4,4,128]{4,3,2,1,0:T(4,128)S(1)}, u32[]{:S(2)}, u32[]{:S(2)}) collective-permute-start(f32[8,4,4,4,128]{4,3,2,1,0:T(4,128)S(1)} %all-to-all-done.1.own), channel_id=1, source_target_pairs={{0,248},{8,16},{16,8},{24,32},{32,24},{40,48},{48,40},{56,64},{64,... | collective-permute-start | bytes 786440 | tf_op jit(solution)/shard_map/ppermute | solution.py:447
  23.5 0.7 slice_select_fusion
  24.2 6.3 %collective-permute-start.10 = (f32[8,2,4,4,128]{4,3,2,1,0:T(4,128)}, f32[8,2,4,4,128]{4,3,2,1,0:T(4,128)}, u32[]{:S(2)}, u32[]{:S(2)}) collective-permute-start(f32[8,2,4,4,128]{4,3,2,1,0:T(4,128)} %slice_select_fusion), channel_id=1, source_target_pairs={{0,16},{8,248},{16,32},{24,8},{32,48},{40,24},{48,64},{56,40},{64,... | collective-permute-start | bytes 393224 | tf_op jit(solution)/shard_map/ppermute | solution.py:451
  30.4 0.0 collective-permute-done.2.xlo_ref
  30.4 0.0 collective-permute-done.3.xhi_ref
  30.4 1.2 %shard_map.42 = (f32[8,8,8,128]{3,2,1,0:T(8,128)S(1)}, f32[8,8,8,128]{3,2,1,0:T(8,128)S(1)}, f32[12,12,8,128]{3,2,1,0:T(8,128)S(1)}, f32[8,2,8,128]{3,2,1,0:T(8,...) custom-call(f32[8,8,8,128]{3,2,1,0:T(8,128)S(1)} %copy-done.3, f32[2,8,8,8,128]{4,3,2,1,0:T(8,128)S(1)} %copy-done, ...), custom_call_target="tpu_custom_call" | custom-call | tf_op jit(solution)/shard_map/pallas_call | solution.py:165
  31.7 0.6 copy-done.9
  32.3 0.8 broadcast_in_dim.6
  33.1 3.5 %all-to-all-start = ((f32[8,4,4,4,128]{4,3,2,1,0:T(4,128)}), f32[8,4,4,4,128]{4,3,2,1,0:T(4,128)S(1)}, u32[]{:S(2)}, u32[]{:S(2)}) async-start(f32[8,4,4,4,128]{4,3,2,1,0:T(4,128)} %broadcast_in_dim.6), calls=%async_computation | async-start | bytes 524288 | tf_op jit(solution)/shard_map/all_to_all | solution.py:455
  36.7 1.4 %collective-permute-start.17 = (f32[8,2,8,128]{3,2,1,0:T(8,128)}, f32[8,2,8,128]{3,2,1,0:T(8,128)S(1)}, u32[]{:S(2)}, u32[]{:S(2)}) collective-permute-start(f32[8,2,8,128]{3,2,1,0:T(8,128)} %copy-done.8), channel_id=1, source_target_pairs={{0,1},{1,2},{2,3},{3,4},{4,5},{5,6},{6,7},{7,0},{8,9},{9,10},{10,1... | collective-permute-start | bytes 196616 | tf_op jit(solution)/shard_map/ppermute | solution.py:439
  38.0 2.3 %collective-permute-start.18 = (f32[8,2,8,128]{3,2,1,0:T(8,128)S(1)}, f32[8,2,8,128]{3,2,1,0:T(8,128)S(1)}, u32[]{:S(2)}, u32[]{:S(2)}) collective-permute-start(f32[8,2,8,128]{3,2,1,0:T(8,128)S(1)} %copy-done.10), channel_id=1, source_target_pairs={{0,7},{1,0},{2,1},{3,2},{4,3},{5,4},{6,5},{7,6},{8,15},{9,8},{10,9... | collective-permute-start | bytes 196616 | tf_op jit(solution)/shard_map/ppermute | solution.py:439
  40.3 0.7 fusion.2
  41.0 0.0 collective-permute-done.10.skip
  41.0 0.0 collective-permute-done.8.pair
  41.0 0.0 collective-permute-done.9.outer
  41.0 2.0 %all-to-all-done.own = f32[8,4,4,4,128]{4,3,2,1,0:T(4,128)S(1)} async-done(((f32[8,4,4,4,128]{4,3,2,1,0:T(4,128)}), f32[8,4,4,4,128]{4,3,2,1,0:T(4,128)S(1)}, u32[]{:S(2)}, u32[]{:S(2)}) %all-to-all-start) | async-done | bytes 262176 | tf_op jit(solution)/shard_map/all_to_all | solution.py:455
  43.0 2.0 %collective-permute-start.4 = (f32[8,4,4,4,128]{4,3,2,1,0:T(4,128)S(1)}, f32[8,4,4,4,128]{4,3,2,1,0:T(4,128)S(1)}, u32[]{:S(2)}, u32[]{:S(2)}) collective-permute-start(f32[8,4,4,4,128]{4,3,2,1,0:T(4,128)S(1)} %all-to-all-done.own), channel_id=1, source_target_pairs={{0,8},{8,0},{16,24},{24,16},{32,40},{40,32},{48,56},{56,48},{64,72... | collective-permute-start | bytes 786440 | tf_op jit(solution)/shard_map/ppermute | solution.py:443
  45.0 0.0 collective-permute-start.5
  45.1 5.0 %collective-permute-start.6 = (f32[8,2,4,4,128]{4,3,2,1,0:T(4,128)S(1)}, f32[8,2,4,4,128]{4,3,2,1,0:T(4,128)S(1)}, u32[]{:S(2)}, u32[]{:S(2)}) collective-permute-start(f32[8,2,4,4,128]{4,3,2,1,0:T(4,128)S(1)} %slice_select_fusion.1), channel_id=1, source_target_pairs={{0,16},{8,248},{16,32},{24,8},{32,48},{40,24},{48,64},{56,40},{64,... | collective-permute-start | bytes 393224 | tf_op jit(solution)/shard_map/ppermute | solution.py:451
  50.2 4.2 %collective-permute-done.6.skip = f32[8,2,4,4,128]{4,3,2,1,0:T(4,128)S(1)} collective-permute-done((f32[8,2,4,4,128]{4,3,2,1,0:T(4,128)S(1)}, f32[8,2,4,4,128]{4,3,2,1,0:T(4,128)S(1)}, u32[]{:S(2)}, u32[]{:S(2)}) %collective-permute-start.6) | collective-permute-done | bytes 131104 | tf_op jit(solution)/shard_map/ppermute | solution.py:451
  54.3 4.5 %collective-permute-start.11 = (f32[8,2,4,4,128]{4,3,2,1,0:T(4,128)S(1)}, f32[8,2,4,4,128]{4,3,2,1,0:T(4,128)S(1)}, u32[]{:S(2)}, u32[]{:S(2)}) collective-permute-start(f32[8,2,4,4,128]{4,3,2,1,0:T(4,128)S(1)} %slice_select_fusion.2), channel_id=1, source_target_pairs={{0,8},{8,0},{16,24},{24,16},{32,40},{40,32},{48,56},{56,48},{64,72... | collective-permute-start | bytes 393224 | tf_op jit(solution)/shard_map/ppermute | solution.py:443
  58.8 0.1 collective-permute-start.7
  58.9 0.0 collective-permute-done.18.fyhi_ref
  59.0 0.6 fusion.6
  59.6 0.2 collective-permute-done.11.far
  59.8 1.5 %shard_map.43 = (f32[16,4,32,128]{3,2,1,0:T(8,128)S(1)}, f32[8,2,16,128]{3,2,1,0:T(8,128)S(1)}, f32[8,128]{1,0:T(8,128)S(1)}) custom-call(s32[2]{0:T(128)S(1)} %pad_add_fusion.index_ref, f32[8,4,4,4,128]{4,3,2,1,0:T(4,128)S(1)} %all-to-all-done.1.own, f32[8,4,4,4,128]{4,3,2,1,0:T(4,128)S(1)} %collective-permute-done.8.pair, ...), custom_call_target="tpu_custom_call" | custom-call | tf_op jit(solution)/shard_map/pallas_call | solution.py:228
  61.3 0.0 collective-permute-done.7.far
  61.3 2.9 %shard_map.44 = (f32[10,4,32,128]{3,2,1,0:T(8,128)S(1)}, f32[8,4,32,128]{3,2,1,0:T(8,128)S(1)}, f32[2,2,2,16,128]{4,3,2,1,0:T(8,128)}, f32[2,16,128]{2,1,0:T(8,128)}, f32[2,8,128]{2,1,0:T(8,128)S(1)}) custom-call(s32[2]{0:T(128)S(1)} %pad_add_fusion.index_ref, f32[8,4,4,4,128]{4,3,2,1,0:T(4,128)S(1)} %all-to-all-done.own, ...), custom_call_target="tpu_custom_call" | custom-call | tf_op jit(solution)/shard_map/pallas_call | solution.py:283
  64.2 0.7 broadcast_in_dim.8
  64.9 5.1 %all-to-all-start.2 = ((f32[16,2,8,128]{3,2,1,0:T(8,128)}), f32[16,2,8,128]{3,2,1,0:T(8,128)S(1)}, u32[]{:S(2)}, u32[]{:S(2)}) async-start(f32[16,2,8,128]{3,2,1,0:T(8,128)} %broadcast_in_dim.8), calls=%async_computation.2 | async-start | bytes 262144 | tf_op jit(solution)/shard_map/all_to_all | solution.py:494
  70.1 0.8 copy-done.12
  70.9 0.7 pad_maximum_fusion.2
  71.5 3.5 %collective-permute-start.19 = (f32[2,12,8,128]{3,2,1,0:T(8,128)}, f32[2,12,8,128]{3,2,1,0:T(8,128)}, u32[]{:S(2)}, u32[]{:S(2)}) collective-permute-start(f32[2,12,8,128]{3,2,1,0:T(8,128)} %pad_maximum_fusion.2), channel_id=1, source_target_pairs={{0,8},{8,16},{16,24},{24,32},{32,40},{40,48},{48,56},{56,64},{64,7... | collective-permute-start | bytes 294920 | tf_op jit(solution)/shard_map/ppermute | solution.py:439
  75.0 0.0 collective-permute-start.14
  75.0 0.6 pad_maximum_fusion.3
  75.7 2.3 %collective-permute-start.20 = (f32[2,12,8,128]{3,2,1,0:T(8,128)}, f32[2,12,8,128]{3,2,1,0:T(8,128)}, u32[]{:S(2)}, u32[]{:S(2)}) collective-permute-start(f32[2,12,8,128]{3,2,1,0:T(8,128)} %pad_maximum_fusion.3), channel_id=1, source_target_pairs={{0,248},{8,0},{16,8},{24,16},{32,24},{40,32},{48,40},{56,48},{64,5... | collective-permute-start | bytes 294920 | tf_op jit(solution)/shard_map/ppermute | solution.py:439
  78.0 0.1 collective-permute-start.13
  78.0 3.1 %collective-permute-start.15 = (f32[2,16,128]{2,1,0:T(8,128)}, f32[2,16,128]{2,1,0:T(8,128)S(1)}, u32[]{:S(2)}, u32[]{:S(2)}) collective-permute-start(f32[2,16,128]{2,1,0:T(8,128)} %get-tuple-element.44), channel_id=1, source_target_pairs={{0,16},{8,248},{16,32},{24,8},{32,48},{40,24},{48,64},{56,40},{64,... | collective-permute-start | bytes 49160 | tf_op jit(solution)/shard_map/ppermute | solution.py:451
  81.1 0.7 collective-permute-done.14.outer2
  81.9 0.0 all-to-all-done.2.mine3
  81.9 0.4 collective-permute-start.12
  82.3 0.0 collective-permute-done.19.fxlo_ref
  82.3 0.2 collective-permute-start.16
  82.5 0.6 collective-permute-done.20.fxhi_ref
  83.0 0.0 collective-permute-done.15.skip2
  83.0 0.0 collective-permute-done.13.pair2
  83.0 0.5 collective-permute-done.16.far2
  83.5 0.0 collective-permute-done.12.other3
  83.5 0.6 copy-done.7
  84.1 0.9 %copy-done.2 = f32[8,8,8,128]{3,2,1,0:T(8,128)S(1)} copy-done((f32[8,8,8,128]{3,2,1,0:T(8,128)S(1)}, f32[8,8,8,128]{3,2,1,0:T(8,128)}, u32[]{:S(2)}) %copy-start.2) | copy-done | bytes 262168
  85.1 6.0 %shard_map.45 = (f32[8,8,1024]{2,1,0:T(8,128)}, f32[8,8,1024]{2,1,0:T(8,128)}) custom-call(s32[2]{0:T(128)S(1)} %copy-done.7, f32[16,2,8,128]{3,2,1,0:T(8,128)S(1)} %all-to-all-done.2.mine3, f32[16,2,8,128]{3,2,1,0:T(8,128)S(1)} %collective-permute-done.12.other3, f32[2,2,2,16,128]{4,3,2,1,0:T(8,128)} %get-tuple-element.43.fs2, ...), custom_call_target="tpu_custom_call" | custom-call | tf_op jit(solution)/shard_map/pallas_call | solution.py:429
  (38 shorter events, 0.2 us)
Async XLA Ops:
  3.1 9.4 %copy-start = (f32[2,8,8,8,128]{4,3,2,1,0:T(8,128)S(1)}, f32[2,8,8,8,128]{4,3,2,1,0:T(8,128)}, u32[]{:S(2)}) copy-start(f32[2,8,8,8,128]{4,3,2,1,0:T(8,128)} %get-tuple-element.28.sg_ref) | copy-start | bytes 1572868
  3.2 9.6 %collective-permute-start = (f32[2,8,2,8,128]{4,3,2,1,0:T(8,128)}, f32[2,8,2,8,128]{4,3,2,1,0:T(8,128)S(1)}, u32[]{:S(2)}, u32[]{:S(2)}) collective-permute-start(f32[2,8,2,8,128]{4,3,2,1,0:T(8,128)} %get-tuple-element.29), channel_id=1, source_target_pairs={{0,1},{1,2},{2,3},{3,4},{4,5},{5,6},{6,7},{7,0},{8,9},{9,10},{10,1... | collective-permute-start | bytes 393224 | tf_op jit(solution)/shard_map/ppermute | solution.py:439
  5.4 7.3 %collective-permute-start.1 = (f32[2,8,2,8,128]{4,3,2,1,0:T(8,128)}, f32[2,8,2,8,128]{4,3,2,1,0:T(8,128)S(1)}, u32[]{:S(2)}, u32[]{:S(2)}) collective-permute-start(f32[2,8,2,8,128]{4,3,2,1,0:T(8,128)} %get-tuple-element.30), channel_id=1, source_target_pairs={{0,7},{1,0},{2,1},{3,2},{4,3},{5,4},{6,5},{7,6},{8,15},{9,8},{10,9... | collective-permute-start | bytes 393224 | tf_op jit(solution)/shard_map/ppermute | solution.py:439
  9.1 9.1 %all-to-all-start.1 = ((f32[8,4,4,4,128]{4,3,2,1,0:T(4,128)}), f32[8,4,4,4,128]{4,3,2,1,0:T(4,128)S(1)}, u32[]{:S(2)}, u32[]{:S(2)}) async-start(f32[8,4,4,4,128]{4,3,2,1,0:T(4,128)} %broadcast_in_dim.7), calls=%async_computation.1 | async-start | bytes 524288 | tf_op jit(solution)/shard_map/all_to_all | solution.py:455
  12.7 48.6 %copy-start.6 = (s32[2]{0:T(128)}, s32[2]{0:T(128)S(1)}, u32[]{:S(2)}) copy-start(s32[2]{0:T(128)S(1)} %pad_add_fusion.index_ref) | copy-start | bytes 28
  12.8 17.7 %collective-permute-start.2 = (f32[2,2,12,8,128]{4,3,2,1,0:T(8,128)S(1)}, f32[2,2,12,8,128]{4,3,2,1,0:T(8,128)S(1)}, u32[]{:S(2)}, u32[]{:S(2)}) collective-permute-start(f32[2,2,12,8,128]{4,3,2,1,0:T(8,128)S(1)} %pad_maximum_fusion), channel_id=1, source_target_pairs={{0,8},{8,16},{16,24},{24,32},{32,40},{40,48},{48,56},{56,64},{64,7... | collective-permute-start | bytes 589832 | tf_op jit(solution)/shard_map/ppermute | solution.py:439
  16.9 13.5 %copy-start.3 = (f32[8,8,8,128]{3,2,1,0:T(8,128)S(1)}, f32[8,8,8,128]{3,2,1,0:T(8,128)}, u32[]{:S(2)}) copy-start(f32[8,8,8,128]{3,2,1,0:T(8,128)} %get-tuple-element.27.f_ref) | copy-start | bytes 786436
  17.0 13.5 %collective-permute-start.3 = (f32[2,2,12,8,128]{4,3,2,1,0:T(8,128)S(1)}, f32[2,2,12,8,128]{4,3,2,1,0:T(8,128)S(1)}, u32[]{:S(2)}, u32[]{:S(2)}) collective-permute-start(f32[2,2,12,8,128]{4,3,2,1,0:T(8,128)S(1)} %pad_maximum_fusion.1), channel_id=1, source_target_pairs={{0,248},{8,0},{16,8},{24,16},{32,24},{40,32},{48,40},{56,48},{64,5... | collective-permute-start | bytes 589832 | tf_op jit(solution)/shard_map/ppermute | solution.py:439
  18.3 22.7 %collective-permute-start.8 = (f32[8,4,4,4,128]{4,3,2,1,0:T(4,128)S(1)}, f32[8,4,4,4,128]{4,3,2,1,0:T(4,128)S(1)}, u32[]{:S(2)}, u32[]{:S(2)}) collective-permute-start(f32[8,4,4,4,128]{4,3,2,1,0:T(4,128)S(1)} %all-to-all-done.1.own), channel_id=1, source_target_pairs={{0,8},{8,0},{16,24},{24,16},{32,40},{40,32},{48,56},{56,48},{64,72... | collective-permute-start | bytes 786440 | tf_op jit(solution)/shard_map/ppermute | solution.py:443
  22.4 18.6 %collective-permute-start.9 = (f32[8,4,4,4,128]{4,3,2,1,0:T(4,128)S(1)}, f32[8,4,4,4,128]{4,3,2,1,0:T(4,128)S(1)}, u32[]{:S(2)}, u32[]{:S(2)}) collective-permute-start(f32[8,4,4,4,128]{4,3,2,1,0:T(4,128)S(1)} %all-to-all-done.1.own), channel_id=1, source_target_pairs={{0,248},{8,16},{16,8},{24,32},{32,24},{40,48},{48,40},{56,64},{64,... | collective-permute-start | bytes 786440 | tf_op jit(solution)/shard_map/ppermute | solution.py:447
  24.2 16.8 %collective-permute-start.10 = (f32[8,2,4,4,128]{4,3,2,1,0:T(4,128)}, f32[8,2,4,4,128]{4,3,2,1,0:T(4,128)}, u32[]{:S(2)}, u32[]{:S(2)}) collective-permute-start(f32[8,2,4,4,128]{4,3,2,1,0:T(4,128)} %slice_select_fusion), channel_id=1, source_target_pairs={{0,16},{8,248},{16,32},{24,8},{32,48},{40,24},{48,64},{56,40},{64,... | collective-permute-start | bytes 393224 | tf_op jit(solution)/shard_map/ppermute | solution.py:451
  31.7 0.6 copy-start.9
  32.3 0.8 copy-start.1
  32.3 0.8 copy-start.8
  33.1 4.9 %copy-start.10 = (f32[8,2,8,128]{3,2,1,0:T(8,128)S(1)}, f32[8,2,8,128]{3,2,1,0:T(8,128)}, u32[]{:S(2)}) copy-start(f32[8,2,8,128]{3,2,1,0:T(8,128)} %copy-done.9) | copy-start | bytes 196612
  33.1 9.9 %all-to-all-start = ((f32[8,4,4,4,128]{4,3,2,1,0:T(4,128)}), f32[8,4,4,4,128]{4,3,2,1,0:T(4,128)S(1)}, u32[]{:S(2)}, u32[]{:S(2)}) async-start(f32[8,4,4,4,128]{4,3,2,1,0:T(4,128)} %broadcast_in_dim.6), calls=%async_computation | async-start | bytes 524288 | tf_op jit(solution)/shard_map/all_to_all | solution.py:455
  36.7 33.4 %collective-permute-start.17 = (f32[8,2,8,128]{3,2,1,0:T(8,128)}, f32[8,2,8,128]{3,2,1,0:T(8,128)S(1)}, u32[]{:S(2)}, u32[]{:S(2)}) collective-permute-start(f32[8,2,8,128]{3,2,1,0:T(8,128)} %copy-done.8), channel_id=1, source_target_pairs={{0,1},{1,2},{2,3},{3,4},{4,5},{5,6},{6,7},{7,0},{8,9},{9,10},{10,1... | collective-permute-start | bytes 196616 | tf_op jit(solution)/shard_map/ppermute | solution.py:439
  38.0 20.9 %collective-permute-start.18 = (f32[8,2,8,128]{3,2,1,0:T(8,128)S(1)}, f32[8,2,8,128]{3,2,1,0:T(8,128)S(1)}, u32[]{:S(2)}, u32[]{:S(2)}) collective-permute-start(f32[8,2,8,128]{3,2,1,0:T(8,128)S(1)} %copy-done.10), channel_id=1, source_target_pairs={{0,7},{1,0},{2,1},{3,2},{4,3},{5,4},{6,5},{7,6},{8,15},{9,8},{10,9... | collective-permute-start | bytes 196616 | tf_op jit(solution)/shard_map/ppermute | solution.py:439
  43.0 15.8 %collective-permute-start.4 = (f32[8,4,4,4,128]{4,3,2,1,0:T(4,128)S(1)}, f32[8,4,4,4,128]{4,3,2,1,0:T(4,128)S(1)}, u32[]{:S(2)}, u32[]{:S(2)}) collective-permute-start(f32[8,4,4,4,128]{4,3,2,1,0:T(4,128)S(1)} %all-to-all-done.own), channel_id=1, source_target_pairs={{0,8},{8,0},{16,24},{24,16},{32,40},{40,32},{48,56},{56,48},{64,72... | collective-permute-start | bytes 786440 | tf_op jit(solution)/shard_map/ppermute | solution.py:443
  45.0 13.8 %collective-permute-start.5 = (f32[8,4,4,4,128]{4,3,2,1,0:T(4,128)S(1)}, f32[8,4,4,4,128]{4,3,2,1,0:T(4,128)S(1)}, u32[]{:S(2)}, u32[]{:S(2)}) collective-permute-start(f32[8,4,4,4,128]{4,3,2,1,0:T(4,128)S(1)} %all-to-all-done.own), channel_id=1, source_target_pairs={{0,248},{8,16},{16,8},{24,32},{32,24},{40,48},{48,40},{56,64},{64,... | collective-permute-start | bytes 786440 | tf_op jit(solution)/shard_map/ppermute | solution.py:447
  45.1 9.2 %collective-permute-start.6 = (f32[8,2,4,4,128]{4,3,2,1,0:T(4,128)S(1)}, f32[8,2,4,4,128]{4,3,2,1,0:T(4,128)S(1)}, u32[]{:S(2)}, u32[]{:S(2)}) collective-permute-start(f32[8,2,4,4,128]{4,3,2,1,0:T(4,128)S(1)} %slice_select_fusion.1), channel_id=1, source_target_pairs={{0,16},{8,248},{16,32},{24,8},{32,48},{40,24},{48,64},{56,40},{64,... | collective-permute-start | bytes 393224 | tf_op jit(solution)/shard_map/ppermute | solution.py:451
  54.3 5.5 %collective-permute-start.11 = (f32[8,2,4,4,128]{4,3,2,1,0:T(4,128)S(1)}, f32[8,2,4,4,128]{4,3,2,1,0:T(4,128)S(1)}, u32[]{:S(2)}, u32[]{:S(2)}) collective-permute-start(f32[8,2,4,4,128]{4,3,2,1,0:T(4,128)S(1)} %slice_select_fusion.2), channel_id=1, source_target_pairs={{0,8},{8,0},{16,24},{24,16},{32,40},{40,32},{48,56},{56,48},{64,72... | collective-permute-start | bytes 393224 | tf_op jit(solution)/shard_map/ppermute | solution.py:443
  58.8 2.4 %collective-permute-start.7 = (f32[8,2,4,4,128]{4,3,2,1,0:T(4,128)S(1)}, f32[8,2,4,4,128]{4,3,2,1,0:T(4,128)S(1)}, u32[]{:S(2)}, u32[]{:S(2)}) collective-permute-start(f32[8,2,4,4,128]{4,3,2,1,0:T(4,128)S(1)} %slice_select_fusion.3), channel_id=1, source_target_pairs={{0,8},{8,0},{16,24},{24,16},{32,40},{40,32},{48,56},{56,48},{64,72... | collective-permute-start | bytes 393224 | tf_op jit(solution)/shard_map/ppermute | solution.py:443
  58.9 2.3 %copy-start.4 = (f32[8,2,8,128]{3,2,1,0:T(8,128)}, f32[8,2,8,128]{3,2,1,0:T(8,128)S(1)}, u32[]{:S(2)}) copy-start(f32[8,2,8,128]{3,2,1,0:T(8,128)S(1)} %collective-permute-done.18.fyhi_ref) | copy-start | bytes 196612
  64.9 5.2 %copy-start.14 = (f32[2,2,8,128]{3,2,1,0:T(8,128)S(1)}, f32[2,2,8,128]{3,2,1,0:T(8,128)}, u32[]{:S(2)}) copy-start(f32[2,2,8,128]{3,2,1,0:T(8,128)} %get-tuple-element.63) | copy-start | bytes 49156
  64.9 17.0 %all-to-all-start.2 = ((f32[16,2,8,128]{3,2,1,0:T(8,128)}), f32[16,2,8,128]{3,2,1,0:T(8,128)S(1)}, u32[]{:S(2)}, u32[]{:S(2)}) async-start(f32[16,2,8,128]{3,2,1,0:T(8,128)} %broadcast_in_dim.8), calls=%async_computation.2 | async-start | bytes 262144 | tf_op jit(solution)/shard_map/all_to_all | solution.py:494
  70.0 0.8 copy-start.12
  70.9 4.1 %copy-start.11 = (f32[2,8,8,128]{3,2,1,0:T(8,128)S(1)}, f32[2,8,8,128]{3,2,1,0:T(8,128)}, u32[]{:S(2)}) copy-start(f32[2,8,8,128]{3,2,1,0:T(8,128)} %get-tuple-element.54) | copy-start | bytes 196612
  70.9 4.1 %copy-start.13 = (f32[2,2,8,128]{3,2,1,0:T(8,128)S(1)}, f32[2,2,8,128]{3,2,1,0:T(8,128)}, u32[]{:S(2)}) copy-start(f32[2,2,8,128]{3,2,1,0:T(8,128)} %get-tuple-element.62) | copy-start | bytes 49156
  71.5 10.7 %collective-permute-start.19 = (f32[2,12,8,128]{3,2,1,0:T(8,128)}, f32[2,12,8,128]{3,2,1,0:T(8,128)}, u32[]{:S(2)}, u32[]{:S(2)}) collective-permute-start(f32[2,12,8,128]{3,2,1,0:T(8,128)} %pad_maximum_fusion.2), channel_id=1, source_target_pairs={{0,8},{8,16},{16,24},{24,32},{32,40},{40,48},{48,56},{56,64},{64,7... | collective-permute-start | bytes 294920 | tf_op jit(solution)/shard_map/ppermute | solution.py:439
  75.0 6.9 %collective-permute-start.14 = (f32[2,2,2,16,128]{4,3,2,1,0:T(8,128)}, f32[2,2,2,16,128]{4,3,2,1,0:T(8,128)S(1)}, u32[]{:S(2)}, u32[]{:S(2)}) collective-permute-start(f32[2,2,2,16,128]{4,3,2,1,0:T(8,128)} %get-tuple-element.43.fs2), channel_id=1, source_target_pairs={{0,248},{8,16},{16,8},{24,32},{32,24},{40,48},{48,40},{56,64},{64,... | collective-permute-start | bytes 196616 | tf_op jit(solution)/shard_map/ppermute | solution.py:447
  75.0 8.5 %copy-start.5 = (f32[8,2,8,128]{3,2,1,0:T(8,128)S(1)}, f32[8,2,8,128]{3,2,1,0:T(8,128)}, u32[]{:S(2)}) copy-start(f32[8,2,8,128]{3,2,1,0:T(8,128)} %copy-done.4) | copy-start | bytes 196612
  75.7 7.4 %collective-permute-start.20 = (f32[2,12,8,128]{3,2,1,0:T(8,128)}, f32[2,12,8,128]{3,2,1,0:T(8,128)}, u32[]{:S(2)}, u32[]{:S(2)}) collective-permute-start(f32[2,12,8,128]{3,2,1,0:T(8,128)} %pad_maximum_fusion.3), channel_id=1, source_target_pairs={{0,248},{8,0},{16,8},{24,16},{32,24},{40,32},{48,40},{56,48},{64,5... | collective-permute-start | bytes 294920 | tf_op jit(solution)/shard_map/ppermute | solution.py:439
  78.0 5.1 %collective-permute-start.13 = (f32[2,2,2,16,128]{4,3,2,1,0:T(8,128)}, f32[2,2,2,16,128]{4,3,2,1,0:T(8,128)}, u32[]{:S(2)}, u32[]{:S(2)}) collective-permute-start(f32[2,2,2,16,128]{4,3,2,1,0:T(8,128)} %get-tuple-element.43.fs2), channel_id=1, source_target_pairs={{0,8},{8,0},{16,24},{24,16},{32,40},{40,32},{48,56},{56,48},{64,72... | collective-permute-start | bytes 196616 | tf_op jit(solution)/shard_map/ppermute | solution.py:443
  78.0 5.0 %collective-permute-start.15 = (f32[2,16,128]{2,1,0:T(8,128)}, f32[2,16,128]{2,1,0:T(8,128)S(1)}, u32[]{:S(2)}, u32[]{:S(2)}) collective-permute-start(f32[2,16,128]{2,1,0:T(8,128)} %get-tuple-element.44), channel_id=1, source_target_pairs={{0,16},{8,248},{16,32},{24,8},{32,48},{40,24},{48,64},{56,40},{64,... | collective-permute-start | bytes 49160 | tf_op jit(solution)/shard_map/ppermute | solution.py:451
  81.9 1.7 %collective-permute-start.12 = (f32[16,2,8,128]{3,2,1,0:T(8,128)S(1)}, f32[16,2,8,128]{3,2,1,0:T(8,128)S(1)}, u32[]{:S(2)}, u32[]{:S(2)}) collective-permute-start(f32[16,2,8,128]{3,2,1,0:T(8,128)S(1)} %all-to-all-done.2.mine3), channel_id=1, source_target_pairs={{0,8},{8,0},{16,24},{24,16},{32,40},{40,32},{48,56},{56,48},{64,72... | collective-permute-start | bytes 393224 | tf_op jit(solution)/shard_map/ppermute | solution.py:443
  82.3 1.3 %collective-permute-start.16 = (f32[2,16,128]{2,1,0:T(8,128)S(1)}, f32[2,16,128]{2,1,0:T(8,128)S(1)}, u32[]{:S(2)}, u32[]{:S(2)}) collective-permute-start(f32[2,16,128]{2,1,0:T(8,128)S(1)} %fusion), channel_id=1, source_target_pairs={{0,8},{8,0},{16,24},{24,16},{32,40},{40,32},{48,56},{56,48},{64,72... | collective-permute-start | bytes 49160 | tf_op jit(solution)/shard_map/ppermute | solution.py:443
  83.5 0.6 copy-start.7
  84.1 0.9 %copy-start.2 = (f32[8,8,8,128]{3,2,1,0:T(8,128)S(1)}, f32[8,8,8,128]{3,2,1,0:T(8,128)}, u32[]{:S(2)}) copy-start(f32[8,8,8,128]{3,2,1,0:T(8,128)} %copy-done.1) | copy-start | bytes 786436

commit v3 on v1

--- a/solution.py
+++ b/solution.py
@@ -135,7 +135,7 @@
         s1[x, 1:11] = THIRD * s0[x, 1:11] + gext_ref[x, 1:11] * total
         return carry
 
-    lax.fori_loop(1, 11, first, 0)
+    lax.fori_loop(1, 11, first, 0, unroll=4)
 
     def second(x, carry):
         f1 = THIRD * f_ref[x - 2] + fine_neighbours(s0, x, 2, 10)
@@ -143,7 +143,7 @@
         src_ref[x - 2] = s0[x, 2:10] + s1[x, 2:10]
         return carry
 
-    lax.fori_loop(2, 10, second, 0)
+    lax.fori_loop(2, 10, second, 0, unroll=4)
     fylo_ref[...] = f2_ref[:, 0:2]
     fyhi_ref[...] = f2_ref[:, 6:8]
     block_pairs(f2_ref, pairs)
@@ -206,7 +206,7 @@
         g1_ref[x] = OMEGA / (6.0 + 4.0 * field[x])
         return carry
 
-    lax.fori_loop(0, 16, scale1, 0)
+    lax.fori_loop(0, 16, scale1, 0, unroll=4)
     for x in range(8):
         c2[x] = restrict_middle(field, 2 * x, pairs, 0.125)
         g2_ref[x] = OMEGA / (6.0 + 16.0 * c2[x])
@@ -234,7 +234,7 @@
         s0[x] = g1_ref[x] * rhs[x]
         return carry
 
-    lax.fori_loop(0, 16, start, 0)
+    lax.fori_loop(0, 16, start, 0, unroll=4)
 
     def first(x, carry):
         total = coarse_neighbours(s0, x)
@@ -242,13 +242,13 @@
         rhs[x] = THIRD * rhs[x] + total
         return carry
 
-    lax.fori_loop(1, 15, first, 0)
+    lax.fori_loop(1, 15, first, 0, unroll=4)
 
     def second(x, carry):
         f2[x - 2] = THIRD * rhs[x] + coarse_neighbours(s1, x)
         return carry
 
-    lax.fori_loop(2, 14, second, 0)
+    lax.fori_loop(2, 14, second, 0, unroll=4)
     f1_ref[...] = f2[1:11]
     src1_ref[...] = s0[4:12] + s1[4:12]
 
@@ -292,7 +292,7 @@
     g0_ref, f0_ref, src0_ref, fylo_ref, fyhi_ref, fxlo_ref, fxhi_ref,
     guess_ref, source_ref,
     e3, out3, f2, src2, r2, sa2, out2, r1, sa1, out1,
-    rep, r0, f0, s3, s4, turned, placed,
+    r0, f0, s3, s4, turned, placed,
 ):
     core = core_of(index_ref)
     chip = lax.div(index_ref[0], 2)
@@ -349,7 +349,7 @@
         sa1[x] = g * (f1_ref[x - 1] - (OMEGA / g) * r1[x] + coarse_neighbours(r1, x))
         return carry
 
-    lax.fori_loop(1, 11, middle1, 0)
+    lax.fori_loop(1, 11, middle1, 0, unroll=4)
 
     def last1(x, carry):
         sb = THIRD * sa1[x] + g1_ref[x + 2] * coarse_neighbours(sa1, x)
@@ -358,20 +358,18 @@
             out1[x - 2, pl.ds(32 * c, 32), :] = row[c]
         return carry
 
-    lax.fori_loop(2, 10, last1, 0)
+    lax.fori_loop(2, 10, last1, 0, unroll=4)
 
     def spread0(x, carry):
         for y in range(8):
             row = out1[x, pl.ds(14 + y, 4, stride=32), :]
-            rep[pl.ds(0, 4, stride=2), :] = row
-            rep[pl.ds(1, 4, stride=2), :] = row
-            both = rep[...]
             for p in range(2):
                 for q in range(2):
-                    r0[2 * x + p, 2 * y + q] = both
-        return carry
-
-    lax.fori_loop(0, 8, spread0, 0)
+                    for c in range(2):
+                        r0[2 * x + p, 2 * y + q, pl.ds(c, 4, stride=2), :] = row
+        return carry
+
+    lax.fori_loop(0, 8, spread0, 0, unroll=4)
     f0[2:10, 2:10] = f0_ref[...]
     f0[2:10, 0:2] = fylo_ref[...]
     f0[2:10, 10:12] = fyhi_ref[...]
@@ -385,13 +383,13 @@
         s3[x] = g * f
         return carry
 
-    lax.fori_loop(0, 12, residual0, 0)
+    lax.fori_loop(0, 12, residual0, 0, unroll=4)
 
     def first0(x, carry):
         s4[x, 1:11] = THIRD * s3[x, 1:11] + g0_ref[x, 1:11] * fine_neighbours(s3, x, 1, 11)
         return carry
 
-    lax.fori_loop(1, 11, first0, 0)
+    lax.fori_loop(1, 11, first0, 0, unroll=4)
 
     def second0(x, carry):
         f4 = THIRD * f0[x, 2:10] + fine_neighbours(s3, x, 2, 10)
@@ -401,7 +399,7 @@
         placed[pl.ds(64 * (x - 2) + 512, 64), :] = source.reshape(64, 128)
         return carry
 
-    lax.fori_loop(2, 10, second0, 0)
+    lax.fori_loop(2, 10, second0, 0, unroll=4)
     for c in range(8):
         turned[pl.ds(c, 128, stride=8), :] = placed[pl.ds(c, 128, stride=8), :].T
     result = turned[...].T
@@ -414,7 +412,7 @@
         (32, 2, 8, 128), (32, 8, 128), (6, 2, 16, 128), (6, 2, 16, 128),
         (10, 2, 16, 128), (10, 2, 16, 128), (6, 2, 16, 128),
         (12, 4, 32, 128), (12, 4, 32, 128), (8, 128, 128),
-        (8, 128), (16, 16, 8, 128), (12, 12, 8, 128), (12, 12, 8, 128), (12, 12, 8, 128),
+        (16, 16, 8, 128), (12, 12, 8, 128), (12, 12, 8, 128), (12, 12, 8, 128),
         (1024, 128), (1024, 128),
     ]
     return pl.pallas_call(
@@ -446,10 +444,15 @@
     return lax.all_to_all(jnp.broadcast_to(v[None], (GY,) + v.shape), "gy", 0, 0)
 
 
+def together(*arrays):
+    return lax.optimization_barrier(arrays)
+
+
 def level1_rows(core, v):
     pair = swap_core(v)
     outer = swap_outer(v)
     skip = skip_chip(jnp.where(core == 0, v[:, 2:4], v[:, 0:2]))
+    pair, outer, skip = together(pair, outer, skip)
     far = swap_core(jnp.where(core == 0, outer[:, 2:4], outer[:, 0:2]))
     return v, pair, outer, skip, far
 

time: 97.1 us -> 90.8 us (0.935)
  waiting for transfers between devices: 15 us -> 8.83 us
  Pallas kernels: 16.1 us -> 11.1 us
  starting transfers between devices: 54.3 us -> 57.9 us
    ppermute x7, starting transfers between devices: 1.23 us -> 11.6 us  [swap_core(): return lax.ppermute(v, 'gx', [(i, i ^ 1) for i in range(GX)])]
    ppermute x3, waiting for transfers between devices: 10.3 us -> 0.81 us  [swap_outer(): lax.ppermute(v, 'gx', [(i, (i + 1 if i % 2 else i - 1) % GX) for i in ran...]
    ppermute x3, starting transfers between devices: 5.21 us -> 1.1 us  [swap_outer(): lax.ppermute(v, 'gx', [(i, (i + 1 if i % 2 else i - 1) % GX) for i in ran...]
    ppermute x3, waiting for transfers between devices: 0.11 us -> 4.16 us  [skip_chip(): lax.ppermute(v, 'gx', [(i, (i - 2 if i % 2 else i + 2) % GX) for i in ran...]
    pallas_call x1, Pallas kernels: 8.01 us -> 5.51 us  [up(): pl.pallas_call(up_kernel, out_shape=(shape(8, 8, 1024), shape(8, 8, 1024)...]
    all_to_all x1, starting transfers between devices: 7.1 us -> 5.31 us  [per_device(): lax.all_to_all(jnp.broadcast_to(both3[None], (16,) + both3.shape), 'gx',...]
    pallas_call x1, Pallas kernels: 2.51 us -> 1.03 us  [fine_down(): pl.pallas_call(fine_down_kernel, out_shape=(shape(8, 8, 8, 128), shape(8,...]
    pallas_call x1, Pallas kernels: 3.89 us -> 2.65 us  [middle_down(): pl.pallas_call(middle_down_kernel, out_shape=(shape(10, 4, 32, 128), shap...]
  transfers between devices with their start and end apart: 24 -> 24, of which waited for: 7 -> 6; matrix products, arithmetic and copies ran while one was open for 6% -> 6% of each run, Pallas kernels for 8% -> 6%
where the time goes in v3:
time: 90.8 us; the launch traced here: 89.4 us
  starting transfers between devices  57.9 us (64%)
  Pallas kernels  11.1 us (12%)
  waiting for transfers between devices  8.83 us (10%)
  local copies, waits for them, and re-layouts  8.44 us (9%)
  other arithmetic  2.21 us (2%)
    ppermute x8, starting transfers between devices, shifted(): lax.ppermute(v, axis, [(i, (i + step) % count) for i in range(count)])  18.6 us
    ppermute x3, starting transfers between devices, skip_chip(): lax.ppermute(v, 'gx', [(i, (i - 2 if i % 2 else i + 2) % GX) for i in ran...  14.4 us
    ppermute x7, starting transfers between devices, swap_core(): return lax.ppermute(v, 'gx', [(i, i ^ 1) for i in range(GX)])  11.6 us
    all_to_all x2, starting transfers between devices, gather_y(): lax.all_to_all(jnp.broadcast_to(v[None], (GY,) + v.shape), 'gy', 0, 0)  6.96 us
    pallas_call x1, Pallas kernels, up(): pl.pallas_call(up_kernel, out_shape=(shape(8, 8, 1024), shape(8, 8, 1024)...  5.51 us
    all_to_all x1, starting transfers between devices, per_device(): lax.all_to_all(jnp.broadcast_to(both3[None], (16,) + both3.shape), 'gx',...  5.31 us
    unnamed x30, local copies, waits for them, and re-layouts  4.91 us
    ppermute x3, waiting for transfers between devices, skip_chip(): lax.ppermute(v, 'gx', [(i, (i - 2 if i % 2 else i + 2) % GX) for i in ran...  4.16 us
  transfers between devices with their start and end apart: 24, of which 6 were waited for; matrix products, arithmetic and copies ran while one was open for 6% of the time, Pallas kernels for 6%

profile of v3, /device:TPU:1, one launch (start us, length us, event | category | flops | bytes accessed | tf_op | source)
XLA Modules:
  0.0 89.4 jit_solution(14925093261014652739)
XLA Ops:
  0.6 0.9 %copy-done.2 = f32[8,8,1024]{2,1,0:T(8,128)S(1)} copy-done((f32[8,8,1024]{2,1,0:T(8,128)S(1)}, f32[8,8,1024]{2,1,0:T(8,128)}, u32[]{:S(2)}) %copy-start.2) | copy-done | bytes 262168
  1.6 0.9 %copy-done.3 = f32[8,8,1024]{2,1,0:T(8,128)S(1)} copy-done((f32[8,8,1024]{2,1,0:T(8,128)S(1)}, f32[8,8,1024]{2,1,0:T(8,128)}, u32[]{:S(2)}) %copy-start.3) | copy-done | bytes 262168
  2.5 0.5 shard_map.41
  3.0 2.2 %collective-permute-start = (f32[2,8,2,8,128]{4,3,2,1,0:T(8,128)S(1)}, f32[2,8,2,8,128]{4,3,2,1,0:T(8,128)S(1)}, u32[]{:S(2)}, u32[]{:S(2)}) collective-permute-start(f32[2,8,2,8,128]{4,3,2,1,0:T(8,128)S(1)} %get-tuple-element.29), channel_id=1, source_target_pairs={{0,1},{1,2},{2,3},{3,4},{4,5},{5,6},{6,7},{7,0},{8,9},{9,10},{10,1... | collective-permute-start | bytes 393224 | tf_op jit(solution)/shard_map/ppermute | solution.py:428
  5.2 2.3 %collective-permute-start.1 = (f32[2,8,2,8,128]{4,3,2,1,0:T(8,128)S(1)}, f32[2,8,2,8,128]{4,3,2,1,0:T(8,128)S(1)}, u32[]{:S(2)}, u32[]{:S(2)}) collective-permute-start(f32[2,8,2,8,128]{4,3,2,1,0:T(8,128)S(1)} %get-tuple-element.30), channel_id=1, source_target_pairs={{0,7},{1,0},{2,1},{3,2},{4,3},{5,4},{6,5},{7,6},{8,15},{9,8},{10,9... | collective-permute-start | bytes 393224 | tf_op jit(solution)/shard_map/ppermute | solution.py:428
  7.5 0.7 broadcast_in_dim.7
  8.3 3.4 %all-to-all-start.1 = ((f32[8,4,4,4,128]{4,3,2,1,0:T(4,128)}), f32[8,4,4,4,128]{4,3,2,1,0:T(4,128)S(1)}, u32[]{:S(2)}, u32[]{:S(2)}) async-start(f32[8,4,4,4,128]{4,3,2,1,0:T(4,128)} %broadcast_in_dim.7), calls=%async_computation.1 | async-start | bytes 524288 | tf_op jit(solution)/shard_map/all_to_all | solution.py:444
  11.7 0.1 pad_add_fusion.index_ref
  11.8 0.0 collective-permute-done.1.yhi_ref
  11.8 0.0 collective-permute-done.ylo_ref
  11.9 4.7 %collective-permute-start.2 = (f32[2,2,12,8,128]{4,3,2,1,0:T(8,128)S(1)}, f32[2,2,12,8,128]{4,3,2,1,0:T(8,128)S(1)}, u32[]{:S(2)}, u32[]{:S(2)}) collective-permute-start(f32[2,2,12,8,128]{4,3,2,1,0:T(8,128)S(1)} %pad_maximum_fusion), channel_id=1, source_target_pairs={{0,8},{8,16},{16,24},{24,32},{32,40},{40,48},{48,56},{56,64},{64,7... | collective-permute-start | bytes 589832 | tf_op jit(solution)/shard_map/ppermute | solution.py:428
  16.6 0.1 collective-permute-start.3
  16.7 0.7 all-to-all-done.1.own
  17.4 4.1 %collective-permute-start.8 = (f32[8,4,4,4,128]{4,3,2,1,0:T(4,128)S(1)}, f32[8,4,4,4,128]{4,3,2,1,0:T(4,128)S(1)}, u32[]{:S(2)}, u32[]{:S(2)}) collective-permute-start(f32[8,4,4,4,128]{4,3,2,1,0:T(4,128)S(1)} %all-to-all-done.1.own), channel_id=1, source_target_pairs={{0,8},{8,0},{16,24},{24,16},{32,40},{40,32},{48,56},{56,48},{64,72... | collective-permute-start | bytes 786440 | tf_op jit(solution)/shard_map/ppermute | solution.py:432
  21.5 1.1 %collective-permute-start.9 = (f32[8,4,4,4,128]{4,3,2,1,0:T(4,128)S(1)}, f32[8,4,4,4,128]{4,3,2,1,0:T(4,128)S(1)}, u32[]{:S(2)}, u32[]{:S(2)}) collective-permute-start(f32[8,4,4,4,128]{4,3,2,1,0:T(4,128)S(1)} %all-to-all-done.1.own), channel_id=1, source_target_pairs={{0,248},{8,16},{16,8},{24,32},{32,24},{40,48},{48,40},{56,64},{64,... | collective-permute-start | bytes 786440 | tf_op jit(solution)/shard_map/ppermute | solution.py:436
  22.6 0.7 slice_select_fusion
  23.3 6.3 %collective-permute-start.10 = (f32[8,2,4,4,128]{4,3,2,1,0:T(4,128)}, f32[8,2,4,4,128]{4,3,2,1,0:T(4,128)}, u32[]{:S(2)}, u32[]{:S(2)}) collective-permute-start(f32[8,2,4,4,128]{4,3,2,1,0:T(4,128)} %slice_select_fusion), channel_id=1, source_target_pairs={{0,16},{8,248},{16,32},{24,8},{32,48},{40,24},{48,64},{56,40},{64,... | collective-permute-start | bytes 393224 | tf_op jit(solution)/shard_map/ppermute | solution.py:440
  29.5 0.0 collective-permute-done.2.xlo_ref
  29.5 0.0 collective-permute-done.3.xhi_ref
  29.5 1.0 %shard_map.42 = (f32[8,8,8,128]{3,2,1,0:T(8,128)S(1)}, f32[8,8,8,128]{3,2,1,0:T(8,128)S(1)}, f32[12,12,8,128]{3,2,1,0:T(8,128)S(1)}, f32[8,2,8,128]{3,2,1,0:T(8,...) custom-call(f32[8,8,8,128]{3,2,1,0:T(8,128)S(1)} %get-tuple-element.27.f_ref, ...), custom_call_target="tpu_custom_call" | custom-call | tf_op jit(solution)/shard_map/pallas_call | solution.py:154
  30.6 0.6 copy-done.9
  31.2 0.8 broadcast_in_dim.6
  32.0 3.5 %all-to-all-start = ((f32[8,4,4,4,128]{4,3,2,1,0:T(4,128)}), f32[8,4,4,4,128]{4,3,2,1,0:T(4,128)S(1)}, u32[]{:S(2)}, u32[]{:S(2)}) async-start(f32[8,4,4,4,128]{4,3,2,1,0:T(4,128)} %broadcast_in_dim.6), calls=%async_computation | async-start | bytes 524288 | tf_op jit(solution)/shard_map/all_to_all | solution.py:444
  35.6 1.4 %collective-permute-start.17 = (f32[8,2,8,128]{3,2,1,0:T(8,128)}, f32[8,2,8,128]{3,2,1,0:T(8,128)S(1)}, u32[]{:S(2)}, u32[]{:S(2)}) collective-permute-start(f32[8,2,8,128]{3,2,1,0:T(8,128)} %copy-done.8), channel_id=1, source_target_pairs={{0,1},{1,2},{2,3},{3,4},{4,5},{5,6},{6,7},{7,0},{8,9},{9,10},{10,1... | collective-permute-start | bytes 196616 | tf_op jit(solution)/shard_map/ppermute | solution.py:428
  36.9 2.3 %collective-permute-start.18 = (f32[8,2,8,128]{3,2,1,0:T(8,128)S(1)}, f32[8,2,8,128]{3,2,1,0:T(8,128)S(1)}, u32[]{:S(2)}, u32[]{:S(2)}) collective-permute-start(f32[8,2,8,128]{3,2,1,0:T(8,128)S(1)} %copy-done.10), channel_id=1, source_target_pairs={{0,7},{1,0},{2,1},{3,2},{4,3},{5,4},{6,5},{7,6},{8,15},{9,8},{10,9... | collective-permute-start | bytes 196616 | tf_op jit(solution)/shard_map/ppermute | solution.py:428
  39.2 0.7 fusion.2
  39.9 0.0 collective-permute-done.10.skip
  39.9 0.0 collective-permute-done.8.pair
  39.9 0.0 collective-permute-done.9.outer
  39.9 2.0 %all-to-all-done.own = f32[8,4,4,4,128]{4,3,2,1,0:T(4,128)S(1)} async-done(((f32[8,4,4,4,128]{4,3,2,1,0:T(4,128)}), f32[8,4,4,4,128]{4,3,2,1,0:T(4,128)S(1)}, u32[]{:S(2)}, u32[]{:S(2)}) %all-to-all-start) | async-done | bytes 262176 | tf_op jit(solution)/shard_map/all_to_all | solution.py:444
  41.9 2.0 %collective-permute-start.4 = (f32[8,4,4,4,128]{4,3,2,1,0:T(4,128)S(1)}, f32[8,4,4,4,128]{4,3,2,1,0:T(4,128)S(1)}, u32[]{:S(2)}, u32[]{:S(2)}) collective-permute-start(f32[8,4,4,4,128]{4,3,2,1,0:T(4,128)S(1)} %all-to-all-done.own), channel_id=1, source_target_pairs={{0,8},{8,0},{16,24},{24,16},{32,40},{40,32},{48,56},{56,48},{64,72... | collective-permute-start | bytes 786440 | tf_op jit(solution)/shard_map/ppermute | solution.py:432
  43.9 0.0 collective-permute-start.5
  44.0 5.0 %collective-permute-start.6 = (f32[8,2,4,4,128]{4,3,2,1,0:T(4,128)S(1)}, f32[8,2,4,4,128]{4,3,2,1,0:T(4,128)S(1)}, u32[]{:S(2)}, u32[]{:S(2)}) collective-permute-start(f32[8,2,4,4,128]{4,3,2,1,0:T(4,128)S(1)} %slice_select_fusion.1), channel_id=1, source_target_pairs={{0,16},{8,248},{16,32},{24,8},{32,48},{40,24},{48,64},{56,40},{64,... | collective-permute-start | bytes 393224 | tf_op jit(solution)/shard_map/ppermute | solution.py:440
  49.0 4.2 %collective-permute-done.6.skip = f32[8,2,4,4,128]{4,3,2,1,0:T(4,128)S(1)} collective-permute-done((f32[8,2,4,4,128]{4,3,2,1,0:T(4,128)S(1)}, f32[8,2,4,4,128]{4,3,2,1,0:T(4,128)S(1)}, u32[]{:S(2)}, u32[]{:S(2)}) %collective-permute-start.6) | collective-permute-done | bytes 131104 | tf_op jit(solution)/shard_map/ppermute | solution.py:440
  53.2 4.5 %collective-permute-start.11 = (f32[8,2,4,4,128]{4,3,2,1,0:T(4,128)S(1)}, f32[8,2,4,4,128]{4,3,2,1,0:T(4,128)S(1)}, u32[]{:S(2)}, u32[]{:S(2)}) collective-permute-start(f32[8,2,4,4,128]{4,3,2,1,0:T(4,128)S(1)} %slice_select_fusion.2), channel_id=1, source_target_pairs={{0,8},{8,0},{16,24},{24,16},{32,40},{40,32},{48,56},{56,48},{64,72... | collective-permute-start | bytes 393224 | tf_op jit(solution)/shard_map/ppermute | solution.py:432
  57.7 0.0 collective-permute-done.4.pair
  57.7 0.3 collective-permute-start.7
  58.0 0.0 collective-permute-done.18.fyhi_ref
  58.0 0.6 fusion.6
  58.6 0.0 collective-permute-done.11.far
  58.7 1.4 %shard_map.43 = (f32[16,4,32,128]{3,2,1,0:T(8,128)S(1)}, f32[8,2,16,128]{3,2,1,0:T(8,128)S(1)}, f32[8,128]{1,0:T(8,128)S(1)}) custom-call(s32[2]{0:T(128)S(1)} %pad_add_fusion.index_ref, f32[8,4,4,4,128]{4,3,2,1,0:T(4,128)S(1)} %all-to-all-done.1.own, f32[8,4,4,4,128]{4,3,2,1,0:T(4,128)S(1)} %collective-permute-done.8.pair, ...), custom_call_target="tpu_custom_call" | custom-call | tf_op jit(solution)/shard_map/pallas_call | solution.py:217
  60.1 0.0 collective-permute-done.7.far
  60.1 2.7 %shard_map.44 = (f32[10,4,32,128]{3,2,1,0:T(8,128)S(1)}, f32[8,4,32,128]{3,2,1,0:T(8,128)S(1)}, f32[2,2,2,16,128]{4,3,2,1,0:T(8,128)}, f32[2,16,128]{2,1,0:T(8,128)}, f32[2,8,128]{2,1,0:T(8,128)S(1)}) custom-call(s32[2]{0:T(128)S(1)} %pad_add_fusion.index_ref, f32[8,4,4,4,128]{4,3,2,1,0:T(4,128)S(1)} %all-to-all-done.own, ...), custom_call_target="tpu_custom_call" | custom-call | tf_op jit(solution)/shard_map/pallas_call | solution.py:272
  62.8 0.7 broadcast_in_dim.8
  63.4 5.3 %all-to-all-start.2 = ((f32[16,2,8,128]{3,2,1,0:T(8,128)}), f32[16,2,8,128]{3,2,1,0:T(8,128)S(1)}, u32[]{:S(2)}, u32[]{:S(2)}) async-start(f32[16,2,8,128]{3,2,1,0:T(8,128)} %broadcast_in_dim.8), calls=%async_computation.2 | async-start | bytes 262144 | tf_op jit(solution)/shard_map/all_to_all | solution.py:483
  68.8 0.0 collective-permute-done.17.fylo_ref
  68.8 0.8 copy-done.12
  69.6 0.7 pad_maximum_fusion.2
  70.3 3.4 %collective-permute-start.19 = (f32[2,12,8,128]{3,2,1,0:T(8,128)}, f32[2,12,8,128]{3,2,1,0:T(8,128)}, u32[]{:S(2)}, u32[]{:S(2)}) collective-permute-start(f32[2,12,8,128]{3,2,1,0:T(8,128)} %pad_maximum_fusion.2), channel_id=1, source_target_pairs={{0,8},{8,16},{16,24},{24,32},{32,40},{40,48},{48,56},{56,64},{64,7... | collective-permute-start | bytes 294920 | tf_op jit(solution)/shard_map/ppermute | solution.py:428
  73.7 0.0 collective-permute-start.14
  73.7 0.6 pad_maximum_fusion.3
  74.3 2.3 %collective-permute-start.20 = (f32[2,12,8,128]{3,2,1,0:T(8,128)}, f32[2,12,8,128]{3,2,1,0:T(8,128)}, u32[]{:S(2)}, u32[]{:S(2)}) collective-permute-start(f32[2,12,8,128]{3,2,1,0:T(8,128)} %pad_maximum_fusion.3), channel_id=1, source_target_pairs={{0,248},{8,0},{16,8},{24,16},{32,24},{40,32},{48,40},{56,48},{64,5... | collective-permute-start | bytes 294920 | tf_op jit(solution)/shard_map/ppermute | solution.py:428
  76.6 0.1 collective-permute-start.13
  76.8 3.0 %collective-permute-start.15 = (f32[2,16,128]{2,1,0:T(8,128)}, f32[2,16,128]{2,1,0:T(8,128)S(1)}, u32[]{:S(2)}, u32[]{:S(2)}) collective-permute-start(f32[2,16,128]{2,1,0:T(8,128)} %get-tuple-element.44), channel_id=1, source_target_pairs={{0,16},{8,248},{16,32},{24,8},{32,48},{40,24},{48,64},{56,40},{64,... | collective-permute-start | bytes 49160 | tf_op jit(solution)/shard_map/ppermute | solution.py:440
  79.8 0.8 collective-permute-done.14.outer2
  80.6 0.4 collective-permute-start.12
  81.0 0.0 collective-permute-done.19.fxlo_ref
  81.0 0.2 collective-permute-start.16
  81.2 0.5 collective-permute-done.20.fxhi_ref
  81.7 0.6 collective-permute-done.16.far2
  82.3 0.0 collective-permute-done.12.other3
  82.3 0.6 copy-done.7
  82.9 0.9 %copy-done.1 = f32[8,8,8,128]{3,2,1,0:T(8,128)S(1)} copy-done((f32[8,8,8,128]{3,2,1,0:T(8,128)S(1)}, f32[8,8,8,128]{3,2,1,0:T(8,128)}, u32[]{:S(2)}) %copy-start.1) | copy-done | bytes 262168
  83.9 5.5 %shard_map.45 = (f32[8,8,1024]{2,1,0:T(8,128)}, f32[8,8,1024]{2,1,0:T(8,128)}) custom-call(s32[2]{0:T(128)S(1)} %copy-done.7, f32[16,2,8,128]{3,2,1,0:T(8,128)S(1)} %all-to-all-done.2.mine3, f32[16,2,8,128]{3,2,1,0:T(8,128)S(1)} %collective-permute-done.12.other3, f32[2,2,2,16,128]{4,3,2,1,0:T(8,128)} %get-tuple-element.43.fs2, ...), custom_call_target="tpu_custom_call" | custom-call | tf_op jit(solution)/shard_map/pallas_call | solution.py:418
  (38 shorter events, 0.2 us)
Async XLA Ops:
  0.6 1.0 %copy-start.2 = (f32[8,8,1024]{2,1,0:T(8,128)S(1)}, f32[8,8,1024]{2,1,0:T(8,128)}, u32[]{:S(2)}) copy-start(f32[8,8,1024]{2,1,0:T(8,128)} %cot_ref.1) | copy-start | bytes 786436
  1.6 0.9 %copy-start.3 = (f32[8,8,1024]{2,1,0:T(8,128)S(1)}, f32[8,8,1024]{2,1,0:T(8,128)}, u32[]{:S(2)}) copy-start(f32[8,8,1024]{2,1,0:T(8,128)} %diag_ref.1) | copy-start | bytes 786436
  3.0 8.8 %collective-permute-start = (f32[2,8,2,8,128]{4,3,2,1,0:T(8,128)S(1)}, f32[2,8,2,8,128]{4,3,2,1,0:T(8,128)S(1)}, u32[]{:S(2)}, u32[]{:S(2)}) collective-permute-start(f32[2,8,2,8,128]{4,3,2,1,0:T(8,128)S(1)} %get-tuple-element.29), channel_id=1, source_target_pairs={{0,1},{1,2},{2,3},{3,4},{4,5},{5,6},{6,7},{7,0},{8,9},{9,10},{10,1... | collective-permute-start | bytes 393224 | tf_op jit(solution)/shard_map/ppermute | solution.py:428
  5.2 6.6 %collective-permute-start.1 = (f32[2,8,2,8,128]{4,3,2,1,0:T(8,128)S(1)}, f32[2,8,2,8,128]{4,3,2,1,0:T(8,128)S(1)}, u32[]{:S(2)}, u32[]{:S(2)}) collective-permute-start(f32[2,8,2,8,128]{4,3,2,1,0:T(8,128)S(1)} %get-tuple-element.30), channel_id=1, source_target_pairs={{0,7},{1,0},{2,1},{3,2},{4,3},{5,4},{6,5},{7,6},{8,15},{9,8},{10,9... | collective-permute-start | bytes 393224 | tf_op jit(solution)/shard_map/ppermute | solution.py:428
  8.3 9.1 %all-to-all-start.1 = ((f32[8,4,4,4,128]{4,3,2,1,0:T(4,128)}), f32[8,4,4,4,128]{4,3,2,1,0:T(4,128)S(1)}, u32[]{:S(2)}, u32[]{:S(2)}) async-start(f32[8,4,4,4,128]{4,3,2,1,0:T(4,128)} %broadcast_in_dim.7), calls=%async_computation.1 | async-start | bytes 524288 | tf_op jit(solution)/shard_map/all_to_all | solution.py:444
  11.8 48.3 %copy-start.6 = (s32[2]{0:T(128)}, s32[2]{0:T(128)S(1)}, u32[]{:S(2)}) copy-start(s32[2]{0:T(128)S(1)} %pad_add_fusion.index_ref) | copy-start | bytes 28
  11.9 17.7 %collective-permute-start.2 = (f32[2,2,12,8,128]{4,3,2,1,0:T(8,128)S(1)}, f32[2,2,12,8,128]{4,3,2,1,0:T(8,128)S(1)}, u32[]{:S(2)}, u32[]{:S(2)}) collective-permute-start(f32[2,2,12,8,128]{4,3,2,1,0:T(8,128)S(1)} %pad_maximum_fusion), channel_id=1, source_target_pairs={{0,8},{8,16},{16,24},{24,32},{32,40},{40,48},{48,56},{56,64},{64,7... | collective-permute-start | bytes 589832 | tf_op jit(solution)/shard_map/ppermute | solution.py:428
  16.6 12.9 %collective-permute-start.3 = (f32[2,2,12,8,128]{4,3,2,1,0:T(8,128)S(1)}, f32[2,2,12,8,128]{4,3,2,1,0:T(8,128)S(1)}, u32[]{:S(2)}, u32[]{:S(2)}) collective-permute-start(f32[2,2,12,8,128]{4,3,2,1,0:T(8,128)S(1)} %pad_maximum_fusion.1), channel_id=1, source_target_pairs={{0,248},{8,0},{16,8},{24,16},{32,24},{40,32},{48,40},{56,48},{64,5... | collective-permute-start | bytes 589832 | tf_op jit(solution)/shard_map/ppermute | solution.py:428
  17.4 22.5 %collective-permute-start.8 = (f32[8,4,4,4,128]{4,3,2,1,0:T(4,128)S(1)}, f32[8,4,4,4,128]{4,3,2,1,0:T(4,128)S(1)}, u32[]{:S(2)}, u32[]{:S(2)}) collective-permute-start(f32[8,4,4,4,128]{4,3,2,1,0:T(4,128)S(1)} %all-to-all-done.1.own), channel_id=1, source_target_pairs={{0,8},{8,0},{16,24},{24,16},{32,40},{40,32},{48,56},{56,48},{64,72... | collective-permute-start | bytes 786440 | tf_op jit(solution)/shard_map/ppermute | solution.py:432
  21.5 18.4 %collective-permute-start.9 = (f32[8,4,4,4,128]{4,3,2,1,0:T(4,128)S(1)}, f32[8,4,4,4,128]{4,3,2,1,0:T(4,128)S(1)}, u32[]{:S(2)}, u32[]{:S(2)}) collective-permute-start(f32[8,4,4,4,128]{4,3,2,1,0:T(4,128)S(1)} %all-to-all-done.1.own), channel_id=1, source_target_pairs={{0,248},{8,16},{16,8},{24,32},{32,24},{40,48},{48,40},{56,64},{64,... | collective-permute-start | bytes 786440 | tf_op jit(solution)/shard_map/ppermute | solution.py:436
  23.3 16.6 %collective-permute-start.10 = (f32[8,2,4,4,128]{4,3,2,1,0:T(4,128)}, f32[8,2,4,4,128]{4,3,2,1,0:T(4,128)}, u32[]{:S(2)}, u32[]{:S(2)}) collective-permute-start(f32[8,2,4,4,128]{4,3,2,1,0:T(4,128)} %slice_select_fusion), channel_id=1, source_target_pairs={{0,16},{8,248},{16,32},{24,8},{32,48},{40,24},{48,64},{56,40},{64,... | collective-permute-start | bytes 393224 | tf_op jit(solution)/shard_map/ppermute | solution.py:440
  30.6 0.6 copy-start.9
  31.2 0.8 copy-start
  31.2 0.8 copy-start.8
  32.0 4.9 %copy-start.10 = (f32[8,2,8,128]{3,2,1,0:T(8,128)S(1)}, f32[8,2,8,128]{3,2,1,0:T(8,128)}, u32[]{:S(2)}) copy-start(f32[8,2,8,128]{3,2,1,0:T(8,128)} %copy-done.9) | copy-start | bytes 196612
  32.0 9.9 %all-to-all-start = ((f32[8,4,4,4,128]{4,3,2,1,0:T(4,128)}), f32[8,4,4,4,128]{4,3,2,1,0:T(4,128)S(1)}, u32[]{:S(2)}, u32[]{:S(2)}) async-start(f32[8,4,4,4,128]{4,3,2,1,0:T(4,128)} %broadcast_in_dim.6), calls=%async_computation | async-start | bytes 524288 | tf_op jit(solution)/shard_map/all_to_all | solution.py:444
  35.6 33.2 %collective-permute-start.17 = (f32[8,2,8,128]{3,2,1,0:T(8,128)}, f32[8,2,8,128]{3,2,1,0:T(8,128)S(1)}, u32[]{:S(2)}, u32[]{:S(2)}) collective-permute-start(f32[8,2,8,128]{3,2,1,0:T(8,128)} %copy-done.8), channel_id=1, source_target_pairs={{0,1},{1,2},{2,3},{3,4},{4,5},{5,6},{6,7},{7,0},{8,9},{9,10},{10,1... | collective-permute-start | bytes 196616 | tf_op jit(solution)/shard_map/ppermute | solution.py:428
  36.9 21.1 %collective-permute-start.18 = (f32[8,2,8,128]{3,2,1,0:T(8,128)S(1)}, f32[8,2,8,128]{3,2,1,0:T(8,128)S(1)}, u32[]{:S(2)}, u32[]{:S(2)}) collective-permute-start(f32[8,2,8,128]{3,2,1,0:T(8,128)S(1)} %copy-done.10), channel_id=1, source_target_pairs={{0,7},{1,0},{2,1},{3,2},{4,3},{5,4},{6,5},{7,6},{8,15},{9,8},{10,9... | collective-permute-start | bytes 196616 | tf_op jit(solution)/shard_map/ppermute | solution.py:428
  41.9 15.7 %collective-permute-start.4 = (f32[8,4,4,4,128]{4,3,2,1,0:T(4,128)S(1)}, f32[8,4,4,4,128]{4,3,2,1,0:T(4,128)S(1)}, u32[]{:S(2)}, u32[]{:S(2)}) collective-permute-start(f32[8,4,4,4,128]{4,3,2,1,0:T(4,128)S(1)} %all-to-all-done.own), channel_id=1, source_target_pairs={{0,8},{8,0},{16,24},{24,16},{32,40},{40,32},{48,56},{56,48},{64,72... | collective-permute-start | bytes 786440 | tf_op jit(solution)/shard_map/ppermute | solution.py:432
  43.9 13.8 %collective-permute-start.5 = (f32[8,4,4,4,128]{4,3,2,1,0:T(4,128)S(1)}, f32[8,4,4,4,128]{4,3,2,1,0:T(4,128)S(1)}, u32[]{:S(2)}, u32[]{:S(2)}) collective-permute-start(f32[8,4,4,4,128]{4,3,2,1,0:T(4,128)S(1)} %all-to-all-done.own), channel_id=1, source_target_pairs={{0,248},{8,16},{16,8},{24,32},{32,24},{40,48},{48,40},{56,64},{64,... | collective-permute-start | bytes 786440 | tf_op jit(solution)/shard_map/ppermute | solution.py:436
  44.0 9.2 %collective-permute-start.6 = (f32[8,2,4,4,128]{4,3,2,1,0:T(4,128)S(1)}, f32[8,2,4,4,128]{4,3,2,1,0:T(4,128)S(1)}, u32[]{:S(2)}, u32[]{:S(2)}) collective-permute-start(f32[8,2,4,4,128]{4,3,2,1,0:T(4,128)S(1)} %slice_select_fusion.1), channel_id=1, source_target_pairs={{0,16},{8,248},{16,32},{24,8},{32,48},{40,24},{48,64},{56,40},{64,... | collective-permute-start | bytes 393224 | tf_op jit(solution)/shard_map/ppermute | solution.py:440
  53.2 5.5 %collective-permute-start.11 = (f32[8,2,4,4,128]{4,3,2,1,0:T(4,128)S(1)}, f32[8,2,4,4,128]{4,3,2,1,0:T(4,128)S(1)}, u32[]{:S(2)}, u32[]{:S(2)}) collective-permute-start(f32[8,2,4,4,128]{4,3,2,1,0:T(4,128)S(1)} %slice_select_fusion.2), channel_id=1, source_target_pairs={{0,8},{8,0},{16,24},{24,16},{32,40},{40,32},{48,56},{56,48},{64,72... | collective-permute-start | bytes 393224 | tf_op jit(solution)/shard_map/ppermute | solution.py:432
  57.7 2.4 %collective-permute-start.7 = (f32[8,2,4,4,128]{4,3,2,1,0:T(4,128)S(1)}, f32[8,2,4,4,128]{4,3,2,1,0:T(4,128)S(1)}, u32[]{:S(2)}, u32[]{:S(2)}) collective-permute-start(f32[8,2,4,4,128]{4,3,2,1,0:T(4,128)S(1)} %slice_select_fusion.3), channel_id=1, source_target_pairs={{0,8},{8,0},{16,24},{24,16},{32,40},{40,32},{48,56},{56,48},{64,72... | collective-permute-start | bytes 393224 | tf_op jit(solution)/shard_map/ppermute | solution.py:432
  58.0 2.1 %copy-start.4 = (f32[8,2,8,128]{3,2,1,0:T(8,128)}, f32[8,2,8,128]{3,2,1,0:T(8,128)S(1)}, u32[]{:S(2)}) copy-start(f32[8,2,8,128]{3,2,1,0:T(8,128)S(1)} %collective-permute-done.18.fyhi_ref) | copy-start | bytes 196612
  63.4 5.4 %copy-start.14 = (f32[2,2,8,128]{3,2,1,0:T(8,128)S(1)}, f32[2,2,8,128]{3,2,1,0:T(8,128)}, u32[]{:S(2)}) copy-start(f32[2,2,8,128]{3,2,1,0:T(8,128)} %get-tuple-element.63) | copy-start | bytes 49156
  63.4 17.2 %all-to-all-start.2 = ((f32[16,2,8,128]{3,2,1,0:T(8,128)}), f32[16,2,8,128]{3,2,1,0:T(8,128)S(1)}, u32[]{:S(2)}, u32[]{:S(2)}) async-start(f32[16,2,8,128]{3,2,1,0:T(8,128)} %broadcast_in_dim.8), calls=%async_computation.2 | async-start | bytes 262144 | tf_op jit(solution)/shard_map/all_to_all | solution.py:483
  68.8 0.8 copy-start.12
  69.6 4.1 %copy-start.11 = (f32[2,8,8,128]{3,2,1,0:T(8,128)S(1)}, f32[2,8,8,128]{3,2,1,0:T(8,128)}, u32[]{:S(2)}) copy-start(f32[2,8,8,128]{3,2,1,0:T(8,128)} %get-tuple-element.54) | copy-start | bytes 196612
  69.6 4.1 %copy-start.13 = (f32[2,2,8,128]{3,2,1,0:T(8,128)S(1)}, f32[2,2,8,128]{3,2,1,0:T(8,128)}, u32[]{:S(2)}) copy-start(f32[2,2,8,128]{3,2,1,0:T(8,128)} %get-tuple-element.62) | copy-start | bytes 49156
  70.3 10.8 %collective-permute-start.19 = (f32[2,12,8,128]{3,2,1,0:T(8,128)}, f32[2,12,8,128]{3,2,1,0:T(8,128)}, u32[]{:S(2)}, u32[]{:S(2)}) collective-permute-start(f32[2,12,8,128]{3,2,1,0:T(8,128)} %pad_maximum_fusion.2), channel_id=1, source_target_pairs={{0,8},{8,16},{16,24},{24,32},{32,40},{40,48},{48,56},{56,64},{64,7... | collective-permute-start | bytes 294920 | tf_op jit(solution)/shard_map/ppermute | solution.py:428
  73.7 7.0 %collective-permute-start.14 = (f32[2,2,2,16,128]{4,3,2,1,0:T(8,128)}, f32[2,2,2,16,128]{4,3,2,1,0:T(8,128)S(1)}, u32[]{:S(2)}, u32[]{:S(2)}) collective-permute-start(f32[2,2,2,16,128]{4,3,2,1,0:T(8,128)} %get-tuple-element.43.fs2), channel_id=1, source_target_pairs={{0,248},{8,16},{16,8},{24,32},{32,24},{40,48},{48,40},{56,64},{64,... | collective-permute-start | bytes 196616 | tf_op jit(solution)/shard_map/ppermute | solution.py:436
  73.7 8.6 %copy-start.5 = (f32[8,2,8,128]{3,2,1,0:T(8,128)S(1)}, f32[8,2,8,128]{3,2,1,0:T(8,128)}, u32[]{:S(2)}) copy-start(f32[8,2,8,128]{3,2,1,0:T(8,128)} %copy-done.4) | copy-start | bytes 196612
  74.3 7.4 %collective-permute-start.20 = (f32[2,12,8,128]{3,2,1,0:T(8,128)}, f32[2,12,8,128]{3,2,1,0:T(8,128)}, u32[]{:S(2)}, u32[]{:S(2)}) collective-permute-start(f32[2,12,8,128]{3,2,1,0:T(8,128)} %pad_maximum_fusion.3), channel_id=1, source_target_pairs={{0,248},{8,0},{16,8},{24,16},{32,24},{40,32},{48,40},{56,48},{64,5... | collective-permute-start | bytes 294920 | tf_op jit(solution)/shard_map/ppermute | solution.py:428
  76.6 5.1 %collective-permute-start.13 = (f32[2,2,2,16,128]{4,3,2,1,0:T(8,128)}, f32[2,2,2,16,128]{4,3,2,1,0:T(8,128)}, u32[]{:S(2)}, u32[]{:S(2)}) collective-permute-start(f32[2,2,2,16,128]{4,3,2,1,0:T(8,128)} %get-tuple-element.43.fs2), channel_id=1, source_target_pairs={{0,8},{8,0},{16,24},{24,16},{32,40},{40,32},{48,56},{56,48},{64,72... | collective-permute-start | bytes 196616 | tf_op jit(solution)/shard_map/ppermute | solution.py:432
  76.8 4.9 %collective-permute-start.15 = (f32[2,16,128]{2,1,0:T(8,128)}, f32[2,16,128]{2,1,0:T(8,128)S(1)}, u32[]{:S(2)}, u32[]{:S(2)}) collective-permute-start(f32[2,16,128]{2,1,0:T(8,128)} %get-tuple-element.44), channel_id=1, source_target_pairs={{0,16},{8,248},{16,32},{24,8},{32,48},{40,24},{48,64},{56,40},{64,... | collective-permute-start | bytes 49160 | tf_op jit(solution)/shard_map/ppermute | solution.py:440
  80.6 1.7 %collective-permute-start.12 = (f32[16,2,8,128]{3,2,1,0:T(8,128)S(1)}, f32[16,2,8,128]{3,2,1,0:T(8,128)S(1)}, u32[]{:S(2)}, u32[]{:S(2)}) collective-permute-start(f32[16,2,8,128]{3,2,1,0:T(8,128)S(1)} %all-to-all-done.2.mine3), channel_id=1, source_target_pairs={{0,8},{8,0},{16,24},{24,16},{32,40},{40,32},{48,56},{56,48},{64,72... | collective-permute-start | bytes 393224 | tf_op jit(solution)/shard_map/ppermute | solution.py:432
  81.0 1.3 %collective-permute-start.16 = (f32[2,16,128]{2,1,0:T(8,128)S(1)}, f32[2,16,128]{2,1,0:T(8,128)S(1)}, u32[]{:S(2)}, u32[]{:S(2)}) collective-permute-start(f32[2,16,128]{2,1,0:T(8,128)S(1)} %fusion), channel_id=1, source_target_pairs={{0,8},{8,0},{16,24},{24,16},{32,40},{40,32},{48,56},{56,48},{64,72... | collective-permute-start | bytes 49160 | tf_op jit(solution)/shard_map/ppermute | solution.py:432
  82.3 0.6 copy-start.7
  82.9 0.9 %copy-start.1 = (f32[8,8,8,128]{3,2,1,0:T(8,128)S(1)}, f32[8,8,8,128]{3,2,1,0:T(8,128)}, u32[]{:S(2)}) copy-start(f32[8,8,8,128]{3,2,1,0:T(8,128)} %copy-done) | copy-start | bytes 786436

commit v4 on v3

--- a/solution.py
+++ b/solution.py
@@ -135,7 +135,7 @@
         s1[x, 1:11] = THIRD * s0[x, 1:11] + gext_ref[x, 1:11] * total
         return carry
 
-    lax.fori_loop(1, 11, first, 0, unroll=4)
+    lax.fori_loop(1, 11, first, 0, unroll=8)
 
     def second(x, carry):
         f1 = THIRD * f_ref[x - 2] + fine_neighbours(s0, x, 2, 10)
@@ -143,7 +143,7 @@
         src_ref[x - 2] = s0[x, 2:10] + s1[x, 2:10]
         return carry
 
-    lax.fori_loop(2, 10, second, 0, unroll=4)
+    lax.fori_loop(2, 10, second, 0, unroll=8)
     fylo_ref[...] = f2_ref[:, 0:2]
     fyhi_ref[...] = f2_ref[:, 6:8]
     block_pairs(f2_ref, pairs)
@@ -206,7 +206,7 @@
         g1_ref[x] = OMEGA / (6.0 + 4.0 * field[x])
         return carry
 
-    lax.fori_loop(0, 16, scale1, 0, unroll=4)
+    lax.fori_loop(0, 16, scale1, 0, unroll=8)
     for x in range(8):
         c2[x] = restrict_middle(field, 2 * x, pairs, 0.125)
         g2_ref[x] = OMEGA / (6.0 + 16.0 * c2[x])
@@ -234,7 +234,7 @@
         s0[x] = g1_ref[x] * rhs[x]
         return carry
 
-    lax.fori_loop(0, 16, start, 0, unroll=4)
+    lax.fori_loop(0, 16, start, 0, unroll=8)
 
     def first(x, carry):
         total = coarse_neighbours(s0, x)
@@ -242,13 +242,13 @@
         rhs[x] = THIRD * rhs[x] + total
         return carry
 
-    lax.fori_loop(1, 15, first, 0, unroll=4)
+    lax.fori_loop(1, 15, first, 0, unroll=8)
 
     def second(x, carry):
         f2[x - 2] = THIRD * rhs[x] + coarse_neighbours(s1, x)
         return carry
 
-    lax.fori_loop(2, 14, second, 0, unroll=4)
+    lax.fori_loop(2, 14, second, 0, unroll=8)
     f1_ref[...] = f2[1:11]
     src1_ref[...] = s0[4:12] + s1[4:12]
 
@@ -349,7 +349,7 @@
         sa1[x] = g * (f1_ref[x - 1] - (OMEGA / g) * r1[x] + coarse_neighbours(r1, x))
         return carry
 
-    lax.fori_loop(1, 11, middle1, 0, unroll=4)
+    lax.fori_loop(1, 11, middle1, 0, unroll=8)
 
     def last1(x, carry):
         sb = THIRD * sa1[x] + g1_ref[x + 2] * coarse_neighbours(sa1, x)
@@ -358,7 +358,7 @@
             out1[x - 2, pl.ds(32 * c, 32), :] = row[c]
         return carry
 
-    lax.fori_loop(2, 10, last1, 0, unroll=4)
+    lax.fori_loop(2, 10, last1, 0, unroll=8)
 
     def spread0(x, carry):
         for y in range(8):
@@ -369,7 +369,7 @@
                         r0[2 * x + p, 2 * y + q, pl.ds(c, 4, stride=2), :] = row
         return carry
 
-    lax.fori_loop(0, 8, spread0, 0, unroll=4)
+    lax.fori_loop(0, 8, spread0, 0, unroll=8)
     f0[2:10, 2:10] = f0_ref[...]
     f0[2:10, 0:2] = fylo_ref[...]
     f0[2:10, 10:12] = fyhi_ref[...]
@@ -383,13 +383,13 @@
         s3[x] = g * f
         return carry
 
-    lax.fori_loop(0, 12, residual0, 0, unroll=4)
+    lax.fori_loop(0, 12, residual0, 0, unroll=8)
 
     def first0(x, carry):
         s4[x, 1:11] = THIRD * s3[x, 1:11] + g0_ref[x, 1:11] * fine_neighbours(s3, x, 1, 11)
         return carry
 
-    lax.fori_loop(1, 11, first0, 0, unroll=4)
+    lax.fori_loop(1, 11, first0, 0, unroll=8)
 
     def second0(x, carry):
         f4 = THIRD * f0[x, 2:10] + fine_neighbours(s3, x, 2, 10)
@@ -399,7 +399,7 @@
         placed[pl.ds(64 * (x - 2) + 512, 64), :] = source.reshape(64, 128)
         return carry
 
-    lax.fori_loop(2, 10, second0, 0, unroll=4)
+    lax.fori_loop(2, 10, second0, 0, unroll=8)
     for c in range(8):
         turned[pl.ds(c, 128, stride=8), :] = placed[pl.ds(c, 128, stride=8), :].T
     result = turned[...].T

time: 90.8 us -> 90.7 us (level)
  no operation moved by 1% of the time
where the time goes in v4:
time: 90.7 us; the launch traced here: 89.4 us
  starting transfers between devices  57.9 us (64%)
  Pallas kernels  11.1 us (12%)
  waiting for transfers between devices  8.83 us (10%)
  local copies, waits for them, and re-layouts  8.45 us (9%)
  other arithmetic  2.21 us (2%)
    ppermute x8, starting transfers between devices, shifted(): lax.ppermute(v, axis, [(i, (i + step) % count) for i in range(count)])  18.6 us
    ppermute x3, starting transfers between devices, skip_chip(): lax.ppermute(v, 'gx', [(i, (i - 2 if i % 2 else i + 2) % GX) for i in ran...  14.4 us
    ppermute x7, starting transfers between devices, swap_core(): return lax.ppermute(v, 'gx', [(i, i ^ 1) for i in range(GX)])  11.6 us
    all_to_all x2, starting transfers between devices, gather_y(): lax.all_to_all(jnp.broadcast_to(v[None], (GY,) + v.shape), 'gy', 0, 0)  6.96 us
    pallas_call x1, Pallas kernels, up(): pl.pallas_call(up_kernel, out_shape=(shape(8, 8, 1024), shape(8, 8, 1024)...  5.33 us
    all_to_all x1, starting transfers between devices, per_device(): lax.all_to_all(jnp.broadcast_to(both3[None], (16,) + both3.shape), 'gx',...  5.31 us
    unnamed x30, local copies, waits for them, and re-layouts  4.91 us
    ppermute x3, waiting for transfers between devices, skip_chip(): lax.ppermute(v, 'gx', [(i, (i - 2 if i % 2 else i + 2) % GX) for i in ran...  4.16 us
  transfers between devices with their start and end apart: 24, of which 6 were waited for; matrix products, arithmetic and copies ran while one was open for 6% of the time, Pallas kernels for 6%

profile of v4, /device:TPU:1, one launch (start us, length us, event | category | flops | bytes accessed | tf_op | source)
XLA Modules:
  0.0 89.4 jit_solution(4494268797002592094)
XLA Ops:
  0.6 0.9 %copy-done.2 = f32[8,8,1024]{2,1,0:T(8,128)S(1)} copy-done((f32[8,8,1024]{2,1,0:T(8,128)S(1)}, f32[8,8,1024]{2,1,0:T(8,128)}, u32[]{:S(2)}) %copy-start.2) | copy-done | bytes 262168
  1.6 0.9 %copy-done.3 = f32[8,8,1024]{2,1,0:T(8,128)S(1)} copy-done((f32[8,8,1024]{2,1,0:T(8,128)S(1)}, f32[8,8,1024]{2,1,0:T(8,128)}, u32[]{:S(2)}) %copy-start.3) | copy-done | bytes 262168
  2.5 0.5 shard_map.41
  3.0 2.2 %collective-permute-start = (f32[2,8,2,8,128]{4,3,2,1,0:T(8,128)S(1)}, f32[2,8,2,8,128]{4,3,2,1,0:T(8,128)S(1)}, u32[]{:S(2)}, u32[]{:S(2)}) collective-permute-start(f32[2,8,2,8,128]{4,3,2,1,0:T(8,128)S(1)} %get-tuple-element.29), channel_id=1, source_target_pairs={{0,1},{1,2},{2,3},{3,4},{4,5},{5,6},{6,7},{7,0},{8,9},{9,10},{10,1... | collective-permute-start | bytes 393224 | tf_op jit(solution)/shard_map/ppermute | solution.py:428
  5.2 2.3 %collective-permute-start.1 = (f32[2,8,2,8,128]{4,3,2,1,0:T(8,128)S(1)}, f32[2,8,2,8,128]{4,3,2,1,0:T(8,128)S(1)}, u32[]{:S(2)}, u32[]{:S(2)}) collective-permute-start(f32[2,8,2,8,128]{4,3,2,1,0:T(8,128)S(1)} %get-tuple-element.30), channel_id=1, source_target_pairs={{0,7},{1,0},{2,1},{3,2},{4,3},{5,4},{6,5},{7,6},{8,15},{9,8},{10,9... | collective-permute-start | bytes 393224 | tf_op jit(solution)/shard_map/ppermute | solution.py:428
  7.5 0.7 broadcast_in_dim.7
  8.3 3.4 %all-to-all-start.1 = ((f32[8,4,4,4,128]{4,3,2,1,0:T(4,128)}), f32[8,4,4,4,128]{4,3,2,1,0:T(4,128)S(1)}, u32[]{:S(2)}, u32[]{:S(2)}) async-start(f32[8,4,4,4,128]{4,3,2,1,0:T(4,128)} %broadcast_in_dim.7), calls=%async_computation.1 | async-start | bytes 524288 | tf_op jit(solution)/shard_map/all_to_all | solution.py:444
  11.7 0.1 pad_add_fusion.index_ref
  11.8 0.0 collective-permute-done.1.yhi_ref
  11.8 0.0 collective-permute-done.ylo_ref
  11.9 4.7 %collective-permute-start.2 = (f32[2,2,12,8,128]{4,3,2,1,0:T(8,128)S(1)}, f32[2,2,12,8,128]{4,3,2,1,0:T(8,128)S(1)}, u32[]{:S(2)}, u32[]{:S(2)}) collective-permute-start(f32[2,2,12,8,128]{4,3,2,1,0:T(8,128)S(1)} %pad_maximum_fusion), channel_id=1, source_target_pairs={{0,8},{8,16},{16,24},{24,32},{32,40},{40,48},{48,56},{56,64},{64,7... | collective-permute-start | bytes 589832 | tf_op jit(solution)/shard_map/ppermute | solution.py:428
  16.6 0.1 collective-permute-start.3
  16.7 0.7 all-to-all-done.1.own
  17.4 4.1 %collective-permute-start.8 = (f32[8,4,4,4,128]{4,3,2,1,0:T(4,128)S(1)}, f32[8,4,4,4,128]{4,3,2,1,0:T(4,128)S(1)}, u32[]{:S(2)}, u32[]{:S(2)}) collective-permute-start(f32[8,4,4,4,128]{4,3,2,1,0:T(4,128)S(1)} %all-to-all-done.1.own), channel_id=1, source_target_pairs={{0,8},{8,0},{16,24},{24,16},{32,40},{40,32},{48,56},{56,48},{64,72... | collective-permute-start | bytes 786440 | tf_op jit(solution)/shard_map/ppermute | solution.py:432
  21.5 1.1 %collective-permute-start.9 = (f32[8,4,4,4,128]{4,3,2,1,0:T(4,128)S(1)}, f32[8,4,4,4,128]{4,3,2,1,0:T(4,128)S(1)}, u32[]{:S(2)}, u32[]{:S(2)}) collective-permute-start(f32[8,4,4,4,128]{4,3,2,1,0:T(4,128)S(1)} %all-to-all-done.1.own), channel_id=1, source_target_pairs={{0,248},{8,16},{16,8},{24,32},{32,24},{40,48},{48,40},{56,64},{64,... | collective-permute-start | bytes 786440 | tf_op jit(solution)/shard_map/ppermute | solution.py:436
  22.6 0.7 slice_select_fusion
  23.3 6.3 %collective-permute-start.10 = (f32[8,2,4,4,128]{4,3,2,1,0:T(4,128)}, f32[8,2,4,4,128]{4,3,2,1,0:T(4,128)}, u32[]{:S(2)}, u32[]{:S(2)}) collective-permute-start(f32[8,2,4,4,128]{4,3,2,1,0:T(4,128)} %slice_select_fusion), channel_id=1, source_target_pairs={{0,16},{8,248},{16,32},{24,8},{32,48},{40,24},{48,64},{56,40},{64,... | collective-permute-start | bytes 393224 | tf_op jit(solution)/shard_map/ppermute | solution.py:440
  29.5 0.0 collective-permute-done.2.xlo_ref
  29.5 0.0 collective-permute-done.3.xhi_ref
  29.5 0.8 shard_map.42
  30.4 0.6 copy-done.9
  31.0 0.8 broadcast_in_dim.6
  31.8 3.5 %all-to-all-start = ((f32[8,4,4,4,128]{4,3,2,1,0:T(4,128)}), f32[8,4,4,4,128]{4,3,2,1,0:T(4,128)S(1)}, u32[]{:S(2)}, u32[]{:S(2)}) async-start(f32[8,4,4,4,128]{4,3,2,1,0:T(4,128)} %broadcast_in_dim.6), calls=%async_computation | async-start | bytes 524288 | tf_op jit(solution)/shard_map/all_to_all | solution.py:444
  35.4 1.4 %collective-permute-start.17 = (f32[8,2,8,128]{3,2,1,0:T(8,128)}, f32[8,2,8,128]{3,2,1,0:T(8,128)S(1)}, u32[]{:S(2)}, u32[]{:S(2)}) collective-permute-start(f32[8,2,8,128]{3,2,1,0:T(8,128)} %copy-done.8), channel_id=1, source_target_pairs={{0,1},{1,2},{2,3},{3,4},{4,5},{5,6},{6,7},{7,0},{8,9},{9,10},{10,1... | collective-permute-start | bytes 196616 | tf_op jit(solution)/shard_map/ppermute | solution.py:428
  36.7 2.3 %collective-permute-start.18 = (f32[8,2,8,128]{3,2,1,0:T(8,128)S(1)}, f32[8,2,8,128]{3,2,1,0:T(8,128)S(1)}, u32[]{:S(2)}, u32[]{:S(2)}) collective-permute-start(f32[8,2,8,128]{3,2,1,0:T(8,128)S(1)} %copy-done.10), channel_id=1, source_target_pairs={{0,7},{1,0},{2,1},{3,2},{4,3},{5,4},{6,5},{7,6},{8,15},{9,8},{10,9... | collective-permute-start | bytes 196616 | tf_op jit(solution)/shard_map/ppermute | solution.py:428
  39.0 0.7 fusion.2
  39.7 0.0 collective-permute-done.10.skip
  39.7 0.0 collective-permute-done.8.pair
  39.7 0.0 collective-permute-done.9.outer
  39.7 2.0 %all-to-all-done.own = f32[8,4,4,4,128]{4,3,2,1,0:T(4,128)S(1)} async-done(((f32[8,4,4,4,128]{4,3,2,1,0:T(4,128)}), f32[8,4,4,4,128]{4,3,2,1,0:T(4,128)S(1)}, u32[]{:S(2)}, u32[]{:S(2)}) %all-to-all-start) | async-done | bytes 262176 | tf_op jit(solution)/shard_map/all_to_all | solution.py:444
  41.8 2.0 %collective-permute-start.4 = (f32[8,4,4,4,128]{4,3,2,1,0:T(4,128)S(1)}, f32[8,4,4,4,128]{4,3,2,1,0:T(4,128)S(1)}, u32[]{:S(2)}, u32[]{:S(2)}) collective-permute-start(f32[8,4,4,4,128]{4,3,2,1,0:T(4,128)S(1)} %all-to-all-done.own), channel_id=1, source_target_pairs={{0,8},{8,0},{16,24},{24,16},{32,40},{40,32},{48,56},{56,48},{64,72... | collective-permute-start | bytes 786440 | tf_op jit(solution)/shard_map/ppermute | solution.py:432
  43.7 0.0 collective-permute-start.5
  43.8 5.0 %collective-permute-start.6 = (f32[8,2,4,4,128]{4,3,2,1,0:T(4,128)S(1)}, f32[8,2,4,4,128]{4,3,2,1,0:T(4,128)S(1)}, u32[]{:S(2)}, u32[]{:S(2)}) collective-permute-start(f32[8,2,4,4,128]{4,3,2,1,0:T(4,128)S(1)} %slice_select_fusion.1), channel_id=1, source_target_pairs={{0,16},{8,248},{16,32},{24,8},{32,48},{40,24},{48,64},{56,40},{64,... | collective-permute-start | bytes 393224 | tf_op jit(solution)/shard_map/ppermute | solution.py:440
  48.9 4.2 %collective-permute-done.6.skip = f32[8,2,4,4,128]{4,3,2,1,0:T(4,128)S(1)} collective-permute-done((f32[8,2,4,4,128]{4,3,2,1,0:T(4,128)S(1)}, f32[8,2,4,4,128]{4,3,2,1,0:T(4,128)S(1)}, u32[]{:S(2)}, u32[]{:S(2)}) %collective-permute-start.6) | collective-permute-done | bytes 131104 | tf_op jit(solution)/shard_map/ppermute | solution.py:440
  53.0 4.5 %collective-permute-start.11 = (f32[8,2,4,4,128]{4,3,2,1,0:T(4,128)S(1)}, f32[8,2,4,4,128]{4,3,2,1,0:T(4,128)S(1)}, u32[]{:S(2)}, u32[]{:S(2)}) collective-permute-start(f32[8,2,4,4,128]{4,3,2,1,0:T(4,128)S(1)} %slice_select_fusion.2), channel_id=1, source_target_pairs={{0,8},{8,0},{16,24},{24,16},{32,40},{40,32},{48,56},{56,48},{64,72... | collective-permute-start | bytes 393224 | tf_op jit(solution)/shard_map/ppermute | solution.py:432
  57.5 0.3 collective-permute-start.7
  57.8 0.6 fusion.6
  58.5 0.0 collective-permute-done.11.far
  58.5 1.4 %shard_map.43 = (f32[16,4,32,128]{3,2,1,0:T(8,128)S(1)}, f32[8,2,16,128]{3,2,1,0:T(8,128)S(1)}, f32[8,128]{1,0:T(8,128)S(1)}) custom-call(s32[2]{0:T(128)S(1)} %pad_add_fusion.index_ref, f32[8,4,4,4,128]{4,3,2,1,0:T(4,128)S(1)} %all-to-all-done.1.own, f32[8,4,4,4,128]{4,3,2,1,0:T(4,128)S(1)} %collective-permute-done.8.pair, ...), custom_call_target="tpu_custom_call" | custom-call | tf_op jit(solution)/shard_map/pallas_call | solution.py:217
  59.9 3.0 %shard_map.44 = (f32[10,4,32,128]{3,2,1,0:T(8,128)S(1)}, f32[8,4,32,128]{3,2,1,0:T(8,128)S(1)}, f32[2,2,2,16,128]{4,3,2,1,0:T(8,128)}, f32[2,16,128]{2,1,0:T(8,128)}, f32[2,8,128]{2,1,0:T(8,128)S(1)}) custom-call(s32[2]{0:T(128)S(1)} %pad_add_fusion.index_ref, f32[8,4,4,4,128]{4,3,2,1,0:T(4,128)S(1)} %all-to-all-done.own, ...), custom_call_target="tpu_custom_call" | custom-call | tf_op jit(solution)/shard_map/pallas_call | solution.py:272
  62.9 0.7 broadcast_in_dim.8
  63.6 5.3 %all-to-all-start.2 = ((f32[16,2,8,128]{3,2,1,0:T(8,128)}), f32[16,2,8,128]{3,2,1,0:T(8,128)S(1)}, u32[]{:S(2)}, u32[]{:S(2)}) async-start(f32[16,2,8,128]{3,2,1,0:T(8,128)} %broadcast_in_dim.8), calls=%async_computation.2 | async-start | bytes 262144 | tf_op jit(solution)/shard_map/all_to_all | solution.py:483
  68.9 0.0 collective-permute-done.17.fylo_ref
  69.0 0.8 copy-done.12
  69.8 0.7 pad_maximum_fusion.2
  70.4 3.4 %collective-permute-start.19 = (f32[2,12,8,128]{3,2,1,0:T(8,128)}, f32[2,12,8,128]{3,2,1,0:T(8,128)}, u32[]{:S(2)}, u32[]{:S(2)}) collective-permute-start(f32[2,12,8,128]{3,2,1,0:T(8,128)} %pad_maximum_fusion.2), channel_id=1, source_target_pairs={{0,8},{8,16},{16,24},{24,32},{32,40},{40,48},{48,56},{56,64},{64,7... | collective-permute-start | bytes 294920 | tf_op jit(solution)/shard_map/ppermute | solution.py:428
  73.8 0.0 collective-permute-start.14
  73.9 0.6 pad_maximum_fusion.3
  74.5 2.3 %collective-permute-start.20 = (f32[2,12,8,128]{3,2,1,0:T(8,128)}, f32[2,12,8,128]{3,2,1,0:T(8,128)}, u32[]{:S(2)}, u32[]{:S(2)}) collective-permute-start(f32[2,12,8,128]{3,2,1,0:T(8,128)} %pad_maximum_fusion.3), channel_id=1, source_target_pairs={{0,248},{8,0},{16,8},{24,16},{32,24},{40,32},{48,40},{56,48},{64,5... | collective-permute-start | bytes 294920 | tf_op jit(solution)/shard_map/ppermute | solution.py:428
  76.8 0.1 collective-permute-start.13
  76.9 3.0 %collective-permute-start.15 = (f32[2,16,128]{2,1,0:T(8,128)}, f32[2,16,128]{2,1,0:T(8,128)S(1)}, u32[]{:S(2)}, u32[]{:S(2)}) collective-permute-start(f32[2,16,128]{2,1,0:T(8,128)} %get-tuple-element.44), channel_id=1, source_target_pairs={{0,16},{8,248},{16,32},{24,8},{32,48},{40,24},{48,64},{56,40},{64,... | collective-permute-start | bytes 49160 | tf_op jit(solution)/shard_map/ppermute | solution.py:440
  80.0 0.8 collective-permute-done.14.outer2
  80.8 0.0 all-to-all-done.2.mine3
  80.8 0.4 collective-permute-start.12
  81.2 0.0 collective-permute-done.19.fxlo_ref
  81.2 0.2 collective-permute-start.16
  81.4 0.5 collective-permute-done.20.fxhi_ref
  81.9 0.0 collective-permute-done.15.skip2
  81.9 0.0 collective-permute-done.13.pair2
  81.9 0.6 collective-permute-done.16.far2
  82.5 0.0 collective-permute-done.12.other3
  82.5 0.6 copy-done.7
  83.1 0.9 %copy-done.1 = f32[8,8,8,128]{3,2,1,0:T(8,128)S(1)} copy-done((f32[8,8,8,128]{3,2,1,0:T(8,128)S(1)}, f32[8,8,8,128]{3,2,1,0:T(8,128)}, u32[]{:S(2)}) %copy-start.1) | copy-done | bytes 262168
  84.0 5.3 %shard_map.45 = (f32[8,8,1024]{2,1,0:T(8,128)}, f32[8,8,1024]{2,1,0:T(8,128)}) custom-call(s32[2]{0:T(128)S(1)} %copy-done.7, f32[16,2,8,128]{3,2,1,0:T(8,128)S(1)} %all-to-all-done.2.mine3, f32[16,2,8,128]{3,2,1,0:T(8,128)S(1)} %collective-permute-done.12.other3, f32[2,2,2,16,128]{4,3,2,1,0:T(8,128)} %get-tuple-element.43.fs2, ...), custom_call_target="tpu_custom_call" | custom-call | tf_op jit(solution)/shard_map/pallas_call | solution.py:418
  (38 shorter events, 0.2 us)
Async XLA Ops:
  0.6 1.0 %copy-start.2 = (f32[8,8,1024]{2,1,0:T(8,128)S(1)}, f32[8,8,1024]{2,1,0:T(8,128)}, u32[]{:S(2)}) copy-start(f32[8,8,1024]{2,1,0:T(8,128)} %cot_ref.1) | copy-start | bytes 786436
  1.6 0.9 %copy-start.3 = (f32[8,8,1024]{2,1,0:T(8,128)S(1)}, f32[8,8,1024]{2,1,0:T(8,128)}, u32[]{:S(2)}) copy-start(f32[8,8,1024]{2,1,0:T(8,128)} %diag_ref.1) | copy-start | bytes 786436
  3.0 8.8 %collective-permute-start = (f32[2,8,2,8,128]{4,3,2,1,0:T(8,128)S(1)}, f32[2,8,2,8,128]{4,3,2,1,0:T(8,128)S(1)}, u32[]{:S(2)}, u32[]{:S(2)}) collective-permute-start(f32[2,8,2,8,128]{4,3,2,1,0:T(8,128)S(1)} %get-tuple-element.29), channel_id=1, source_target_pairs={{0,1},{1,2},{2,3},{3,4},{4,5},{5,6},{6,7},{7,0},{8,9},{9,10},{10,1... | collective-permute-start | bytes 393224 | tf_op jit(solution)/shard_map/ppermute | solution.py:428
  5.2 6.6 %collective-permute-start.1 = (f32[2,8,2,8,128]{4,3,2,1,0:T(8,128)S(1)}, f32[2,8,2,8,128]{4,3,2,1,0:T(8,128)S(1)}, u32[]{:S(2)}, u32[]{:S(2)}) collective-permute-start(f32[2,8,2,8,128]{4,3,2,1,0:T(8,128)S(1)} %get-tuple-element.30), channel_id=1, source_target_pairs={{0,7},{1,0},{2,1},{3,2},{4,3},{5,4},{6,5},{7,6},{8,15},{9,8},{10,9... | collective-permute-start | bytes 393224 | tf_op jit(solution)/shard_map/ppermute | solution.py:428
  8.3 9.1 %all-to-all-start.1 = ((f32[8,4,4,4,128]{4,3,2,1,0:T(4,128)}), f32[8,4,4,4,128]{4,3,2,1,0:T(4,128)S(1)}, u32[]{:S(2)}, u32[]{:S(2)}) async-start(f32[8,4,4,4,128]{4,3,2,1,0:T(4,128)} %broadcast_in_dim.7), calls=%async_computation.1 | async-start | bytes 524288 | tf_op jit(solution)/shard_map/all_to_all | solution.py:444
  11.8 48.1 %copy-start.6 = (s32[2]{0:T(128)}, s32[2]{0:T(128)S(1)}, u32[]{:S(2)}) copy-start(s32[2]{0:T(128)S(1)} %pad_add_fusion.index_ref) | copy-start | bytes 28
  11.9 17.7 %collective-permute-start.2 = (f32[2,2,12,8,128]{4,3,2,1,0:T(8,128)S(1)}, f32[2,2,12,8,128]{4,3,2,1,0:T(8,128)S(1)}, u32[]{:S(2)}, u32[]{:S(2)}) collective-permute-start(f32[2,2,12,8,128]{4,3,2,1,0:T(8,128)S(1)} %pad_maximum_fusion), channel_id=1, source_target_pairs={{0,8},{8,16},{16,24},{24,32},{32,40},{40,48},{48,56},{56,64},{64,7... | collective-permute-start | bytes 589832 | tf_op jit(solution)/shard_map/ppermute | solution.py:428
  16.6 12.9 %collective-permute-start.3 = (f32[2,2,12,8,128]{4,3,2,1,0:T(8,128)S(1)}, f32[2,2,12,8,128]{4,3,2,1,0:T(8,128)S(1)}, u32[]{:S(2)}, u32[]{:S(2)}) collective-permute-start(f32[2,2,12,8,128]{4,3,2,1,0:T(8,128)S(1)} %pad_maximum_fusion.1), channel_id=1, source_target_pairs={{0,248},{8,0},{16,8},{24,16},{32,24},{40,32},{48,40},{56,48},{64,5... | collective-permute-start | bytes 589832 | tf_op jit(solution)/shard_map/ppermute | solution.py:428
  17.4 22.3 %collective-permute-start.8 = (f32[8,4,4,4,128]{4,3,2,1,0:T(4,128)S(1)}, f32[8,4,4,4,128]{4,3,2,1,0:T(4,128)S(1)}, u32[]{:S(2)}, u32[]{:S(2)}) collective-permute-start(f32[8,4,4,4,128]{4,3,2,1,0:T(4,128)S(1)} %all-to-all-done.1.own), channel_id=1, source_target_pairs={{0,8},{8,0},{16,24},{24,16},{32,40},{40,32},{48,56},{56,48},{64,72... | collective-permute-start | bytes 786440 | tf_op jit(solution)/shard_map/ppermute | solution.py:432
  21.5 18.2 %collective-permute-start.9 = (f32[8,4,4,4,128]{4,3,2,1,0:T(4,128)S(1)}, f32[8,4,4,4,128]{4,3,2,1,0:T(4,128)S(1)}, u32[]{:S(2)}, u32[]{:S(2)}) collective-permute-start(f32[8,4,4,4,128]{4,3,2,1,0:T(4,128)S(1)} %all-to-all-done.1.own), channel_id=1, source_target_pairs={{0,248},{8,16},{16,8},{24,32},{32,24},{40,48},{48,40},{56,64},{64,... | collective-permute-start | bytes 786440 | tf_op jit(solution)/shard_map/ppermute | solution.py:436
  23.3 16.4 %collective-permute-start.10 = (f32[8,2,4,4,128]{4,3,2,1,0:T(4,128)}, f32[8,2,4,4,128]{4,3,2,1,0:T(4,128)}, u32[]{:S(2)}, u32[]{:S(2)}) collective-permute-start(f32[8,2,4,4,128]{4,3,2,1,0:T(4,128)} %slice_select_fusion), channel_id=1, source_target_pairs={{0,16},{8,248},{16,32},{24,8},{32,48},{40,24},{48,64},{56,40},{64,... | collective-permute-start | bytes 393224 | tf_op jit(solution)/shard_map/ppermute | solution.py:440
  30.4 0.6 copy-start.9
  31.0 0.8 copy-start
  31.0 0.8 copy-start.8
  31.8 4.9 %copy-start.10 = (f32[8,2,8,128]{3,2,1,0:T(8,128)S(1)}, f32[8,2,8,128]{3,2,1,0:T(8,128)}, u32[]{:S(2)}) copy-start(f32[8,2,8,128]{3,2,1,0:T(8,128)} %copy-done.9) | copy-start | bytes 196612
  31.8 9.9 %all-to-all-start = ((f32[8,4,4,4,128]{4,3,2,1,0:T(4,128)}), f32[8,4,4,4,128]{4,3,2,1,0:T(4,128)S(1)}, u32[]{:S(2)}, u32[]{:S(2)}) async-start(f32[8,4,4,4,128]{4,3,2,1,0:T(4,128)} %broadcast_in_dim.6), calls=%async_computation | async-start | bytes 524288 | tf_op jit(solution)/shard_map/all_to_all | solution.py:444
  35.4 33.5 %collective-permute-start.17 = (f32[8,2,8,128]{3,2,1,0:T(8,128)}, f32[8,2,8,128]{3,2,1,0:T(8,128)S(1)}, u32[]{:S(2)}, u32[]{:S(2)}) collective-permute-start(f32[8,2,8,128]{3,2,1,0:T(8,128)} %copy-done.8), channel_id=1, source_target_pairs={{0,1},{1,2},{2,3},{3,4},{4,5},{5,6},{6,7},{7,0},{8,9},{9,10},{10,1... | collective-permute-start | bytes 196616 | tf_op jit(solution)/shard_map/ppermute | solution.py:428
  36.7 21.1 %collective-permute-start.18 = (f32[8,2,8,128]{3,2,1,0:T(8,128)S(1)}, f32[8,2,8,128]{3,2,1,0:T(8,128)S(1)}, u32[]{:S(2)}, u32[]{:S(2)}) collective-permute-start(f32[8,2,8,128]{3,2,1,0:T(8,128)S(1)} %copy-done.10), channel_id=1, source_target_pairs={{0,7},{1,0},{2,1},{3,2},{4,3},{5,4},{6,5},{7,6},{8,15},{9,8},{10,9... | collective-permute-start | bytes 196616 | tf_op jit(solution)/shard_map/ppermute | solution.py:428
  41.8 15.7 %collective-permute-start.4 = (f32[8,4,4,4,128]{4,3,2,1,0:T(4,128)S(1)}, f32[8,4,4,4,128]{4,3,2,1,0:T(4,128)S(1)}, u32[]{:S(2)}, u32[]{:S(2)}) collective-permute-start(f32[8,4,4,4,128]{4,3,2,1,0:T(4,128)S(1)} %all-to-all-done.own), channel_id=1, source_target_pairs={{0,8},{8,0},{16,24},{24,16},{32,40},{40,32},{48,56},{56,48},{64,72... | collective-permute-start | bytes 786440 | tf_op jit(solution)/shard_map/ppermute | solution.py:432
  43.7 13.8 %collective-permute-start.5 = (f32[8,4,4,4,128]{4,3,2,1,0:T(4,128)S(1)}, f32[8,4,4,4,128]{4,3,2,1,0:T(4,128)S(1)}, u32[]{:S(2)}, u32[]{:S(2)}) collective-permute-start(f32[8,4,4,4,128]{4,3,2,1,0:T(4,128)S(1)} %all-to-all-done.own), channel_id=1, source_target_pairs={{0,248},{8,16},{16,8},{24,32},{32,24},{40,48},{48,40},{56,64},{64,... | collective-permute-start | bytes 786440 | tf_op jit(solution)/shard_map/ppermute | solution.py:436
  43.8 9.2 %collective-permute-start.6 = (f32[8,2,4,4,128]{4,3,2,1,0:T(4,128)S(1)}, f32[8,2,4,4,128]{4,3,2,1,0:T(4,128)S(1)}, u32[]{:S(2)}, u32[]{:S(2)}) collective-permute-start(f32[8,2,4,4,128]{4,3,2,1,0:T(4,128)S(1)} %slice_select_fusion.1), channel_id=1, source_target_pairs={{0,16},{8,248},{16,32},{24,8},{32,48},{40,24},{48,64},{56,40},{64,... | collective-permute-start | bytes 393224 | tf_op jit(solution)/shard_map/ppermute | solution.py:440
  53.0 5.5 %collective-permute-start.11 = (f32[8,2,4,4,128]{4,3,2,1,0:T(4,128)S(1)}, f32[8,2,4,4,128]{4,3,2,1,0:T(4,128)S(1)}, u32[]{:S(2)}, u32[]{:S(2)}) collective-permute-start(f32[8,2,4,4,128]{4,3,2,1,0:T(4,128)S(1)} %slice_select_fusion.2), channel_id=1, source_target_pairs={{0,8},{8,0},{16,24},{24,16},{32,40},{40,32},{48,56},{56,48},{64,72... | collective-permute-start | bytes 393224 | tf_op jit(solution)/shard_map/ppermute | solution.py:432
  57.5 2.4 %collective-permute-start.7 = (f32[8,2,4,4,128]{4,3,2,1,0:T(4,128)S(1)}, f32[8,2,4,4,128]{4,3,2,1,0:T(4,128)S(1)}, u32[]{:S(2)}, u32[]{:S(2)}) collective-permute-start(f32[8,2,4,4,128]{4,3,2,1,0:T(4,128)S(1)} %slice_select_fusion.3), channel_id=1, source_target_pairs={{0,8},{8,0},{16,24},{24,16},{32,40},{40,32},{48,56},{56,48},{64,72... | collective-permute-start | bytes 393224 | tf_op jit(solution)/shard_map/ppermute | solution.py:432
  57.8 2.1 %copy-start.4 = (f32[8,2,8,128]{3,2,1,0:T(8,128)}, f32[8,2,8,128]{3,2,1,0:T(8,128)S(1)}, u32[]{:S(2)}) copy-start(f32[8,2,8,128]{3,2,1,0:T(8,128)S(1)} %collective-permute-done.18.fyhi_ref) | copy-start | bytes 196612
  63.6 5.4 %copy-start.14 = (f32[2,2,8,128]{3,2,1,0:T(8,128)S(1)}, f32[2,2,8,128]{3,2,1,0:T(8,128)}, u32[]{:S(2)}) copy-start(f32[2,2,8,128]{3,2,1,0:T(8,128)} %get-tuple-element.63) | copy-start | bytes 49156
  63.6 17.2 %all-to-all-start.2 = ((f32[16,2,8,128]{3,2,1,0:T(8,128)}), f32[16,2,8,128]{3,2,1,0:T(8,128)S(1)}, u32[]{:S(2)}, u32[]{:S(2)}) async-start(f32[16,2,8,128]{3,2,1,0:T(8,128)} %broadcast_in_dim.8), calls=%async_computation.2 | async-start | bytes 262144 | tf_op jit(solution)/shard_map/all_to_all | solution.py:483
  68.9 0.8 copy-start.12
  69.8 4.1 %copy-start.11 = (f32[2,8,8,128]{3,2,1,0:T(8,128)S(1)}, f32[2,8,8,128]{3,2,1,0:T(8,128)}, u32[]{:S(2)}) copy-start(f32[2,8,8,128]{3,2,1,0:T(8,128)} %get-tuple-element.54) | copy-start | bytes 196612
  69.8 4.1 %copy-start.13 = (f32[2,2,8,128]{3,2,1,0:T(8,128)S(1)}, f32[2,2,8,128]{3,2,1,0:T(8,128)}, u32[]{:S(2)}) copy-start(f32[2,2,8,128]{3,2,1,0:T(8,128)} %get-tuple-element.62) | copy-start | bytes 49156
  70.4 10.8 %collective-permute-start.19 = (f32[2,12,8,128]{3,2,1,0:T(8,128)}, f32[2,12,8,128]{3,2,1,0:T(8,128)}, u32[]{:S(2)}, u32[]{:S(2)}) collective-permute-start(f32[2,12,8,128]{3,2,1,0:T(8,128)} %pad_maximum_fusion.2), channel_id=1, source_target_pairs={{0,8},{8,16},{16,24},{24,32},{32,40},{40,48},{48,56},{56,64},{64,7... | collective-permute-start | bytes 294920 | tf_op jit(solution)/shard_map/ppermute | solution.py:428
  73.8 7.0 %collective-permute-start.14 = (f32[2,2,2,16,128]{4,3,2,1,0:T(8,128)}, f32[2,2,2,16,128]{4,3,2,1,0:T(8,128)S(1)}, u32[]{:S(2)}, u32[]{:S(2)}) collective-permute-start(f32[2,2,2,16,128]{4,3,2,1,0:T(8,128)} %get-tuple-element.43.fs2), channel_id=1, source_target_pairs={{0,248},{8,16},{16,8},{24,32},{32,24},{40,48},{48,40},{56,64},{64,... | collective-permute-start | bytes 196616 | tf_op jit(solution)/shard_map/ppermute | solution.py:436
  73.9 8.6 %copy-start.5 = (f32[8,2,8,128]{3,2,1,0:T(8,128)S(1)}, f32[8,2,8,128]{3,2,1,0:T(8,128)}, u32[]{:S(2)}) copy-start(f32[8,2,8,128]{3,2,1,0:T(8,128)} %copy-done.4) | copy-start | bytes 196612
  74.5 7.4 %collective-permute-start.20 = (f32[2,12,8,128]{3,2,1,0:T(8,128)}, f32[2,12,8,128]{3,2,1,0:T(8,128)}, u32[]{:S(2)}, u32[]{:S(2)}) collective-permute-start(f32[2,12,8,128]{3,2,1,0:T(8,128)} %pad_maximum_fusion.3), channel_id=1, source_target_pairs={{0,248},{8,0},{16,8},{24,16},{32,24},{40,32},{48,40},{56,48},{64,5... | collective-permute-start | bytes 294920 | tf_op jit(solution)/shard_map/ppermute | solution.py:428
  76.8 5.1 %collective-permute-start.13 = (f32[2,2,2,16,128]{4,3,2,1,0:T(8,128)}, f32[2,2,2,16,128]{4,3,2,1,0:T(8,128)}, u32[]{:S(2)}, u32[]{:S(2)}) collective-permute-start(f32[2,2,2,16,128]{4,3,2,1,0:T(8,128)} %get-tuple-element.43.fs2), channel_id=1, source_target_pairs={{0,8},{8,0},{16,24},{24,16},{32,40},{40,32},{48,56},{56,48},{64,72... | collective-permute-start | bytes 196616 | tf_op jit(solution)/shard_map/ppermute | solution.py:432
  76.9 4.9 %collective-permute-start.15 = (f32[2,16,128]{2,1,0:T(8,128)}, f32[2,16,128]{2,1,0:T(8,128)S(1)}, u32[]{:S(2)}, u32[]{:S(2)}) collective-permute-start(f32[2,16,128]{2,1,0:T(8,128)} %get-tuple-element.44), channel_id=1, source_target_pairs={{0,16},{8,248},{16,32},{24,8},{32,48},{40,24},{48,64},{56,40},{64,... | collective-permute-start | bytes 49160 | tf_op jit(solution)/shard_map/ppermute | solution.py:440
  80.8 1.7 %collective-permute-start.12 = (f32[16,2,8,128]{3,2,1,0:T(8,128)S(1)}, f32[16,2,8,128]{3,2,1,0:T(8,128)S(1)}, u32[]{:S(2)}, u32[]{:S(2)}) collective-permute-start(f32[16,2,8,128]{3,2,1,0:T(8,128)S(1)} %all-to-all-done.2.mine3), channel_id=1, source_target_pairs={{0,8},{8,0},{16,24},{24,16},{32,40},{40,32},{48,56},{56,48},{64,72... | collective-permute-start | bytes 393224 | tf_op jit(solution)/shard_map/ppermute | solution.py:432
  81.2 1.3 %collective-permute-start.16 = (f32[2,16,128]{2,1,0:T(8,128)S(1)}, f32[2,16,128]{2,1,0:T(8,128)S(1)}, u32[]{:S(2)}, u32[]{:S(2)}) collective-permute-start(f32[2,16,128]{2,1,0:T(8,128)S(1)} %fusion), channel_id=1, source_target_pairs={{0,8},{8,0},{16,24},{24,16},{32,40},{40,32},{48,56},{56,48},{64,72... | collective-permute-start | bytes 49160 | tf_op jit(solution)/shard_map/ppermute | solution.py:432
  82.5 0.6 copy-start.7
  83.1 0.9 %copy-start.1 = (f32[8,8,8,128]{3,2,1,0:T(8,128)S(1)}, f32[8,8,8,128]{3,2,1,0:T(8,128)}, u32[]{:S(2)}) copy-start(f32[8,8,8,128]{3,2,1,0:T(8,128)} %copy-done) | copy-start | bytes 786436
